TPU v7x, 512 devices: a whole 4x8x8 slice. The times are simulated.
512 devices in a mesh: band: 4 (over z_hi, core), dom: 128 (over y, x, z_lo).
Axes of the slice: x: 4, y: 8, z: 8 (z_hi: 2, z_lo: 4; z = z_hi * 4 + z_lo), core: 2. Of those that a mesh axis runs over, the one named last changes fastest.
Arguments:
- orbitals: float32 [128, 8, 12, 16, 512], P('dom', None, None, None, 'band'), may hold values from -8 to 8, as said below
- potential: float32 [128, 8, 12, 16], P('dom'), may hold values from -2 to 0.5
- bounds: float32 [3], replicated, may hold values from -2.6 to 36, as said below
- rotation: float32 [512, 512], P(None, 'band'), may hold values from -0.2 to 1.2
Outputs:
- rotated: float32 [128, 8, 12, 16, 512], P('dom', None, None, None, 'band')
- margin: float32 [512, 512], P(None, 'band')
- projected: float32 [512, 512], P(None, 'band')
Inputs may be any that keep to these rules, and one draw needn't show every extreme that they name: `orbitals`: amplitudes vary smoothly in size across the grid. bounds holds the lowest-eigenvalue estimate, the cutoff and a bound above the largest eigenvalue of H, in that order.
All inputs are finite; a program needn't handle non-finite values.
Results may differ from a plain program's by a relative error of at most 0.0001.
Values sent between devices are 32-bit elements; how exact they have to be, the bound alone decides.
No kernel may reach another device: no remote copies, remote signals or barrier semaphores. Data moves between devices by JAX's collectives and lax.ppermute only.
A program may use at most 64 MiB of HBM per device.

v0:
```python
from functools import partial

import jax
import jax.numpy as jnp
from jax import lax
from jax.sharding import PartitionSpec as P

DEGREE = 3


STENCIL = (
    -5369.0 / 1800.0,
    12.0 / 7.0,
    -15.0 / 56.0,
    10.0 / 189.0,
    -1.0 / 112.0,
    2.0 / 1925.0,
    -1.0 / 16632.0,
)
INV_SPACING2 = 1.0 / 0.36


def from_behind(x, axis, by):
    size = lax.axis_size(axis)
    pairs = [(i, i + by) for i in range(size) if 0 <= i + by < size]
    return lax.ppermute(x, axis, pairs)


def neighbor(face_cells, distance):
    return from_behind(face_cells, "dom", distance)


def block_hamiltonian(values, local_potential, coords, counts, strides, dom_size):
    stencil_reach = len(STENCIL) - 1
    summed = 3.0 * STENCIL[0] * values
    for dim_index in range(3):
        length = values.shape[dim_index]
        upper_face = lax.slice_in_dim(values, length - stencil_reach, length, axis=dim_index)
        bottom = lax.slice_in_dim(values, 0, stencil_reach, axis=dim_index)
        from_below = neighbor(upper_face, strides[dim_index])
        from_above = neighbor(bottom, -strides[dim_index])
        from_below = jnp.where(coords[dim_index] > 0, from_below, 0.0)
        from_above = jnp.where(coords[dim_index] < counts[dim_index] - 1, from_above, 0.0)
        extended = jnp.concatenate([from_below, values, from_above], axis=dim_index)
        for offset in range(1, stencil_reach + 1):
            upper_part = lax.slice_in_dim(
                extended, stencil_reach + offset, stencil_reach + offset + length, axis=dim_index
            )
            lower_part = lax.slice_in_dim(
                extended, stencil_reach - offset, stencil_reach - offset + length, axis=dim_index
            )
            summed = summed + STENCIL[offset] * (upper_part + lower_part)
    return -0.5 * INV_SPACING2 * summed + local_potential[..., None] * values


def chebyshev(start_block, operator_fn, bounds):
    lowest, cutoff, highest = (bounds[0], bounds[1], bounds[2])
    half_width = (highest - cutoff) / 2.0
    centre = (highest + cutoff) / 2.0
    sigma_now = half_width / (lowest - centre)
    tau_value = 2.0 / sigma_now
    previous = start_block
    current = (operator_fn(start_block) - centre * start_block) * (sigma_now / half_width)
    for turn_index in range(DEGREE - 1):
        sigma_next = 1.0 / (tau_value - sigma_now)
        following = (
            2.0 * sigma_next / half_width * (operator_fn(current) - centre * current)
            - sigma_now * sigma_next * previous
        )
        previous = current
        current = following
        sigma_now = sigma_next
    return current


def contract(left, right):
    return lax.dot_general(
        left,
        right,
        (((0,), (0,)), ((), ())),
        precision=lax.Precision.HIGHEST,
        preferred_element_type=jnp.float32,
    )


def local(orbitals, potential, bounds, rotation):
    dom_size = lax.axis_size("dom")
    count_z = min(8, dom_size)
    count_y = min(4, dom_size // count_z)
    count_x = dom_size // (count_z * count_y)
    counts = (count_x, count_y, count_z)
    sides = (orbitals.shape[1], orbitals.shape[2], orbitals.shape[3])
    band_width = orbitals.shape[4]
    cell_count = sides[0] * sides[1] * sides[2]
    dom_place = lax.axis_index("dom")
    coords = (dom_place // (count_z * count_y), dom_place // count_z % count_y, dom_place % count_z)
    strides = (count_y * count_z, count_z, 1)
    operator_fn = partial(
        block_hamiltonian,
        local_potential=potential[0],
        coords=coords,
        counts=counts,
        strides=strides,
        dom_size=dom_size,
    )
    filtered = chebyshev(orbitals[0], operator_fn, bounds)
    image_field = operator_fn(filtered)
    flat_filtered = filtered.reshape(cell_count, band_width)
    flat_image = image_field.reshape(cell_count, band_width)
    squares = lax.psum(jnp.sum(flat_filtered * flat_filtered, axis=0), "dom")
    norms_own = jnp.sqrt(squares)
    normed = flat_filtered / norms_own
    normed_image = flat_image / norms_own
    shard_piece = lax.all_gather(normed, "band", axis=1, tiled=True)
    margin_rows = contract(shard_piece, normed)
    hamilton_rows = contract(shard_piece, normed_image)
    rotated_sum = jnp.dot(
        shard_piece, rotation, precision=lax.Precision.HIGHEST, preferred_element_type=jnp.float32
    )
    margin_rows, hamilton_rows, rotated = (margin_rows, hamilton_rows, rotated_sum)
    margin, projected = lax.psum((margin_rows, hamilton_rows), "dom")
    rotated = rotated.reshape(1, sides[0], sides[1], sides[2], band_width)
    return (rotated, margin, projected)


def solution(mesh):
    in_specs = (
        P("dom", None, None, None, "band"),
        P("dom", None, None, None),
        P(),
        P(None, "band"),
    )
    out_specs = (P("dom", None, None, None, "band"), P(None, "band"), P(None, "band"))
    return jax.shard_map(local, mesh=mesh, in_specs=in_specs, out_specs=out_specs, check_vma=False)
```

profile of v0, /device:TPU:32, one launch (start us, length us, event | category | flops | bytes accessed | tf_op | source)
XLA Modules:
  0.0 2015.5 jit_solution(17272518371270383169)
XLA Ops:
  19.7 8.0 collective-permute-start.4
  42.9 17.8 collective-permute-done.5
  61.9 5.1 collective-permute-done
  67.0 5.8 fusion.176
  72.9 13.2 collective-permute-start.10
  90.2 7.5 collective-permute-start.8
  99.6 6.0 collective-permute-start.6
  105.7 13.1 collective-permute-done.11
  119.1 7.2 collective-permute-done.6
  126.3 5.9 fusion.120
  132.3 12.9 collective-permute-start.16
  149.3 7.5 collective-permute-start.14
  158.7 6.0 collective-permute-start.12
  164.8 14.0 collective-permute-done.17
  189.0 6.1 multiply_reduce_fusion
  195.9 9.9 collective-permute-start.22
  210.7 7.5 collective-permute-start.20
  222.3 384.3 %psum.21 = f32[128]{0:T(128)S(1)} all-reduce(f32[128]{0:T(128)S(1)} %get-tuple-element.5), channel_id=1, replica_groups=mesh['band'=4,'dom'=128] {'dom'}, use_global_device_ids=true, to_apply=%region_1.2 | all-reduce | flops 128 | bytes 1024 | tf_op jit(solution)/shard_map/psum | solution.py:110
  610.9 8.5 collective-permute-done.18
  619.4 5.7 fusion.6
  626.7 58.5 %all-gather.2.cloned.1.call-done = f32[1536,512]{1,0:T(8,128)} async-done(((f32[1536,128]{1,0:T(8,128)}), f32[1536,512]{1,0:T(8,128)}) %all-gather.2.cloned.1.call-update) | async-done | bytes 3145744 | tf_op jit(solution)/shard_map/all_gather | solution.py:114
  685.2 8.0 fusion.366
  693.2 6.9 fusion.367
  703.6 1301.7 %all-reduce.3.cloned.1.call-done = (f32[512,128]{1,0:T(8,128)}, f32[512,128]{1,0:T(8,128)}) async-done(((f32[512,128]{1,0:T(8,128)}, f32[512,128]{1,0:T(8,128)}), (f32[512,128]{1,0:T(8,128)}, f32[512,128]{1,0:T(8,128)})) %all-reduce.3.cloned.1.call-update) | async-done | bytes 524304 | tf_op jit(solution)/shard_map/psum | solution.py:121
  (90 shorter events, 70.2 us)
Async XLA Ops:
  7.2 678.0 %all-gather.2.cloned.1.call-start = ((), (), s32[]{:S(2)}) async-start(), calls=%async_computation | async-start | bytes 3932160 | tf_op jit(solution)/shard_map/all_gather | solution.py:114
  9.2 51.5 %collective-permute-start.3 = (f32[8,6,16,128]{3,2,1,0:T(8,128)}, f32[8,6,16,128]{3,2,1,0:T(8,128)}, u32[]{:S(2)}, u32[]{:S(2)}) collective-permute-start(f32[8,6,16,128]{3,2,1,0:T(8,128)} %get-tuple-element.28), channel_id=1, source_target_pairs={{0,8},{1,9},{2,10},{3,11},{4,12},{5,13},{6,14},{7,15},{8,16},{9,17... | collective-permute-start | bytes 1179656 | tf_op jit(solution)/shard_map/ppermute | solution.py:26
  14.2 46.6 %collective-permute-start.2 = (f32[8,6,16,128]{3,2,1,0:T(8,128)S(1)}, f32[8,6,16,128]{3,2,1,0:T(8,128)}, u32[]{:S(2)}, u32[]{:S(2)}) collective-permute-start(f32[8,6,16,128]{3,2,1,0:T(8,128)S(1)} %get-tuple-element.27), channel_id=1, source_target_pairs={{8,0},{9,1},{10,2},{11,3},{12,4},{13,5},{14,6},{15,7},{16,8},{17,9... | collective-permute-start | bytes 1179656 | tf_op jit(solution)/shard_map/ppermute | solution.py:26
  27.7 33.0 %collective-permute-start.5 = (f32[8,12,6,128]{3,2,1,0:T(8,128)}, f32[8,12,6,128]{3,2,1,0:T(8,128)}, u32[]{:S(2)}, u32[]{:S(2)}) collective-permute-start(f32[8,12,6,128]{3,2,1,0:T(8,128)} %get-tuple-element.30), channel_id=1, source_target_pairs={{0,1},{1,2},{2,3},{3,4},{4,5},{5,6},{6,7},{7,8},{8,9},{9,10},{10,1... | collective-permute-start | bytes 884744 | tf_op jit(solution)/shard_map/ppermute | solution.py:26
  29.8 32.0 %collective-permute-start.1 = (f32[6,12,16,128]{3,2,1,0:T(8,128)S(1)}, f32[6,12,16,128]{3,2,1,0:T(8,128)S(1)}, u32[]{:S(2)}, u32[]{:S(2)}) collective-permute-start(f32[6,12,16,128]{3,2,1,0:T(8,128)S(1)} %get-tuple-element.26), channel_id=1, source_target_pairs={{0,32},{1,33},{2,34},{3,35},{4,36},{5,37},{6,38},{7,39},{8,40},{9,... | collective-permute-start | bytes 1769480 | tf_op jit(solution)/shard_map/ppermute | solution.py:26
  38.8 28.2 %collective-permute-start = (f32[6,12,16,128]{3,2,1,0:T(8,128)S(1)}, f32[6,12,16,128]{3,2,1,0:T(8,128)S(1)}, u32[]{:S(2)}, u32[]{:S(2)}) collective-permute-start(f32[6,12,16,128]{3,2,1,0:T(8,128)S(1)} %get-tuple-element.25), channel_id=1, source_target_pairs={{32,0},{33,1},{34,2},{35,3},{36,4},{37,5},{38,6},{39,7},{40,8},{41... | collective-permute-start | bytes 1769480 | tf_op jit(solution)/shard_map/ppermute | solution.py:26
  72.9 26.8 %collective-permute-start.10 = (f32[8,12,6,128]{3,2,1,0:T(8,128)S(1)}, f32[8,12,6,128]{3,2,1,0:T(8,128)S(1)}, u32[]{:S(2)}, u32[]{:S(2)}) collective-permute-start(f32[8,12,6,128]{3,2,1,0:T(8,128)S(1)} %get-tuple-element.23), channel_id=1, source_target_pairs={{1,0},{2,1},{3,2},{4,3},{5,4},{6,5},{7,6},{8,7},{9,8},{10,9},{11,1... | collective-permute-start | bytes 884744 | tf_op jit(solution)/shard_map/ppermute | solution.py:26
  86.2 32.6 %collective-permute-start.11 = (f32[8,12,6,128]{3,2,1,0:T(8,128)S(1)}, f32[8,12,6,128]{3,2,1,0:T(8,128)S(1)}, u32[]{:S(2)}, u32[]{:S(2)}) collective-permute-start(f32[8,12,6,128]{3,2,1,0:T(8,128)S(1)} %get-tuple-element.24), channel_id=1, source_target_pairs={{0,1},{1,2},{2,3},{3,4},{4,5},{5,6},{6,7},{7,8},{8,9},{9,10},{10,1... | collective-permute-start | bytes 884744 | tf_op jit(solution)/shard_map/ppermute | solution.py:26
  88.2 30.7 %collective-permute-start.9 = (f32[8,6,16,128]{3,2,1,0:T(8,128)S(1)}, f32[8,6,16,128]{3,2,1,0:T(8,128)S(1)}, u32[]{:S(2)}, u32[]{:S(2)}) collective-permute-start(f32[8,6,16,128]{3,2,1,0:T(8,128)S(1)} %get-tuple-element.22), channel_id=1, source_target_pairs={{0,8},{1,9},{2,10},{3,11},{4,12},{5,13},{6,14},{7,15},{8,16},{9,17... | collective-permute-start | bytes 1179656 | tf_op jit(solution)/shard_map/ppermute | solution.py:26
  90.2 28.8 %collective-permute-start.8 = (f32[8,6,16,128]{3,2,1,0:T(8,128)S(1)}, f32[8,6,16,128]{3,2,1,0:T(8,128)S(1)}, u32[]{:S(2)}, u32[]{:S(2)}) collective-permute-start(f32[8,6,16,128]{3,2,1,0:T(8,128)S(1)} %get-tuple-element.21), channel_id=1, source_target_pairs={{8,0},{9,1},{10,2},{11,3},{12,4},{13,5},{14,6},{15,7},{16,8},{17,9... | collective-permute-start | bytes 1179656 | tf_op jit(solution)/shard_map/ppermute | solution.py:26
  97.7 21.3 %collective-permute-start.7 = (f32[6,12,16,128]{3,2,1,0:T(8,128)S(1)}, f32[6,12,16,128]{3,2,1,0:T(8,128)S(1)}, u32[]{:S(2)}, u32[]{:S(2)}) collective-permute-start(f32[6,12,16,128]{3,2,1,0:T(8,128)S(1)} %get-tuple-element.20), channel_id=1, source_target_pairs={{0,32},{1,33},{2,34},{3,35},{4,36},{5,37},{6,38},{7,39},{8,40},{9,... | collective-permute-start | bytes 1769480 | tf_op jit(solution)/shard_map/ppermute | solution.py:26
  99.6 26.6 %collective-permute-start.6 = (f32[6,12,16,128]{3,2,1,0:T(8,128)S(1)}, f32[6,12,16,128]{3,2,1,0:T(8,128)S(1)}, u32[]{:S(2)}, u32[]{:S(2)}) collective-permute-start(f32[6,12,16,128]{3,2,1,0:T(8,128)S(1)} %get-tuple-element.19), channel_id=1, source_target_pairs={{32,0},{33,1},{34,2},{35,3},{36,4},{37,5},{38,6},{39,7},{40,8},{41... | collective-permute-start | bytes 1769480 | tf_op jit(solution)/shard_map/ppermute | solution.py:26
  132.3 26.4 %collective-permute-start.16 = (f32[8,12,6,128]{3,2,1,0:T(8,128)S(1)}, f32[8,12,6,128]{3,2,1,0:T(8,128)S(1)}, u32[]{:S(2)}, u32[]{:S(2)}) collective-permute-start(f32[8,12,6,128]{3,2,1,0:T(8,128)S(1)} %get-tuple-element.17), channel_id=1, source_target_pairs={{1,0},{2,1},{3,2},{4,3},{5,4},{6,5},{7,6},{8,7},{9,8},{10,9},{11,1... | collective-permute-start | bytes 884744 | tf_op jit(solution)/shard_map/ppermute | solution.py:26
  145.3 33.5 %collective-permute-start.17 = (f32[8,12,6,128]{3,2,1,0:T(8,128)S(1)}, f32[8,12,6,128]{3,2,1,0:T(8,128)S(1)}, u32[]{:S(2)}, u32[]{:S(2)}) collective-permute-start(f32[8,12,6,128]{3,2,1,0:T(8,128)S(1)} %get-tuple-element.18), channel_id=1, source_target_pairs={{0,1},{1,2},{2,3},{3,4},{4,5},{5,6},{6,7},{7,8},{8,9},{9,10},{10,1... | collective-permute-start | bytes 884744 | tf_op jit(solution)/shard_map/ppermute | solution.py:26
  147.3 31.9 %collective-permute-start.15 = (f32[8,6,16,128]{3,2,1,0:T(8,128)S(1)}, f32[8,6,16,128]{3,2,1,0:T(8,128)S(1)}, u32[]{:S(2)}, u32[]{:S(2)}) collective-permute-start(f32[8,6,16,128]{3,2,1,0:T(8,128)S(1)} %get-tuple-element.16), channel_id=1, source_target_pairs={{0,8},{1,9},{2,10},{3,11},{4,12},{5,13},{6,14},{7,15},{8,16},{9,17... | collective-permute-start | bytes 1179656 | tf_op jit(solution)/shard_map/ppermute | solution.py:26
  149.3 30.0 %collective-permute-start.14 = (f32[8,6,16,128]{3,2,1,0:T(8,128)S(1)}, f32[8,6,16,128]{3,2,1,0:T(8,128)S(1)}, u32[]{:S(2)}, u32[]{:S(2)}) collective-permute-start(f32[8,6,16,128]{3,2,1,0:T(8,128)S(1)} %get-tuple-element.15), channel_id=1, source_target_pairs={{8,0},{9,1},{10,2},{11,3},{12,4},{13,5},{14,6},{15,7},{16,8},{17,9... | collective-permute-start | bytes 1179656 | tf_op jit(solution)/shard_map/ppermute | solution.py:26
  156.8 27.1 %collective-permute-start.13 = (f32[6,12,16,128]{3,2,1,0:T(8,128)S(1)}, f32[6,12,16,128]{3,2,1,0:T(8,128)S(1)}, u32[]{:S(2)}, u32[]{:S(2)}) collective-permute-start(f32[6,12,16,128]{3,2,1,0:T(8,128)S(1)} %get-tuple-element.14), channel_id=1, source_target_pairs={{0,32},{1,33},{2,34},{3,35},{4,36},{5,37},{6,38},{7,39},{8,40},{9,... | collective-permute-start | bytes 1769480 | tf_op jit(solution)/shard_map/ppermute | solution.py:26
  158.7 30.2 %collective-permute-start.12 = (f32[6,12,16,128]{3,2,1,0:T(8,128)S(1)}, f32[6,12,16,128]{3,2,1,0:T(8,128)S(1)}, u32[]{:S(2)}, u32[]{:S(2)}) collective-permute-start(f32[6,12,16,128]{3,2,1,0:T(8,128)S(1)} %get-tuple-element.13), channel_id=1, source_target_pairs={{32,0},{33,1},{34,2},{35,3},{36,4},{37,5},{38,6},{39,7},{40,8},{41... | collective-permute-start | bytes 1769480 | tf_op jit(solution)/shard_map/ppermute | solution.py:26
  195.9 410.8 %collective-permute-start.22 = (f32[8,12,6,128]{3,2,1,0:T(8,128)}, f32[8,12,6,128]{3,2,1,0:T(8,128)}, u32[]{:S(2)}, u32[]{:S(2)}) collective-permute-start(f32[8,12,6,128]{3,2,1,0:T(8,128)} %get-tuple-element.11), channel_id=1, source_target_pairs={{1,0},{2,1},{3,2},{4,3},{5,4},{6,5},{7,6},{8,7},{9,8},{10,9},{11,1... | collective-permute-start | bytes 884744 | tf_op jit(solution)/shard_map/ppermute | solution.py:26
  205.9 403.8 %collective-permute-start.23 = (f32[8,12,6,128]{3,2,1,0:T(8,128)S(1)}, f32[8,12,6,128]{3,2,1,0:T(8,128)}, u32[]{:S(2)}, u32[]{:S(2)}) collective-permute-start(f32[8,12,6,128]{3,2,1,0:T(8,128)S(1)} %get-tuple-element.12), channel_id=1, source_target_pairs={{0,1},{1,2},{2,3},{3,4},{4,5},{5,6},{6,7},{7,8},{8,9},{9,10},{10,1... | collective-permute-start | bytes 884744 | tf_op jit(solution)/shard_map/ppermute | solution.py:26
  208.8 401.0 %collective-permute-start.21 = (f32[8,6,16,128]{3,2,1,0:T(8,128)}, f32[8,6,16,128]{3,2,1,0:T(8,128)}, u32[]{:S(2)}, u32[]{:S(2)}) collective-permute-start(f32[8,6,16,128]{3,2,1,0:T(8,128)} %get-tuple-element.10), channel_id=1, source_target_pairs={{0,8},{1,9},{2,10},{3,11},{4,12},{5,13},{6,14},{7,15},{8,16},{9,17... | collective-permute-start | bytes 1179656 | tf_op jit(solution)/shard_map/ppermute | solution.py:26
  210.7 399.1 %collective-permute-start.20 = (f32[8,6,16,128]{3,2,1,0:T(8,128)}, f32[8,6,16,128]{3,2,1,0:T(8,128)}, u32[]{:S(2)}, u32[]{:S(2)}) collective-permute-start(f32[8,6,16,128]{3,2,1,0:T(8,128)} %get-tuple-element.9), channel_id=1, source_target_pairs={{8,0},{9,1},{10,2},{11,3},{12,4},{13,5},{14,6},{15,7},{16,8},{17,9... | collective-permute-start | bytes 1179656 | tf_op jit(solution)/shard_map/ppermute | solution.py:26
  218.2 392.6 %collective-permute-start.19 = (f32[6,12,16,128]{3,2,1,0:T(8,128)S(1)}, f32[6,12,16,128]{3,2,1,0:T(8,128)S(1)}, u32[]{:S(2)}, u32[]{:S(2)}) collective-permute-start(f32[6,12,16,128]{3,2,1,0:T(8,128)S(1)} %get-tuple-element.8), channel_id=1, source_target_pairs={{0,32},{1,33},{2,34},{3,35},{4,36},{5,37},{6,38},{7,39},{8,40},{9,... | collective-permute-start | bytes 1769480 | tf_op jit(solution)/shard_map/ppermute | solution.py:26
  626.5 1378.8 %all-reduce.3.cloned.1.call-start = ((), (), s32[]{:S(2)}) async-start(), calls=%async_computation.1 | async-start | bytes 1048576 | tf_op jit(solution)/shard_map/psum | solution.py:121
  (7 other events, 759.5 us)
Sparse Core Ops, SparseCore 0:
  626.6 58.5 all-gather.1
  700.2 1305.0 all-reduce.2
where the time goes:
time: 2020 us
  waiting for transfers between devices  1440 us (71%)
  blocking collectives  384 us (19%)
  starting transfers between devices  118 us (6%)
  other arithmetic  29.8 us (1%)
    psum x1, waiting for transfers between devices, local(): margin, projected = lax.psum((margin_rows, hamilton_rows), 'dom')  1300 us
    psum x1, blocking collectives, local(): squares = lax.psum(jnp.sum(flat_filtered * flat_filtered, axis=0), 'dom')  384 us
    ppermute x24, starting transfers between devices, from_behind(): return lax.ppermute(x, axis, pairs)  118 us
    ppermute x24, waiting for transfers between devices, from_behind(): return lax.ppermute(x, axis, pairs)  77 us
    all_gather x1, waiting for transfers between devices, local(): shard_piece = lax.all_gather(normed, 'band', axis=1, tiled=True)  58.5 us
  transfers between devices with their start and end apart: 26, of which 12 were waited for; matrix products, arithmetic and copies ran while one was open for 1% of the time, Pallas kernels for 0%

commit v1 on v0

v1 whole, which is shorter than its diff:
```python
import itertools
from functools import partial

import jax
import jax.numpy as jnp
from jax import lax
from jax.experimental import pallas as pl
from jax.experimental.pallas import tpu as pltpu
from jax.sharding import PartitionSpec as P

STENCIL = (
    -5369.0 / 1800.0,
    12.0 / 7.0,
    -15.0 / 56.0,
    10.0 / 189.0,
    -1.0 / 112.0,
    2.0 / 1925.0,
    -1.0 / 16632.0,
)
REACH = 6
KINETIC = -0.5 / 0.36
BX, BY, BZ = 8, 12, 16
CELLS = BX * BY * BZ
HALF = CELLS // 2
PX, PY, PZ = 4, 4, 8
BLOCKS = PX * PY * PZ
LANES = 128

ORDER = [(ix * PY + iy) * PZ + iz for iz in range(PZ) for ix in range(PX) for iy in range(PY)]
STEP_X, STEP_Y, STEP_Z = PY, 1, PX * PY


def flat(band, dom):
    return band * BLOCKS + dom


def chip(y, x, z):
    return (y * 4 + x) * 4 + z


CORE_GROUPS = [[flat(2 * h + c, d) for d in ORDER for h in range(2)] for c in range(2)]
X_GROUPS = [
    [flat(b, chip(y, x, z)) for x in range(4)]
    for b in range(4)
    for y in range(8)
    for z in range(4)
]
PLANE_GROUPS = [
    [flat(2 * h + c, chip(y, x, z)) for y in range(8) for z in range(4) for h in range(2)]
    for c in range(2)
    for x in range(4)
]
CORE_SWAP = [(0, 1), (1, 0), (2, 3), (3, 2)]
Z_SWAP = [(0, 2), (2, 0), (1, 3), (3, 1)]


def exchange(x, groups):
    return lax.all_to_all(x, ("band", "dom"), 0, 0, tiled=True, axis_index_groups=groups)


OX, OY, OZ = REACH, REACH, 8
EXT = (BX + 2 * REACH, BY + 2 * REACH, BZ + 16, LANES)


def filter_kernel(coef_ref, x_ref, v_own_ref, v_other_ref, out_ref, ea, eb, pot, img):
    lane = lax.broadcasted_iota(jnp.int32, (1, LANES), 1)
    iz, ix, iy = lane // STEP_Z, lane // STEP_X % PX, lane % PY

    def spread(ext):
        own_y, own_z = slice(OY, OY + BY), slice(OZ, OZ + BZ)

        def below(v, step, keep):
            return jnp.where(keep, pltpu.roll(v, step, v.ndim - 1), 0.0)

        def above(v, step, keep):
            return jnp.where(keep, pltpu.roll(v, LANES - step, v.ndim - 1), 0.0)

        def inner(i, carry):
            at = i + OX
            ext[at, own_y, 0:8] = below(ext[at, own_y, OZ + 8 : OZ + 16], STEP_Z, iz > 0)
            ext[at, own_y, OZ + BZ : OZ + BZ + 8] = above(ext[at, own_y, OZ : OZ + 8], STEP_Z, iz < PZ - 1)
            ext[at, 0:OY, own_z] = below(ext[at, BY : BY + OY, own_z], STEP_Y, iy > 0)
            ext[at, OY + BY :, own_z] = above(ext[at, OY : 2 * OY, own_z], STEP_Y, iy < PY - 1)
            return carry

        def outer(i, carry):
            ext[i, own_y, own_z] = below(ext[i + BX, own_y, own_z], STEP_X, ix > 0)
            ext[i + OX + BX, own_y, own_z] = above(ext[i + OX, own_y, own_z], STEP_X, ix < PX - 1)
            return carry

        lax.fori_loop(0, BX, inner, 0)
        lax.fori_loop(0, REACH, outer, 0)

    def part(ext, i, y0, ys):
        return ext[i + OX, OY + y0 : OY + y0 + ys, OZ : OZ + BZ]

    def image(ext, i, y0, ys, scale, shift):
        at, y, z = i + OX, OY + y0, OZ
        centre = ext[at, y : y + ys, z : z + BZ]
        total = (3.0 * STENCIL[0]) * centre
        for k in range(1, REACH + 1):
            pair_x = ext[at - k, y : y + ys, z : z + BZ] + ext[at + k, y : y + ys, z : z + BZ]
            pair_y = ext[at, y - k : y - k + ys, z : z + BZ] + ext[at, y + k : y + k + ys, z : z + BZ]
            pair_z = ext[at, y : y + ys, z - k : z - k + BZ] + ext[at, y : y + ys, z + k : z + k + BZ]
            total = total + STENCIL[k] * ((pair_x + pair_y) + pair_z)
        local = pot[i, y0 : y0 + ys] - shift
        return (scale * KINETIC) * total + scale * (local * centre)

    second = coef_ref[7]
    for q in range(CELLS // LANES):
        cells = slice(q * LANES, (q + 1) * LANES)
        tile = jnp.transpose(x_ref[:, cells]).reshape(LANES // BZ, BZ, LANES)
        at = q % (HALF // LANES) * LANES
        own, other = v_own_ref[:, at : at + LANES], v_other_ref[:, at : at + LANES]
        swap = second > 0.5 if q < HALF // LANES else second < 0.5
        vtile = jnp.transpose(jnp.where(swap, other, own)).reshape(LANES // BZ, BZ, LANES)
        for r in range(LANES // BZ):
            row = q * (LANES // BZ) + r
            ea[OX + row // BY, OY + row % BY, OZ : OZ + BZ] = tile[r]
            pot[row // BY, row % BY] = vtile[r]

    ys = BY // 2

    def first(i, carry):
        for y0 in range(0, BY, ys):
            eb[i + OX, OY + y0 : OY + y0 + ys, OZ : OZ + BZ] = image(ea, i, y0, ys, coef_ref[0], coef_ref[1])
        return carry

    def later(src, dst, scale, back):
        def body(i, squares):
            for y0 in range(0, BY, ys):
                new = image(src, i, y0, ys, scale, coef_ref[1]) - back * part(dst, i, y0, ys)
                dst[i + OX, OY + y0 : OY + y0 + ys, OZ : OZ + BZ] = new
                squares = squares + jnp.sum(new * new, axis=0)
            return squares

        return body

    def last(i, carry):
        for y0 in range(0, BY, ys):
            img[i, y0 : y0 + ys] = image(eb, i, y0, ys, 1.0, 0.0)
        return carry

    zero = jnp.zeros((BZ, LANES), jnp.float32)
    spread(ea)
    lax.fori_loop(0, BX, first, 0)
    spread(eb)
    lax.fori_loop(0, BX, later(eb, ea, coef_ref[2], coef_ref[3]), zero)
    spread(ea)
    squares = lax.fori_loop(0, BX, later(ea, eb, coef_ref[4], coef_ref[5]), zero)
    spread(eb)
    lax.fori_loop(0, BX, last, 0)
    norm = jnp.sqrt(jnp.sum(squares, keepdims=True))
    for q in range(CELLS // LANES):
        rows = [q * (LANES // BZ) + r for r in range(LANES // BZ)]
        at = q // (HALF // LANES) * CELLS + q % (HALF // LANES) * LANES
        field = jnp.concatenate([eb[OX + r // BY, OY + r % BY, OZ : OZ + BZ] for r in rows], 0)
        out_ref[:, at : at + LANES] = jnp.transpose(field / norm)
        field = jnp.concatenate([img[r // BY, r % BY] for r in rows], 0)
        out_ref[:, at + HALF : at + HALF + LANES] = jnp.transpose(field / norm)


def filtered_fields(coef, x, v_own, v_other):
    vmem = pl.BlockSpec(memory_space=pltpu.VMEM)
    return pl.pallas_call(
        filter_kernel,
        out_shape=jax.ShapeDtypeStruct((BLOCKS, 2 * CELLS), jnp.float32),
        in_specs=[pl.BlockSpec(memory_space=pltpu.SMEM), vmem, vmem, vmem],
        out_specs=vmem,
        scratch_shapes=[
            pltpu.VMEM(EXT, jnp.float32),
            pltpu.VMEM(EXT, jnp.float32),
            pltpu.VMEM((BX, BY, BZ, LANES), jnp.float32),
            pltpu.VMEM((BX, BY, BZ, LANES), jnp.float32),
        ],
        compiler_params=pltpu.CompilerParams(vmem_limit_bytes=40 * 1024 * 1024),
    )(coef, x, v_own, v_other)


def filter_coefficients(bounds, second):
    lowest, cutoff, highest = bounds[0], bounds[1], bounds[2]
    half_width = (highest - cutoff) / 2.0
    centre = (highest + cutoff) / 2.0
    s1 = half_width / (lowest - centre)
    tau = 2.0 / s1
    s2 = 1.0 / (tau - s1)
    s3 = 1.0 / (tau - s2)
    return jnp.stack(
        [
            s1 / half_width,
            centre,
            2.0 * s2 / half_width,
            s1 * s2,
            2.0 * s3 / half_width,
            s2 * s3,
            jnp.float32(0.0),
            second,
        ]
    )


def contract(left, right, dims):
    return lax.dot_general(
        left,
        right,
        (dims, ((), ())),
        precision=lax.Precision.HIGH,
        preferred_element_type=jnp.float32,
    )


def local(orbitals, potential, bounds, rotation):
    width = rotation.shape[1]
    band = lax.axis_index("band")
    z_hi, core = band // 2, band % 2
    coef = filter_coefficients(bounds, core.astype(jnp.float32))
    rotation_far = lax.ppermute(rotation, "band", Z_SWAP)

    fields = orbitals.reshape(CELLS, width).T
    half = lax.dynamic_slice_in_dim(potential.reshape(CELLS), core * HALF, HALF)
    sent = jnp.concatenate([fields, jnp.broadcast_to(half[None], (BLOCKS, HALF))], axis=1)
    got = lax.all_to_all(sent, "dom", 0, 0, tiled=True, axis_index_groups=[ORDER])
    v_own = got[:, CELLS:]
    v_other = lax.ppermute(v_own, "band", CORE_SWAP)
    images = filtered_fields(coef, got[:, :CELLS], v_own, v_other)

    got = exchange(images.reshape(2 * BLOCKS, CELLS), CORE_GROUPS)
    got = got.reshape(BLOCKS, 2, 2, HALF).transpose(1, 2, 0, 3)
    phi = got[:, 0].reshape(2 * BLOCKS, HALF)
    phi_other = lax.ppermute(phi, "band", CORE_SWAP)
    phi_all = jnp.concatenate([phi, phi_other], axis=0)
    columns = got.transpose(1, 0, 2, 3).reshape(4 * BLOCKS, HALF)
    gram = contract(phi_all, columns, ((1,), (1,)))

    def by_core(weights):
        weights = weights.reshape(2, 2, BLOCKS, width)
        swapped = jnp.where(core == 0, weights, weights[:, ::-1])
        return swapped.transpose(1, 0, 2, 3).reshape(4 * BLOCKS, width)

    rotated_far = contract(phi_all, by_core(rotation_far), ((0,), (0,)))
    rotated_far = lax.ppermute(rotated_far, "band", Z_SWAP)
    rotated_near = contract(phi_all, by_core(rotation), ((0,), (0,)))

    terms = exchange(gram.reshape(4, BLOCKS, 4 * BLOCKS), X_GROUPS)
    terms = jnp.sum(terms, axis=0)
    terms = terms.reshape(32, 4, 2, 2, BLOCKS).transpose(0, 3, 1, 2, 4).reshape(64, 8 * BLOCKS)
    terms = jnp.sum(exchange(terms, PLANE_GROUPS), axis=0)
    whole = lax.all_to_all(
        jnp.broadcast_to(terms[None], (BLOCKS, 8 * BLOCKS)), "dom", 0, 0, tiled=True
    )
    whole = whole.reshape(8, 2, 2, 4, 4, 2, BLOCKS).transpose(5, 2, 1, 0, 3, 4, 6)
    whole = whole.reshape(2, 2, 2, BLOCKS, BLOCKS)
    whole = jnp.where(core == 0, whole, whole[:, :, ::-1])
    whole = whole.reshape(2, 4 * BLOCKS, BLOCKS)
    lower = jnp.where(z_hi == 0, rotated_near, rotated_far)
    upper = jnp.where(z_hi == 0, rotated_far, rotated_near)
    rotated = jnp.concatenate([lower, upper], axis=0).reshape(1, BX, BY, BZ, width)
    return (rotated, whole[0], whole[1])


def solution(mesh):
    in_specs = (
        P("dom", None, None, None, "band"),
        P("dom", None, None, None),
        P(),
        P(None, "band"),
    )
    out_specs = (P("dom", None, None, None, "band"), P(None, "band"), P(None, "band"))
    return jax.shard_map(local, mesh=mesh, in_specs=in_specs, out_specs=out_specs, check_vma=False)
```

time: 2020 us -> 242 us (0.12)
  the two profiles are of different devices: /device:TPU:32 before, /device:TPU:1 now
where the time goes in v1:
time: 242 us; the launch traced here: 241 us
  blocking collectives  121 us (50%)
  waiting for transfers between devices  44.6 us (18%)
  starting transfers between devices  32.6 us (13%)
  Pallas kernels  14.7 us (6%)
  local copies, waits for them, and re-layouts  11.6 us (5%)
  other arithmetic  8.13 us (3%)
  between operations  4.44 us (2%)
  matrix products  4.28 us (2%)
    all_to_all x2, blocking collectives, exchange(): lax.all_to_all(x, ('band', 'dom'), 0, 0, tiled=True, axis_index_groups=gr...  73 us
    all_to_all x1, blocking collectives, local(): lax.all_to_all(sent, 'dom', 0, 0, tiled=True, axis_index_groups=[ORDER])  48 us
    ppermute x1, waiting for transfers between devices, local(): rotated_far = lax.ppermute(rotated_far, 'band', Z_SWAP)  25.8 us
    ppermute x1, waiting for transfers between devices, local(): rotation_far = lax.ppermute(rotation, 'band', Z_SWAP)  17.2 us
    pallas_call x1, Pallas kernels, filtered_fields(): pl.pallas_call(filter_kernel, out_shape=jax.ShapeDtypeStruct((BLOCKS, 2 *...  14.7 us
    all_to_all x1, starting transfers between devices, local(): lax.all_to_all(jnp.broadcast_to(terms[None], (BLOCKS, 8 * BLOCKS)), 'dom'...  8.09 us
    ppermute x1, starting transfers between devices, local(): rotation_far = lax.ppermute(rotation, 'band', Z_SWAP)  6.83 us
    all_to_all x1, starting transfers between devices, exchange(): lax.all_to_all(x, ('band', 'dom'), 0, 0, tiled=True, axis_index_groups=gr...  5.78 us
  transfers between devices with their start and end apart: 6, of which 3 were waited for; matrix products, arithmetic and copies ran while one was open for 2% of the time, Pallas kernels for 0%

profile of v1, /device:TPU:1, one launch (start us, length us, event | category | flops | bytes accessed | tf_op | source)
XLA Modules:
  0.0 241.4 jit_solution(16511899926564127353)
XLA Ops:
  1.6 1.5 maximum_bitcast_fusion
  3.1 1.6 copy.23
  4.7 48.0 %all_to_all.42 = f32[128,1,2304]{2,1,0:T(1,128)S(1)} all-to-all(f32[128,1,2304]{2,1,0:T(1,128)S(1)} %copy.23), channel_id=1, replica_groups={{0,8,16,24,32,40,48,56,64,72,80,88,96,104,112,120,1,9,17,25,33,41,49,57..., dimensions={0} | all-to-all | bytes 2359296 | tf_op jit(solution)/shard_map/all_to_all | solution.py:222
  52.8 4.6 %collective-permute-start = (f32[128,768]{1,0:T(8,128)S(1)}, f32[128,768]{1,0:T(8,128)S(1)}, u32[]{:S(2)}, u32[]{:S(2)}) collective-permute-start(f32[128,768]{1,0:T(8,128)S(1)} %slice.35.v_own_ref), channel_id=1, source_target_pairs={{0,128},{128,0},{256,384},{384,256},{1,129},{129,1},{257,385},{385... | collective-permute-start | bytes 1179656 | tf_op jit(solution)/shard_map/ppermute | solution.py:224
  61.8 14.7 %shard_map.67 = f32[128,3072]{1,0:T(8,128)S(1)} custom-call(f32[8]{0:T(128)S(1)} %stack.28.coef_ref, f32[128,1536]{1,0:T(8,128)S(1)} %slice.34.x_ref, f32[128,768]{1,0:T(8,128)S(1)} %slice.35.v_own_ref, f32[128,768]{1,0:T(8,128)S(1)} %collective-permute-done.v_other_ref), custom_call_target="tpu_custom_call" | custom-call | tf_op jit(solution)/shard_map/pallas_call | solution.py:165
  76.5 1.9 all_to_all.36
  78.4 56.3 %all_to_all.43 = f32[256,1,1536]{2,1,0:T(1,128)S(1)} all-to-all(f32[256,1,1536]{2,1,0:T(1,128)S(1)} %all_to_all.36), channel_id=1, replica_groups={{0,256,8,264,16,272,24,280,32,288,40,296,48,304,56,312,64,320,72,328,80..., dimensions={0} | all-to-all | bytes 3145728 | tf_op jit(solution)/shard_map/all_to_all | solution.py:58
  134.6 5.3 %reduce.1 = f32[256,1536]{1,0:T(8,128)} reduce(f32[256,1,1536]{2,1,0:T(1,128)S(1)} %all_to_all.43, f32[]{:T(128)} %constant.50), dimensions={1}, to_apply=%all_to_all.31.reduce_sub_computation | reduce | bytes 3145732 | tf_op jit(solution)/shard_map/all_to_all | solution.py:58
  139.9 2.3 reshape.78
  142.8 4.1 %collective-permute-start.1 = (f32[256,768]{1,0:T(8,128)S(1)}, f32[256,768]{1,0:T(8,128)S(1)}, u32[]{:S(2)}, u32[]{:S(2)}) collective-permute-start(f32[256,768]{1,0:T(8,128)S(1)} %bitcast.45), channel_id=1, source_target_pairs={{0,128},{128,0},{256,384},{384,256},{1,129},{129,1},{257,385},{385... | collective-permute-start | bytes 2359304 | tf_op jit(solution)/shard_map/ppermute | solution.py:230
  147.3 1.6 collective-permute-done.1
  149.0 1.5 fusion.6
  150.5 16.8 %all_to_all.44 = f32[4,128,512]{2,1,0:T(8,128)S(1)} all-to-all(f32[4,128,512]{2,1,0:T(8,128)S(1)} %fusion.6), channel_id=1, replica_groups={{0,4,8,12},{1,5,9,13},{2,6,10,14},{3,7,11,15},{16,20,24,28},{17,21,25,2..., dimensions={0} | all-to-all | bytes 2097152 | tf_op jit(solution)/shard_map/all_to_all | solution.py:58
  167.5 0.8 copy.29
  168.4 5.8 %all-to-all-start.3 = ((f32[64,1,1024]{2,1,0:T(1,128)}), f32[64,1,1024]{2,1,0:T(1,128)S(1)}, u32[]{:S(2)}, u32[]{:S(2)}) async-start(f32[64,1,1024]{2,1,0:T(1,128)} %bitcast.25), calls=%async_computation.3 | async-start | bytes 524288 | tf_op jit(solution)/shard_map/all_to_all | solution.py:58
  174.2 6.8 %collective-permute-start.2 = (f32[512,128]{1,0:T(8,128)S(1)}, f32[512,128]{1,0:T(8,128)S(1)}, u32[]{:S(2)}, u32[]{:S(2)}) collective-permute-start(f32[512,128]{1,0:T(8,128)S(1)} %copy-done), channel_id=1, source_target_pairs={{0,256},{256,0},{128,384},{384,128},{1,257},{257,1},{129,385},{385... | collective-permute-start | bytes 786440 | tf_op jit(solution)/shard_map/ppermute | solution.py:217
  181.0 17.2 %collective-permute-done.2 = f32[512,128]{1,0:T(8,128)S(1)} collective-permute-done((f32[512,128]{1,0:T(8,128)S(1)}, f32[512,128]{1,0:T(8,128)S(1)}, u32[]{:S(2)}, u32[]{:S(2)}) %collective-permute-start.2) | collective-permute-done | bytes 262176 | tf_op jit(solution)/shard_map/ppermute | solution.py:217
  198.4 1.1 broadcast_in_dim.5
  199.5 8.1 %all-to-all-start.4 = ((f32[128,1,1024]{2,1,0:T(1,128)}), f32[128,1,1024]{2,1,0:T(1,128)S(1)}, u32[]{:S(2)}, u32[]{:S(2)}) async-start(f32[128,1,1024]{2,1,0:T(1,128)} %broadcast_in_dim.5), calls=%async_computation.4 | async-start | bytes 1048576 | tf_op jit(solution)/shard_map/all_to_all | solution.py:248
  207.6 1.4 fusion.2
  209.0 3.2 %collective-permute-start.3 = (f32[768,128]{1,0:T(8,128)S(1)}, f32[768,128]{1,0:T(8,128)S(1)}, u32[]{:S(2)}, u32[]{:S(2)}) collective-permute-start(f32[768,128]{1,0:T(8,128)S(1)} %fusion.2), channel_id=1, source_target_pairs={{0,256},{256,0},{128,384},{384,128},{1,257},{257,1},{129,385},{385... | collective-permute-start | bytes 1179656 | tf_op jit(solution)/shard_map/ppermute | solution.py:241
  212.2 25.8 %collective-permute-done.3 = f32[768,128]{1,0:T(8,128)S(1)} collective-permute-done((f32[768,128]{1,0:T(8,128)S(1)}, f32[768,128]{1,0:T(8,128)S(1)}, u32[]{:S(2)}, u32[]{:S(2)}) %collective-permute-start.3) | collective-permute-done | bytes 393248 | tf_op jit(solution)/shard_map/ppermute | solution.py:241
  238.0 1.4 broadcast_select_fusion.1
  239.4 0.9 pad_maximum_fusion.1
  (32 shorter events, 4.4 us)
Async XLA Ops:
  52.7 4.8 %copy-start.2 = (f32[3]{0:T(128)S(1)}, f32[3]{0:T(128)}, u32[]{:S(2)}) copy-start(f32[3]{0:T(128)} %param.6) | copy-start | bytes 40
  52.8 8.9 %collective-permute-start = (f32[128,768]{1,0:T(8,128)S(1)}, f32[128,768]{1,0:T(8,128)S(1)}, u32[]{:S(2)}, u32[]{:S(2)}) collective-permute-start(f32[128,768]{1,0:T(8,128)S(1)} %slice.35.v_own_ref), channel_id=1, source_target_pairs={{0,128},{128,0},{256,384},{384,256},{1,129},{129,1},{257,385},{385... | collective-permute-start | bytes 1179656 | tf_op jit(solution)/shard_map/ppermute | solution.py:224
  142.8 6.0 %collective-permute-start.1 = (f32[256,768]{1,0:T(8,128)S(1)}, f32[256,768]{1,0:T(8,128)S(1)}, u32[]{:S(2)}, u32[]{:S(2)}) collective-permute-start(f32[256,768]{1,0:T(8,128)S(1)} %bitcast.45), channel_id=1, source_target_pairs={{0,128},{128,0},{256,384},{384,256},{1,129},{129,1},{257,385},{385... | collective-permute-start | bytes 2359304 | tf_op jit(solution)/shard_map/ppermute | solution.py:230
  167.3 6.9 %copy-start = (f32[512,128]{1,0:T(8,128)S(1)}, f32[512,128]{1,0:T(8,128)}, u32[]{:S(2)}) copy-start(f32[512,128]{1,0:T(8,128)} %param.7) | copy-start | bytes 786436
  168.4 29.8 %all-to-all-start.3 = ((f32[64,1,1024]{2,1,0:T(1,128)}), f32[64,1,1024]{2,1,0:T(1,128)S(1)}, u32[]{:S(2)}, u32[]{:S(2)}) async-start(f32[64,1,1024]{2,1,0:T(1,128)} %bitcast.25), calls=%async_computation.3 | async-start | bytes 524288 | tf_op jit(solution)/shard_map/all_to_all | solution.py:58
  174.2 24.0 %collective-permute-start.2 = (f32[512,128]{1,0:T(8,128)S(1)}, f32[512,128]{1,0:T(8,128)S(1)}, u32[]{:S(2)}, u32[]{:S(2)}) collective-permute-start(f32[512,128]{1,0:T(8,128)S(1)} %copy-done), channel_id=1, source_target_pairs={{0,256},{256,0},{128,384},{384,128},{1,257},{257,1},{129,385},{385... | collective-permute-start | bytes 786440 | tf_op jit(solution)/shard_map/ppermute | solution.py:217
  199.5 12.7 %copy-start.1 = (f32[512,128]{1,0:T(8,128)S(1)}, f32[512,128]{1,0:T(8,128)}, u32[]{:S(2)}) copy-start(f32[512,128]{1,0:T(8,128)} %param.7) | copy-start | bytes 786436
  199.5 40.9 %all-to-all-start.4 = ((f32[128,1,1024]{2,1,0:T(1,128)}), f32[128,1,1024]{2,1,0:T(1,128)S(1)}, u32[]{:S(2)}, u32[]{:S(2)}) async-start(f32[128,1,1024]{2,1,0:T(1,128)} %broadcast_in_dim.5), calls=%async_computation.4 | async-start | bytes 1048576 | tf_op jit(solution)/shard_map/all_to_all | solution.py:248
  209.0 29.1 %collective-permute-start.3 = (f32[768,128]{1,0:T(8,128)S(1)}, f32[768,128]{1,0:T(8,128)S(1)}, u32[]{:S(2)}, u32[]{:S(2)}) collective-permute-start(f32[768,128]{1,0:T(8,128)S(1)} %fusion.2), channel_id=1, source_target_pairs={{0,256},{256,0},{128,384},{384,128},{1,257},{257,1},{129,385},{385... | collective-permute-start | bytes 1179656 | tf_op jit(solution)/shard_map/ppermute | solution.py:241

commit v2 on v1

--- a/solution.py
+++ b/solution.py
@@ -25,6 +25,9 @@
 PX, PY, PZ = 4, 4, 8
 BLOCKS = PX * PY * PZ
 LANES = 128
+TILES = CELLS // LANES
+HALF_TILES = HALF // LANES
+SENT = TILES + HALF_TILES
 
 ORDER = [(ix * PY + iy) * PZ + iz for iz in range(PZ) for ix in range(PX) for iy in range(PY)]
 STEP_X, STEP_Y, STEP_Z = PY, 1, PX * PY
@@ -62,7 +65,55 @@
 EXT = (BX + 2 * REACH, BY + 2 * REACH, BZ + 16, LANES)
 
 
-def filter_kernel(coef_ref, x_ref, v_own_ref, v_other_ref, out_ref, ea, eb, pot, img):
+def pack_kernel(core_ref, orbitals_ref, potential_ref, out_ref, wide):
+    for t in range(TILES):
+        tile = orbitals_ref[t * LANES : (t + 1) * LANES]
+        out_ref[pl.ds(t, BLOCKS, stride=SENT), :] = jnp.transpose(tile)
+    wide[...] = jnp.concatenate([potential_ref[i] for i in range(BX)], axis=1)
+    for s in range(HALF_TILES):
+        row = wide[pl.ds(core_ref[0] * HALF_TILES + s, 1), :]
+        out_ref[pl.ds(TILES + s, BLOCKS, stride=SENT), :] = jnp.broadcast_to(row, (BLOCKS, LANES))
+
+
+def packed(core, orbitals, potential):
+    vmem = pl.BlockSpec(memory_space=pltpu.VMEM)
+    return pl.pallas_call(
+        pack_kernel,
+        out_shape=jax.ShapeDtypeStruct((BLOCKS * SENT, LANES), jnp.float32),
+        in_specs=[pl.BlockSpec(memory_space=pltpu.SMEM), vmem, vmem],
+        out_specs=vmem,
+        scratch_shapes=[pltpu.VMEM((BY, BX * BZ), jnp.float32)],
+        compiler_params=pltpu.CompilerParams(vmem_limit_bytes=16 * 1024 * 1024),
+    )(core, orbitals, potential)
+
+
+def split_kernel(got_ref, phi_ref, both_ref):
+    for m in range(2):
+        for h in range(2):
+            for t in range(HALF_TILES):
+                tile = got_ref[pl.ds(h * TILES + m * HALF_TILES + t, BLOCKS, stride=2 * TILES), :]
+                cells = slice(t * LANES, (t + 1) * LANES)
+                at = (2 * m + h) * BLOCKS
+                both_ref[at : at + BLOCKS, cells] = tile
+                if m == 0:
+                    phi_ref[at : at + BLOCKS, cells] = tile
+
+
+def split_fields(got):
+    vmem = pl.BlockSpec(memory_space=pltpu.VMEM)
+    return pl.pallas_call(
+        split_kernel,
+        out_shape=(
+            jax.ShapeDtypeStruct((2 * BLOCKS, HALF), jnp.float32),
+            jax.ShapeDtypeStruct((4 * BLOCKS, HALF), jnp.float32),
+        ),
+        in_specs=[vmem],
+        out_specs=(vmem, vmem),
+        compiler_params=pltpu.CompilerParams(vmem_limit_bytes=16 * 1024 * 1024),
+    )(got)
+
+
+def filter_kernel(coef_ref, got_ref, v_other_ref, out_ref, ea, eb, pot, img):
     lane = lax.broadcasted_iota(jnp.int32, (1, LANES), 1)
     iz, ix, iy = lane // STEP_Z, lane // STEP_X % PX, lane % PY
 
@@ -107,17 +158,17 @@
         return (scale * KINETIC) * total + scale * (local * centre)
 
     second = coef_ref[7]
-    for q in range(CELLS // LANES):
-        cells = slice(q * LANES, (q + 1) * LANES)
-        tile = jnp.transpose(x_ref[:, cells]).reshape(LANES // BZ, BZ, LANES)
-        at = q % (HALF // LANES) * LANES
-        own, other = v_own_ref[:, at : at + LANES], v_other_ref[:, at : at + LANES]
-        swap = second > 0.5 if q < HALF // LANES else second < 0.5
-        vtile = jnp.transpose(jnp.where(swap, other, own)).reshape(LANES // BZ, BZ, LANES)
+    for q in range(TILES):
+        tile = jnp.transpose(got_ref[pl.ds(q, BLOCKS, stride=SENT), :]).reshape(LANES // BZ, BZ, LANES)
         for r in range(LANES // BZ):
             row = q * (LANES // BZ) + r
             ea[OX + row // BY, OY + row % BY, OZ : OZ + BZ] = tile[r]
-            pot[row // BY, row % BY] = vtile[r]
+    for y in range(BY):
+        s = y % HALF_TILES
+        own = got_ref[pl.ds(TILES + s, BLOCKS, stride=SENT), :]
+        other = v_other_ref[pl.ds(s, BLOCKS, stride=HALF_TILES), :]
+        swap = second > 0.5 if y < HALF_TILES else second < 0.5
+        pot[:, y] = jnp.transpose(jnp.where(swap, other, own)).reshape(BX, BZ, LANES)
 
     ys = BY // 2
 
@@ -151,21 +202,21 @@
     spread(eb)
     lax.fori_loop(0, BX, last, 0)
     norm = jnp.sqrt(jnp.sum(squares, keepdims=True))
-    for q in range(CELLS // LANES):
+    for q in range(TILES):
         rows = [q * (LANES // BZ) + r for r in range(LANES // BZ)]
-        at = q // (HALF // LANES) * CELLS + q % (HALF // LANES) * LANES
+        at = q // HALF_TILES * TILES + q % HALF_TILES
         field = jnp.concatenate([eb[OX + r // BY, OY + r % BY, OZ : OZ + BZ] for r in rows], 0)
-        out_ref[:, at : at + LANES] = jnp.transpose(field / norm)
+        out_ref[pl.ds(at, BLOCKS, stride=2 * TILES), :] = jnp.transpose(field / norm)
         field = jnp.concatenate([img[r // BY, r % BY] for r in rows], 0)
-        out_ref[:, at + HALF : at + HALF + LANES] = jnp.transpose(field / norm)
-
-
-def filtered_fields(coef, x, v_own, v_other):
+        out_ref[pl.ds(at + HALF_TILES, BLOCKS, stride=2 * TILES), :] = jnp.transpose(field / norm)
+
+
+def filtered_fields(coef, got, v_other):
     vmem = pl.BlockSpec(memory_space=pltpu.VMEM)
     return pl.pallas_call(
         filter_kernel,
-        out_shape=jax.ShapeDtypeStruct((BLOCKS, 2 * CELLS), jnp.float32),
-        in_specs=[pl.BlockSpec(memory_space=pltpu.SMEM), vmem, vmem, vmem],
+        out_shape=jax.ShapeDtypeStruct((BLOCKS * 2 * TILES, LANES), jnp.float32),
+        in_specs=[pl.BlockSpec(memory_space=pltpu.SMEM), vmem, vmem],
         out_specs=vmem,
         scratch_shapes=[
             pltpu.VMEM(EXT, jnp.float32),
@@ -174,7 +225,7 @@
             pltpu.VMEM((BX, BY, BZ, LANES), jnp.float32),
         ],
         compiler_params=pltpu.CompilerParams(vmem_limit_bytes=40 * 1024 * 1024),
-    )(coef, x, v_own, v_other)
+    )(coef, got, v_other)
 
 
 def filter_coefficients(bounds, second):
@@ -216,37 +267,47 @@
     coef = filter_coefficients(bounds, core.astype(jnp.float32))
     rotation_far = lax.ppermute(rotation, "band", Z_SWAP)
 
-    fields = orbitals.reshape(CELLS, width).T
-    half = lax.dynamic_slice_in_dim(potential.reshape(CELLS), core * HALF, HALF)
-    sent = jnp.concatenate([fields, jnp.broadcast_to(half[None], (BLOCKS, HALF))], axis=1)
-    got = lax.all_to_all(sent, "dom", 0, 0, tiled=True, axis_index_groups=[ORDER])
-    v_own = got[:, CELLS:]
-    v_other = lax.ppermute(v_own, "band", CORE_SWAP)
-    images = filtered_fields(coef, got[:, :CELLS], v_own, v_other)
-
-    got = exchange(images.reshape(2 * BLOCKS, CELLS), CORE_GROUPS)
-    got = got.reshape(BLOCKS, 2, 2, HALF).transpose(1, 2, 0, 3)
-    phi = got[:, 0].reshape(2 * BLOCKS, HALF)
+    sent = packed(core.reshape(1), orbitals.reshape(CELLS, width), potential[0])
+    got = lax.all_to_all(
+        sent.reshape(BLOCKS, 1, SENT * LANES), "dom", 0, 0, tiled=True, axis_index_groups=[ORDER]
+    )
+    got, rotation_far = lax.optimization_barrier((got, rotation_far))
+    v_other = lax.ppermute(got[:, :, CELLS:], "band", CORE_SWAP)
+    images = filtered_fields(
+        coef, got.reshape(BLOCKS * SENT, LANES), v_other.reshape(BLOCKS * HALF_TILES, LANES)
+    )
+
+    got = exchange(images.reshape(2 * BLOCKS, 1, CELLS), CORE_GROUPS)
+    phi, both = split_fields(got.reshape(2 * BLOCKS * TILES, LANES))
     phi_other = lax.ppermute(phi, "band", CORE_SWAP)
-    phi_all = jnp.concatenate([phi, phi_other], axis=0)
-    columns = got.transpose(1, 0, 2, 3).reshape(4 * BLOCKS, HALF)
-    gram = contract(phi_all, columns, ((1,), (1,)))
+    gram = jnp.concatenate(
+        [contract(phi, both, ((1,), (1,))), contract(phi_other, both, ((1,), (1,)))], axis=0
+    )
 
     def by_core(weights):
         weights = weights.reshape(2, 2, BLOCKS, width)
         swapped = jnp.where(core == 0, weights, weights[:, ::-1])
         return swapped.transpose(1, 0, 2, 3).reshape(4 * BLOCKS, width)
 
-    rotated_far = contract(phi_all, by_core(rotation_far), ((0,), (0,)))
+    def rotate(weights):
+        weights = by_core(weights)
+        return contract(phi, weights[: 2 * BLOCKS], ((0,), (0,))) + contract(
+            phi_other, weights[2 * BLOCKS :], ((0,), (0,))
+        )
+
+    rotated_far = rotate(rotation_far)
+    gram, rotated_far = lax.optimization_barrier((gram, rotated_far))
     rotated_far = lax.ppermute(rotated_far, "band", Z_SWAP)
-    rotated_near = contract(phi_all, by_core(rotation), ((0,), (0,)))
+    rotated_near = rotate(rotation)
 
     terms = exchange(gram.reshape(4, BLOCKS, 4 * BLOCKS), X_GROUPS)
     terms = jnp.sum(terms, axis=0)
     terms = terms.reshape(32, 4, 2, 2, BLOCKS).transpose(0, 3, 1, 2, 4).reshape(64, 8 * BLOCKS)
-    terms = jnp.sum(exchange(terms, PLANE_GROUPS), axis=0)
+    terms = exchange(terms.reshape(64, 1, 8 * BLOCKS), PLANE_GROUPS)
+    terms, rotated_far = lax.optimization_barrier((terms, rotated_far))
+    terms = jnp.sum(terms, axis=0)
     whole = lax.all_to_all(
-        jnp.broadcast_to(terms[None], (BLOCKS, 8 * BLOCKS)), "dom", 0, 0, tiled=True
+        jnp.broadcast_to(terms[None], (BLOCKS, 1, 8 * BLOCKS)), "dom", 0, 0, tiled=True
     )
     whole = whole.reshape(8, 2, 2, 4, 4, 2, BLOCKS).transpose(5, 2, 1, 0, 3, 4, 6)
     whole = whole.reshape(2, 2, 2, BLOCKS, BLOCKS)

time: 242 us -> 235 us (0.971)
  blocking collectives: 121 us -> 16.8 us
  waiting for transfers between devices: 44.6 us -> 111 us
  starting transfers between devices: 32.6 us -> 70.6 us
  other arithmetic: 8.13 us -> 1.35 us
  local copies, waits for them, and re-layouts: 11.6 us -> 6.96 us
    all_to_all x2 -> x1, blocking collectives: 73 us -> 16.8 us  [exchange(): lax.all_to_all(x, ('band', 'dom'), 0, 0, tiled=True, axis_index_groups=gr...]
    all_to_all x1 -> x0, blocking collectives: 48 us -> none  [local(): lax.all_to_all(sent, 'dom', 0, 0, tiled=True, axis_index_groups=[ORDER])]
    all_to_all x1 -> x2, waiting for transfers between devices: 0.01 us -> 40.5 us  [exchange(): lax.all_to_all(x, ('band', 'dom'), 0, 0, tiled=True, axis_index_groups=gr...]
    all_to_all x1 -> x2, starting transfers between devices: 8.09 us -> 25.9 us  [the longest x1 17.9 us: local(): lax.all_to_all(sent.reshape(BLOCKS, 1, SENT * LANES), 'dom', 0, 0, tiled=...]
    all_to_all x1 -> x2, starting transfers between devices: 5.78 us -> 22.4 us  [exchange(): lax.all_to_all(x, ('band', 'dom'), 0, 0, tiled=True, axis_index_groups=gr...]
    ppermute x1, waiting for transfers between devices: 17.2 us -> 32.8 us  [local(): rotation_far = lax.ppermute(rotation, 'band', Z_SWAP)]
    all_to_all x1 -> x2, waiting for transfers between devices: 0.01 us -> 15.3 us  [the longest x1 15.3 us: local(): lax.all_to_all(jnp.broadcast_to(terms[None], (BLOCKS, 1, 8 * BLOCKS)), 'd...]
    all_to_all x2 -> x0, other arithmetic: 6.75 us -> none  [the longest x1 5.26 us: exchange(): lax.all_to_all(x, ('band', 'dom'), 0, 0, tiled=True, axis_index_groups=gr...]
  transfers between devices with their start and end apart: 6 -> 8, of which waited for: 3 -> 4; matrix products, arithmetic and copies ran while one was open for 2% -> 2% of each run, Pallas kernels for 0% -> 0%
where the time goes in v2:
time: 235 us; the launch traced here: 233 us
  waiting for transfers between devices  111 us (47%)
  starting transfers between devices  70.6 us (30%)
  blocking collectives  16.8 us (7%)
  Pallas kernels  16.4 us (7%)
  local copies, waits for them, and re-layouts  6.96 us (3%)
  matrix products  4.89 us (2%)
  between operations  4.42 us (2%)
    all_to_all x2, waiting for transfers between devices, exchange(): lax.all_to_all(x, ('band', 'dom'), 0, 0, tiled=True, axis_index_groups=gr...  40.5 us
    ppermute x1, waiting for transfers between devices, local(): rotation_far = lax.ppermute(rotation, 'band', Z_SWAP)  32.8 us
    ppermute x1, waiting for transfers between devices, local(): rotated_far = lax.ppermute(rotated_far, 'band', Z_SWAP)  22.8 us
    all_to_all x2, starting transfers between devices, exchange(): lax.all_to_all(x, ('band', 'dom'), 0, 0, tiled=True, axis_index_groups=gr...  22.4 us
    all_to_all x1, starting transfers between devices, local(): lax.all_to_all(sent.reshape(BLOCKS, 1, SENT * LANES), 'dom', 0, 0, tiled=...  17.9 us
    all_to_all x1, blocking collectives, exchange(): lax.all_to_all(x, ('band', 'dom'), 0, 0, tiled=True, axis_index_groups=gr...  16.8 us
    all_to_all x1, waiting for transfers between devices, local(): lax.all_to_all(jnp.broadcast_to(terms[None], (BLOCKS, 1, 8 * BLOCKS)), 'd...  15.3 us
    pallas_call x1, Pallas kernels, filtered_fields(): pl.pallas_call(filter_kernel, out_shape=jax.ShapeDtypeStruct((BLOCKS * 2...  14.7 us
  transfers between devices with their start and end apart: 8, of which 4 were waited for; matrix products, arithmetic and copies ran while one was open for 2% of the time, Pallas kernels for 0%

profile of v2, /device:TPU:1, one launch (start us, length us, event | category | flops | bytes accessed | tf_op | source)
XLA Modules:
  0.0 232.8 jit_solution(4282482904279782214)
XLA Ops:
  0.6 0.8 copy.19
  1.5 1.1 copy-done.1
  2.6 1.4 shard_map.67
  4.0 17.9 %all-to-all-start = ((f32[128,1,2304]{2,1,0:T(1,128)}), f32[128,1,2304]{2,1,0:T(1,128)S(1)}, u32[]{:S(2)}, u32[]{:S(2)}) async-start(f32[128,1,2304]{2,1,0:T(1,128)} %bitcast.11), calls=%async_computation | async-start | bytes 2359296 | tf_op jit(solution)/shard_map/all_to_all | solution.py:271
  21.9 7.9 %collective-permute-start = (f32[512,128]{1,0:T(8,128)S(1)}, f32[512,128]{1,0:T(8,128)S(1)}, u32[]{:S(2)}, u32[]{:S(2)}) collective-permute-start(f32[512,128]{1,0:T(8,128)S(1)} %copy-done.2), channel_id=1, source_target_pairs={{0,256},{256,0},{128,384},{384,128},{1,257},{257,1},{129,385},{385... | collective-permute-start | bytes 786440 | tf_op jit(solution)/shard_map/ppermute | solution.py:268
  29.8 32.8 %collective-permute-done = f32[512,128]{1,0:T(8,128)S(1)} collective-permute-done((f32[512,128]{1,0:T(8,128)S(1)}, f32[512,128]{1,0:T(8,128)S(1)}, u32[]{:S(2)}, u32[]{:S(2)}) %collective-permute-start) | collective-permute-done | bytes 262176 | tf_op jit(solution)/shard_map/ppermute | solution.py:268
  62.8 3.2 %collective-permute-start.1 = (f32[128,1,768]{2,1,0:T(1,128)S(1)}, f32[128,1,768]{2,1,0:T(1,128)S(1)}, u32[]{:S(2)}, u32[]{:S(2)}) collective-permute-start(f32[128,1,768]{2,1,0:T(1,128)S(1)} %slice.47), channel_id=1, source_target_pairs={{0,128},{128,0},{256,384},{384,256},{1,129},{129,1},{257,385},{385... | collective-permute-start | bytes 1179656 | tf_op jit(solution)/shard_map/ppermute | solution.py:275
  70.2 14.7 %shard_map.68 = f32[3072,128]{1,0:T(8,128)S(1)} custom-call(f32[8]{0:T(128)S(1)} %stack.28.coef_ref, f32[2304,128]{1,0:T(8,128)S(1)} %bitcast.50, f32[768,128]{1,0:T(8,128)S(1)} %bitcast.54), custom_call_target="tpu_custom_call" | custom-call | tf_op jit(solution)/shard_map/pallas_call | solution.py:216
  84.9 1.2 copy-done
  86.1 16.6 %all-to-all-start.1 = ((f32[256,1,1536]{2,1,0:T(1,128)}), f32[256,1,1536]{2,1,0:T(1,128)S(1)}, u32[]{:S(2)}, u32[]{:S(2)}) async-start(f32[256,1,1536]{2,1,0:T(1,128)} %bitcast.52), calls=%async_computation.1 | async-start | bytes 3145728 | tf_op jit(solution)/shard_map/all_to_all | solution.py:61
  102.8 40.5 %all-to-all-done.1 = f32[256,1,1536]{2,1,0:T(1,128)S(1)} async-done(((f32[256,1,1536]{2,1,0:T(1,128)}), f32[256,1,1536]{2,1,0:T(1,128)S(1)}, u32[]{:S(2)}, u32[]{:S(2)}) %all-to-all-start.1) | async-done | bytes 1572896 | tf_op jit(solution)/shard_map/all_to_all | solution.py:61
  143.6 4.3 %collective-permute-start.2 = (f32[256,768]{1,0:T(8,128)S(1)}, f32[256,768]{1,0:T(8,128)S(1)}, u32[]{:S(2)}, u32[]{:S(2)}) collective-permute-start(f32[256,768]{1,0:T(8,128)S(1)} %get-tuple-element.12), channel_id=1, source_target_pairs={{0,128},{128,0},{256,384},{384,256},{1,129},{129,1},{257,385},{385... | collective-permute-start | bytes 2359304 | tf_op jit(solution)/shard_map/ppermute | solution.py:282
  148.7 0.8 fusion.7
  149.6 0.8 fusion.8
  151.3 16.8 %all_to_all.25 = f32[4,128,512]{2,1,0:T(8,128)S(1)} all-to-all(f32[4,128,512]{2,1,0:T(8,128)S(1)} %bitcast.56), channel_id=1, replica_groups={{0,4,8,12},{1,5,9,13},{2,6,10,14},{3,7,11,15},{16,20,24,28},{17,21,25,2..., dimensions={0} | all-to-all | bytes 2097152 | tf_op jit(solution)/shard_map/all_to_all | solution.py:61
  168.4 0.8 copy.15
  169.2 5.8 %all-to-all-start.3 = ((f32[64,1,1024]{2,1,0:T(1,128)}), f32[64,1,1024]{2,1,0:T(1,128)S(1)}, u32[]{:S(2)}, u32[]{:S(2)}) async-start(f32[64,1,1024]{2,1,0:T(1,128)} %bitcast.26), calls=%async_computation.3 | async-start | bytes 524288 | tf_op jit(solution)/shard_map/all_to_all | solution.py:61
  175.0 6.8 %collective-permute-start.3 = (f32[768,128]{1,0:T(8,128)S(1)}, f32[768,128]{1,0:T(8,128)S(1)}, u32[]{:S(2)}, u32[]{:S(2)}) collective-permute-start(f32[768,128]{1,0:T(8,128)S(1)} %convolution_add_fusion), channel_id=1, source_target_pairs={{0,256},{256,0},{128,384},{384,128},{1,257},{257,1},{129,385},{385... | collective-permute-start | bytes 1179656 | tf_op jit(solution)/shard_map/ppermute | solution.py:300
  181.8 22.8 %collective-permute-done.3 = f32[768,128]{1,0:T(8,128)S(1)} collective-permute-done((f32[768,128]{1,0:T(8,128)S(1)}, f32[768,128]{1,0:T(8,128)S(1)}, u32[]{:S(2)}, u32[]{:S(2)}) %collective-permute-start.3) | collective-permute-done | bytes 393248 | tf_op jit(solution)/shard_map/ppermute | solution.py:300
  204.8 1.1 broadcast_in_dim.2
  205.9 8.0 %all-to-all-start.4 = ((f32[128,1,1024]{2,1,0:T(1,128)}), f32[128,1,1024]{2,1,0:T(1,128)S(1)}, u32[]{:S(2)}, u32[]{:S(2)}) async-start(f32[128,1,1024]{2,1,0:T(1,128)} %broadcast_in_dim.2), calls=%async_computation.4 | async-start | bytes 1048576 | tf_op jit(solution)/shard_map/all_to_all | solution.py:309
  215.6 0.9 pad_maximum_fusion.1
  216.5 15.3 %all-to-all-done.4 = f32[128,1,1024]{2,1,0:T(1,128)S(1)} async-done(((f32[128,1,1024]{2,1,0:T(1,128)}), f32[128,1,1024]{2,1,0:T(1,128)S(1)}, u32[]{:S(2)}, u32[]{:S(2)}) %all-to-all-start.4) | async-done | bytes 524320 | tf_op jit(solution)/shard_map/all_to_all | solution.py:309
  232.0 0.8 fusion.2
  (28 shorter events, 5.1 us)
Async XLA Ops:
  1.5 1.1 copy-start.1
  3.9 17.9 %copy-start.2 = (f32[512,128]{1,0:T(8,128)S(1)}, f32[512,128]{1,0:T(8,128)}, u32[]{:S(2)}) copy-start(f32[512,128]{1,0:T(8,128)} %param.7) | copy-start | bytes 786436
  4.0 62.0 %copy-start.3 = (f32[3]{0:T(128)S(1)}, f32[3]{0:T(128)}, u32[]{:S(2)}) copy-start(f32[3]{0:T(128)} %param.6) | copy-start | bytes 40
  4.0 58.7 %all-to-all-start = ((f32[128,1,2304]{2,1,0:T(1,128)}), f32[128,1,2304]{2,1,0:T(1,128)S(1)}, u32[]{:S(2)}, u32[]{:S(2)}) async-start(f32[128,1,2304]{2,1,0:T(1,128)} %bitcast.11), calls=%async_computation | async-start | bytes 2359296 | tf_op jit(solution)/shard_map/all_to_all | solution.py:271
  21.9 40.8 %collective-permute-start = (f32[512,128]{1,0:T(8,128)S(1)}, f32[512,128]{1,0:T(8,128)S(1)}, u32[]{:S(2)}, u32[]{:S(2)}) collective-permute-start(f32[512,128]{1,0:T(8,128)S(1)} %copy-done.2), channel_id=1, source_target_pairs={{0,256},{256,0},{128,384},{384,128},{1,257},{257,1},{129,385},{385... | collective-permute-start | bytes 786440 | tf_op jit(solution)/shard_map/ppermute | solution.py:268
  62.8 7.4 %collective-permute-start.1 = (f32[128,1,768]{2,1,0:T(1,128)S(1)}, f32[128,1,768]{2,1,0:T(1,128)S(1)}, u32[]{:S(2)}, u32[]{:S(2)}) collective-permute-start(f32[128,1,768]{2,1,0:T(1,128)S(1)} %slice.47), channel_id=1, source_target_pairs={{0,128},{128,0},{256,384},{384,256},{1,129},{129,1},{257,385},{385... | collective-permute-start | bytes 1179656 | tf_op jit(solution)/shard_map/ppermute | solution.py:275
  84.9 1.2 copy-start
  86.1 57.1 %all-to-all-start.1 = ((f32[256,1,1536]{2,1,0:T(1,128)}), f32[256,1,1536]{2,1,0:T(1,128)S(1)}, u32[]{:S(2)}, u32[]{:S(2)}) async-start(f32[256,1,1536]{2,1,0:T(1,128)} %bitcast.52), calls=%async_computation.1 | async-start | bytes 3145728 | tf_op jit(solution)/shard_map/all_to_all | solution.py:61
  143.6 6.0 %collective-permute-start.2 = (f32[256,768]{1,0:T(8,128)S(1)}, f32[256,768]{1,0:T(8,128)S(1)}, u32[]{:S(2)}, u32[]{:S(2)}) collective-permute-start(f32[256,768]{1,0:T(8,128)S(1)} %get-tuple-element.12), channel_id=1, source_target_pairs={{0,128},{128,0},{256,384},{384,256},{1,129},{129,1},{257,385},{385... | collective-permute-start | bytes 2359304 | tf_op jit(solution)/shard_map/ppermute | solution.py:282
  169.2 35.4 %all-to-all-start.3 = ((f32[64,1,1024]{2,1,0:T(1,128)}), f32[64,1,1024]{2,1,0:T(1,128)S(1)}, u32[]{:S(2)}, u32[]{:S(2)}) async-start(f32[64,1,1024]{2,1,0:T(1,128)} %bitcast.26), calls=%async_computation.3 | async-start | bytes 524288 | tf_op jit(solution)/shard_map/all_to_all | solution.py:61
  175.0 29.6 %collective-permute-start.3 = (f32[768,128]{1,0:T(8,128)S(1)}, f32[768,128]{1,0:T(8,128)S(1)}, u32[]{:S(2)}, u32[]{:S(2)}) collective-permute-start(f32[768,128]{1,0:T(8,128)S(1)} %convolution_add_fusion), channel_id=1, source_target_pairs={{0,256},{256,0},{128,384},{384,128},{1,257},{257,1},{129,385},{385... | collective-permute-start | bytes 1179656 | tf_op jit(solution)/shard_map/ppermute | solution.py:300
  205.9 26.0 %all-to-all-start.4 = ((f32[128,1,1024]{2,1,0:T(1,128)}), f32[128,1,1024]{2,1,0:T(1,128)S(1)}, u32[]{:S(2)}, u32[]{:S(2)}) async-start(f32[128,1,1024]{2,1,0:T(1,128)} %broadcast_in_dim.2), calls=%async_computation.4 | async-start | bytes 1048576 | tf_op jit(solution)/shard_map/all_to_all | solution.py:309

commit v3 on v2

--- a/solution.py
+++ b/solution.py
@@ -1,6 +1,3 @@
-import itertools
-from functools import partial
-
 import jax
 import jax.numpy as jnp
 from jax import lax
@@ -29,8 +26,8 @@
 HALF_TILES = HALF // LANES
 SENT = TILES + HALF_TILES
 
-ORDER = [(ix * PY + iy) * PZ + iz for iz in range(PZ) for ix in range(PX) for iy in range(PY)]
-STEP_X, STEP_Y, STEP_Z = PY, 1, PX * PY
+ORDER = [(ix * PY + iy) * PZ + iz for iz in range(PZ) for iy in range(PY) for ix in range(PX)]
+STEP_X, STEP_Y, STEP_Z = 1, PX, PX * PY
 
 
 def flat(band, dom):
@@ -115,7 +112,7 @@
 
 def filter_kernel(coef_ref, got_ref, v_other_ref, out_ref, ea, eb, pot, img):
     lane = lax.broadcasted_iota(jnp.int32, (1, LANES), 1)
-    iz, ix, iy = lane // STEP_Z, lane // STEP_X % PX, lane % PY
+    iz, iy, ix = lane // STEP_Z, lane // STEP_Y % PY, lane // STEP_X % PX
 
     def spread(ext):
         own_y, own_z = slice(OY, OY + BY), slice(OZ, OZ + BZ)
@@ -265,19 +262,21 @@
     band = lax.axis_index("band")
     z_hi, core = band // 2, band % 2
     coef = filter_coefficients(bounds, core.astype(jnp.float32))
-    rotation_far = lax.ppermute(rotation, "band", Z_SWAP)
 
     sent = packed(core.reshape(1), orbitals.reshape(CELLS, width), potential[0])
     got = lax.all_to_all(
         sent.reshape(BLOCKS, 1, SENT * LANES), "dom", 0, 0, tiled=True, axis_index_groups=[ORDER]
     )
-    got, rotation_far = lax.optimization_barrier((got, rotation_far))
+    got, rotation_near = lax.optimization_barrier((got, rotation))
+    rotation_far = lax.ppermute(rotation_near, "band", Z_SWAP)
     v_other = lax.ppermute(got[:, :, CELLS:], "band", CORE_SWAP)
     images = filtered_fields(
         coef, got.reshape(BLOCKS * SENT, LANES), v_other.reshape(BLOCKS * HALF_TILES, LANES)
     )
 
+    images, rotation_far = lax.optimization_barrier((images, rotation_far))
     got = exchange(images.reshape(2 * BLOCKS, 1, CELLS), CORE_GROUPS)
+    got, rotation_near, rotation_far = lax.optimization_barrier((got, rotation_near, rotation_far))
     phi, both = split_fields(got.reshape(2 * BLOCKS * TILES, LANES))
     phi_other = lax.ppermute(phi, "band", CORE_SWAP)
     gram = jnp.concatenate(
@@ -298,13 +297,13 @@
     rotated_far = rotate(rotation_far)
     gram, rotated_far = lax.optimization_barrier((gram, rotated_far))
     rotated_far = lax.ppermute(rotated_far, "band", Z_SWAP)
-    rotated_near = rotate(rotation)
+    rotated_near = rotate(rotation_near)
 
     terms = exchange(gram.reshape(4, BLOCKS, 4 * BLOCKS), X_GROUPS)
+    terms, rotated_far = lax.optimization_barrier((terms, rotated_far))
     terms = jnp.sum(terms, axis=0)
     terms = terms.reshape(32, 4, 2, 2, BLOCKS).transpose(0, 3, 1, 2, 4).reshape(64, 8 * BLOCKS)
     terms = exchange(terms.reshape(64, 1, 8 * BLOCKS), PLANE_GROUPS)
-    terms, rotated_far = lax.optimization_barrier((terms, rotated_far))
     terms = jnp.sum(terms, axis=0)
     whole = lax.all_to_all(
         jnp.broadcast_to(terms[None], (BLOCKS, 1, 8 * BLOCKS)), "dom", 0, 0, tiled=True

time: 235 us -> 224 us (0.953)
  blocking collectives: 16.8 us -> 74.2 us
  waiting for transfers between devices: 111 us -> 68.8 us
  starting transfers between devices: 70.6 us -> 43.8 us
    all_to_all x0 -> x1, blocking collectives: none -> 48.9 us  [local(): lax.all_to_all(sent.reshape(BLOCKS, 1, SENT * LANES), 'dom', 0, 0, tiled=...]
    ppermute x1, waiting for transfers between devices: 32.8 us -> 0.01 us  [local(): rotation_far = lax.ppermute(rotation_near, 'band', Z_SWAP)]
    all_to_all x1 -> x0, starting transfers between devices: 17.9 us -> none  [local(): lax.all_to_all(sent.reshape(BLOCKS, 1, SENT * LANES), 'dom', 0, 0, tiled=...]
    all_to_all x2, starting transfers between devices: 22.4 us -> 13.1 us  [exchange(): lax.all_to_all(x, ('band', 'dom'), 0, 0, tiled=True, axis_index_groups=gr...]
    all_to_all x1, blocking collectives: 16.8 us -> 25.3 us  [exchange(): lax.all_to_all(x, ('band', 'dom'), 0, 0, tiled=True, axis_index_groups=gr...]
    ppermute x1, waiting for transfers between devices: 22.8 us -> 15.1 us  [local(): rotated_far = lax.ppermute(rotated_far, 'band', Z_SWAP)]
  transfers between devices with their start and end apart: 8 -> 7, of which waited for: 4 -> 3; matrix products, arithmetic and copies ran while one was open for 2% -> 2% of each run, Pallas kernels for 0% -> 7%
where the time goes in v3:
time: 224 us; the launch traced here: 221 us
  blocking collectives  74.2 us (33%)
  waiting for transfers between devices  68.8 us (31%)
  starting transfers between devices  43.8 us (20%)
  Pallas kernels  15.3 us (7%)
  local copies, waits for them, and re-layouts  6.95 us (3%)
  matrix products  5.64 us (3%)
  between operations  4.43 us (2%)
  other arithmetic  2.33 us (1%)
    all_to_all x1, blocking collectives, local(): lax.all_to_all(sent.reshape(BLOCKS, 1, SENT * LANES), 'dom', 0, 0, tiled=...  48.9 us
    all_to_all x2, waiting for transfers between devices, exchange(): lax.all_to_all(x, ('band', 'dom'), 0, 0, tiled=True, axis_index_groups=gr...  38.8 us
    all_to_all x1, blocking collectives, exchange(): lax.all_to_all(x, ('band', 'dom'), 0, 0, tiled=True, axis_index_groups=gr...  25.3 us
    ppermute x1, waiting for transfers between devices, local(): rotated_far = lax.ppermute(rotated_far, 'band', Z_SWAP)  15.1 us
    all_to_all x1, waiting for transfers between devices, local(): lax.all_to_all(jnp.broadcast_to(terms[None], (BLOCKS, 1, 8 * BLOCKS)), 'd...  14.9 us
    pallas_call x1, Pallas kernels, filtered_fields(): pl.pallas_call(filter_kernel, out_shape=jax.ShapeDtypeStruct((BLOCKS * 2...  14.7 us
    all_to_all x2, starting transfers between devices, exchange(): lax.all_to_all(x, ('band', 'dom'), 0, 0, tiled=True, axis_index_groups=gr...  13.1 us
    all_to_all x1, starting transfers between devices, local(): lax.all_to_all(jnp.broadcast_to(terms[None], (BLOCKS, 1, 8 * BLOCKS)), 'd...  8.17 us
  transfers between devices with their start and end apart: 7, of which 3 were waited for; matrix products, arithmetic and copies ran while one was open for 2% of the time, Pallas kernels for 7%

profile of v3, /device:TPU:1, one launch (start us, length us, event | category | flops | bytes accessed | tf_op | source)
XLA Modules:
  0.0 221.5 jit_solution(11968347726366255370)
XLA Ops:
  0.6 0.8 copy.19
  1.5 1.1 copy-done.1
  2.9 48.9 %all_to_all.25 = f32[128,1,2304]{2,1,0:T(1,128)S(1)} all-to-all(f32[128,1,2304]{2,1,0:T(1,128)S(1)} %bitcast.53), channel_id=1, replica_groups={{0,32,64,96,8,40,72,104,16,48,80,112,24,56,88,120,1,33,65,97,9,41,73,10..., dimensions={0} | all-to-all | bytes 2359296 | tf_op jit(solution)/shard_map/all_to_all | solution.py:267
  51.9 4.8 %collective-permute-start = (f32[128,1,768]{2,1,0:T(1,128)S(1)}, f32[128,1,768]{2,1,0:T(1,128)S(1)}, u32[]{:S(2)}, u32[]{:S(2)}) collective-permute-start(f32[128,1,768]{2,1,0:T(1,128)S(1)} %slice.47), channel_id=1, source_target_pairs={{0,128},{128,0},{256,384},{384,256},{1,129},{129,1},{257,385},{385... | collective-permute-start | bytes 1179656 | tf_op jit(solution)/shard_map/ppermute | solution.py:272
  56.7 7.9 %collective-permute-start.1 = (f32[512,128]{1,0:T(8,128)S(1)}, f32[512,128]{1,0:T(8,128)S(1)}, u32[]{:S(2)}, u32[]{:S(2)}) collective-permute-start(f32[512,128]{1,0:T(8,128)S(1)} %copy-done.2), channel_id=1, source_target_pairs={{0,256},{256,0},{128,384},{384,128},{1,257},{257,1},{129,385},{385... | collective-permute-start | bytes 786440 | tf_op jit(solution)/shard_map/ppermute | solution.py:271
  68.8 14.7 %shard_map.68 = f32[3072,128]{1,0:T(8,128)S(1)} custom-call(f32[8]{0:T(128)S(1)} %stack.28.coef_ref, f32[2304,128]{1,0:T(8,128)S(1)} %bitcast.50, f32[768,128]{1,0:T(8,128)S(1)} %bitcast.55), custom_call_target="tpu_custom_call" | custom-call | tf_op jit(solution)/shard_map/pallas_call | solution.py:213
  83.6 1.2 copy-done
  85.5 9.3 %all-to-all-start.1 = ((f32[256,1,1536]{2,1,0:T(1,128)}), f32[256,1,1536]{2,1,0:T(1,128)S(1)}, u32[]{:S(2)}, u32[]{:S(2)}) async-start(f32[256,1,1536]{2,1,0:T(1,128)} %bitcast.52), calls=%async_computation.1 | async-start | bytes 3145728 | tf_op jit(solution)/shard_map/all_to_all | solution.py:58
  94.8 38.8 %all-to-all-done.1 = f32[256,1,1536]{2,1,0:T(1,128)S(1)} async-done(((f32[256,1,1536]{2,1,0:T(1,128)}), f32[256,1,1536]{2,1,0:T(1,128)S(1)}, u32[]{:S(2)}, u32[]{:S(2)}) %all-to-all-start.1) | async-done | bytes 1572896 | tf_op jit(solution)/shard_map/all_to_all | solution.py:58
  133.9 4.9 %collective-permute-start.2 = (f32[256,768]{1,0:T(8,128)S(1)}, f32[256,768]{1,0:T(8,128)S(1)}, u32[]{:S(2)}, u32[]{:S(2)}) collective-permute-start(f32[256,768]{1,0:T(8,128)S(1)} %get-tuple-element.21), channel_id=1, source_target_pairs={{0,128},{128,0},{256,384},{384,256},{1,129},{129,1},{257,385},{385... | collective-permute-start | bytes 2359304 | tf_op jit(solution)/shard_map/ppermute | solution.py:281
  139.6 0.8 fusion.7
  140.5 0.8 fusion.8
  141.3 1.1 pad_maximum_fusion
  142.4 1.6 convolution_add_fusion
  143.9 3.8 %all-to-all-start.2 = ((f32[4,128,512]{2,1,0:T(8,128)}), f32[4,128,512]{2,1,0:T(8,128)S(1)}, u32[]{:S(2)}, u32[]{:S(2)}) async-start(f32[4,128,512]{2,1,0:T(8,128)} %bitcast.24), calls=%async_computation.2 | async-start | bytes 2097152 | tf_op jit(solution)/shard_map/all_to_all | solution.py:58
  147.7 5.0 %collective-permute-start.3 = (f32[768,128]{1,0:T(8,128)}, f32[768,128]{1,0:T(8,128)S(1)}, u32[]{:S(2)}, u32[]{:S(2)}) collective-permute-start(f32[768,128]{1,0:T(8,128)} %convolution_add_fusion), channel_id=1, source_target_pairs={{0,256},{256,0},{128,384},{384,128},{1,257},{257,1},{129,385},{385... | collective-permute-start | bytes 1179656 | tf_op jit(solution)/shard_map/ppermute | solution.py:299
  152.7 15.1 %collective-permute-done.3 = f32[768,128]{1,0:T(8,128)S(1)} collective-permute-done((f32[768,128]{1,0:T(8,128)}, f32[768,128]{1,0:T(8,128)S(1)}, u32[]{:S(2)}, u32[]{:S(2)}) %collective-permute-start.3) | collective-permute-done | bytes 393248 | tf_op jit(solution)/shard_map/ppermute | solution.py:299
  168.3 25.3 %all_to_all.26 = f32[64,1,1024]{2,1,0:T(1,128)S(1)} all-to-all(f32[64,1,1024]{2,1,0:T(1,128)S(1)} %bitcast.60), channel_id=1, replica_groups={{0,256,1,257,2,258,3,259,16,272,17,273,18,274,19,275,32,288,33,289,34,2..., dimensions={0} | all-to-all | bytes 524288 | tf_op jit(solution)/shard_map/all_to_all | solution.py:58
  193.7 1.1 broadcast_in_dim.2
  194.8 8.2 %all-to-all-start.4 = ((f32[128,1,1024]{2,1,0:T(1,128)}), f32[128,1,1024]{2,1,0:T(1,128)S(1)}, u32[]{:S(2)}, u32[]{:S(2)}) async-start(f32[128,1,1024]{2,1,0:T(1,128)} %broadcast_in_dim.2), calls=%async_computation.4 | async-start | bytes 1048576 | tf_op jit(solution)/shard_map/all_to_all | solution.py:308
  203.8 0.8 broadcast_select_fusion.1
  204.7 0.9 pad_maximum_fusion.1
  205.6 14.9 %all-to-all-done.4 = f32[128,1,1024]{2,1,0:T(1,128)S(1)} async-done(((f32[128,1,1024]{2,1,0:T(1,128)}), f32[128,1,1024]{2,1,0:T(1,128)S(1)}, u32[]{:S(2)}, u32[]{:S(2)}) %all-to-all-start.4) | async-done | bytes 524320 | tf_op jit(solution)/shard_map/all_to_all | solution.py:308
  220.6 0.8 fusion.2
  (30 shorter events, 4.5 us)
Async XLA Ops:
  1.5 1.1 copy-start.1
  2.9 53.8 %copy-start.2 = (f32[512,128]{1,0:T(8,128)S(1)}, f32[512,128]{1,0:T(8,128)}, u32[]{:S(2)}) copy-start(f32[512,128]{1,0:T(8,128)} %param.7) | copy-start | bytes 786436
  2.9 61.7 %copy-start.5 = (f32[3]{0:T(128)S(1)}, f32[3]{0:T(128)}, u32[]{:S(2)}) copy-start(f32[3]{0:T(128)} %param.6) | copy-start | bytes 40
  51.9 16.9 %collective-permute-start = (f32[128,1,768]{2,1,0:T(1,128)S(1)}, f32[128,1,768]{2,1,0:T(1,128)S(1)}, u32[]{:S(2)}, u32[]{:S(2)}) collective-permute-start(f32[128,1,768]{2,1,0:T(1,128)S(1)} %slice.47), channel_id=1, source_target_pairs={{0,128},{128,0},{256,384},{384,256},{1,129},{129,1},{257,385},{385... | collective-permute-start | bytes 1179656 | tf_op jit(solution)/shard_map/ppermute | solution.py:272
  56.7 28.1 %collective-permute-start.1 = (f32[512,128]{1,0:T(8,128)S(1)}, f32[512,128]{1,0:T(8,128)S(1)}, u32[]{:S(2)}, u32[]{:S(2)}) collective-permute-start(f32[512,128]{1,0:T(8,128)S(1)} %copy-done.2), channel_id=1, source_target_pairs={{0,256},{256,0},{128,384},{384,128},{1,257},{257,1},{129,385},{385... | collective-permute-start | bytes 786440 | tf_op jit(solution)/shard_map/ppermute | solution.py:271
  83.6 1.2 copy-start
  84.7 0.7 copy-start.3
  85.5 48.1 %all-to-all-start.1 = ((f32[256,1,1536]{2,1,0:T(1,128)}), f32[256,1,1536]{2,1,0:T(1,128)S(1)}, u32[]{:S(2)}, u32[]{:S(2)}) async-start(f32[256,1,1536]{2,1,0:T(1,128)} %bitcast.52), calls=%async_computation.1 | async-start | bytes 3145728 | tf_op jit(solution)/shard_map/all_to_all | solution.py:58
  133.6 5.2 %copy-start.4 = (f32[512,128]{1,0:T(8,128)S(1)}, f32[512,128]{1,0:T(8,128)}, u32[]{:S(2)}) copy-start(f32[512,128]{1,0:T(8,128)} %copy-done.3) | copy-start | bytes 786436
  133.9 6.6 %collective-permute-start.2 = (f32[256,768]{1,0:T(8,128)S(1)}, f32[256,768]{1,0:T(8,128)S(1)}, u32[]{:S(2)}, u32[]{:S(2)}) collective-permute-start(f32[256,768]{1,0:T(8,128)S(1)} %get-tuple-element.21), channel_id=1, source_target_pairs={{0,128},{128,0},{256,384},{384,256},{1,129},{129,1},{257,385},{385... | collective-permute-start | bytes 2359304 | tf_op jit(solution)/shard_map/ppermute | solution.py:281
  143.9 23.9 %all-to-all-start.2 = ((f32[4,128,512]{2,1,0:T(8,128)}), f32[4,128,512]{2,1,0:T(8,128)S(1)}, u32[]{:S(2)}, u32[]{:S(2)}) async-start(f32[4,128,512]{2,1,0:T(8,128)} %bitcast.24), calls=%async_computation.2 | async-start | bytes 2097152 | tf_op jit(solution)/shard_map/all_to_all | solution.py:58
  147.7 20.2 %collective-permute-start.3 = (f32[768,128]{1,0:T(8,128)}, f32[768,128]{1,0:T(8,128)S(1)}, u32[]{:S(2)}, u32[]{:S(2)}) collective-permute-start(f32[768,128]{1,0:T(8,128)} %convolution_add_fusion), channel_id=1, source_target_pairs={{0,256},{256,0},{128,384},{384,128},{1,257},{257,1},{129,385},{385... | collective-permute-start | bytes 1179656 | tf_op jit(solution)/shard_map/ppermute | solution.py:299
  194.8 25.6 %all-to-all-start.4 = ((f32[128,1,1024]{2,1,0:T(1,128)}), f32[128,1,1024]{2,1,0:T(1,128)S(1)}, u32[]{:S(2)}, u32[]{:S(2)}) async-start(f32[128,1,1024]{2,1,0:T(1,128)} %broadcast_in_dim.2), calls=%async_computation.4 | async-start | bytes 1048576 | tf_op jit(solution)/shard_map/all_to_all | solution.py:308

commit v4 on v3

--- a/solution.py
+++ b/solution.py
@@ -110,94 +110,120 @@
     )(got)
 
 
-def filter_kernel(coef_ref, got_ref, v_other_ref, out_ref, ea, eb, pot, img):
+def margins(ext):
     lane = lax.broadcasted_iota(jnp.int32, (1, LANES), 1)
     iz, iy, ix = lane // STEP_Z, lane // STEP_Y % PY, lane // STEP_X % PX
-
-    def spread(ext):
-        own_y, own_z = slice(OY, OY + BY), slice(OZ, OZ + BZ)
-
-        def below(v, step, keep):
-            return jnp.where(keep, pltpu.roll(v, step, v.ndim - 1), 0.0)
-
-        def above(v, step, keep):
-            return jnp.where(keep, pltpu.roll(v, LANES - step, v.ndim - 1), 0.0)
-
-        def inner(i, carry):
-            at = i + OX
-            ext[at, own_y, 0:8] = below(ext[at, own_y, OZ + 8 : OZ + 16], STEP_Z, iz > 0)
-            ext[at, own_y, OZ + BZ : OZ + BZ + 8] = above(ext[at, own_y, OZ : OZ + 8], STEP_Z, iz < PZ - 1)
-            ext[at, 0:OY, own_z] = below(ext[at, BY : BY + OY, own_z], STEP_Y, iy > 0)
-            ext[at, OY + BY :, own_z] = above(ext[at, OY : 2 * OY, own_z], STEP_Y, iy < PY - 1)
-            return carry
-
-        def outer(i, carry):
-            ext[i, own_y, own_z] = below(ext[i + BX, own_y, own_z], STEP_X, ix > 0)
-            ext[i + OX + BX, own_y, own_z] = above(ext[i + OX, own_y, own_z], STEP_X, ix < PX - 1)
-            return carry
-
-        lax.fori_loop(0, BX, inner, 0)
-        lax.fori_loop(0, REACH, outer, 0)
-
-    def part(ext, i, y0, ys):
-        return ext[i + OX, OY + y0 : OY + y0 + ys, OZ : OZ + BZ]
-
-    def image(ext, i, y0, ys, scale, shift):
-        at, y, z = i + OX, OY + y0, OZ
-        centre = ext[at, y : y + ys, z : z + BZ]
-        total = (3.0 * STENCIL[0]) * centre
-        for k in range(1, REACH + 1):
-            pair_x = ext[at - k, y : y + ys, z : z + BZ] + ext[at + k, y : y + ys, z : z + BZ]
-            pair_y = ext[at, y - k : y - k + ys, z : z + BZ] + ext[at, y + k : y + k + ys, z : z + BZ]
-            pair_z = ext[at, y : y + ys, z - k : z - k + BZ] + ext[at, y : y + ys, z + k : z + k + BZ]
-            total = total + STENCIL[k] * ((pair_x + pair_y) + pair_z)
-        local = pot[i, y0 : y0 + ys] - shift
-        return (scale * KINETIC) * total + scale * (local * centre)
-
-    second = coef_ref[7]
+    own_y, own_z = slice(OY, OY + BY), slice(OZ, OZ + BZ)
+
+    def below(v, step, keep):
+        return jnp.where(keep, pltpu.roll(v, step, v.ndim - 1), 0.0)
+
+    def above(v, step, keep):
+        return jnp.where(keep, pltpu.roll(v, LANES - step, v.ndim - 1), 0.0)
+
+    def inner(i, carry):
+        at = i + OX
+        ext[at, own_y, 0:8] = below(ext[at, own_y, OZ + 8 : OZ + 16], STEP_Z, iz > 0)
+        ext[at, own_y, OZ + BZ : OZ + BZ + 8] = above(ext[at, own_y, OZ : OZ + 8], STEP_Z, iz < PZ - 1)
+        ext[at, 0:OY, own_z] = below(ext[at, BY : BY + OY, own_z], STEP_Y, iy > 0)
+        ext[at, OY + BY :, own_z] = above(ext[at, OY : 2 * OY, own_z], STEP_Y, iy < PY - 1)
+        return carry
+
+    def outer(i, carry):
+        ext[i, own_y, own_z] = below(ext[i + BX, own_y, own_z], STEP_X, ix > 0)
+        ext[i + OX + BX, own_y, own_z] = above(ext[i + OX, own_y, own_z], STEP_X, ix < PX - 1)
+        return carry
+
+    lax.fori_loop(0, BX, inner, 0)
+    lax.fori_loop(0, REACH, outer, 0)
+
+
+YS = BY // 2
+
+
+def own(ext, i, y0):
+    return ext[i + OX, OY + y0 : OY + y0 + YS, OZ : OZ + BZ]
+
+
+def set_own(ext, i, y0, value):
+    ext[i + OX, OY + y0 : OY + y0 + YS, OZ : OZ + BZ] = value
+
+
+def laplace(ext, i, y0):
+    at, y, z = i + OX, OY + y0, OZ
+    total = (3.0 * STENCIL[0]) * ext[at, y : y + YS, z : z + BZ]
+    for k in range(1, REACH + 1):
+        pair_x = ext[at - k, y : y + YS, z : z + BZ] + ext[at + k, y : y + YS, z : z + BZ]
+        pair_y = ext[at, y - k : y - k + YS, z : z + BZ] + ext[at, y + k : y + k + YS, z : z + BZ]
+        pair_z = ext[at, y : y + YS, z - k : z - k + BZ] + ext[at, y : y + YS, z + k : z + k + BZ]
+        total = total + STENCIL[k] * ((pair_x + pair_y) + pair_z)
+    return total
+
+
+def laplace_kernel(got_ref, x_ref, lap_ref, pot_ref, ext):
     for q in range(TILES):
         tile = jnp.transpose(got_ref[pl.ds(q, BLOCKS, stride=SENT), :]).reshape(LANES // BZ, BZ, LANES)
         for r in range(LANES // BZ):
             row = q * (LANES // BZ) + r
-            ea[OX + row // BY, OY + row % BY, OZ : OZ + BZ] = tile[r]
-    for y in range(BY):
-        s = y % HALF_TILES
-        own = got_ref[pl.ds(TILES + s, BLOCKS, stride=SENT), :]
-        other = v_other_ref[pl.ds(s, BLOCKS, stride=HALF_TILES), :]
-        swap = second > 0.5 if y < HALF_TILES else second < 0.5
-        pot[:, y] = jnp.transpose(jnp.where(swap, other, own)).reshape(BX, BZ, LANES)
-
-    ys = BY // 2
+            ext[OX + row // BY, OY + row % BY, OZ : OZ + BZ] = tile[r]
+            x_ref[row // BY, row % BY] = tile[r]
+    for s in range(HALF_TILES):
+        tile = jnp.transpose(got_ref[pl.ds(TILES + s, BLOCKS, stride=SENT), :])
+        pot_ref[:, s] = tile.reshape(BX, BZ, LANES)
+    margins(ext)
+
+    def body(i, carry):
+        for y0 in range(0, BY, YS):
+            lap_ref[i, y0 : y0 + YS] = laplace(ext, i, y0)
+        return carry
+
+    lax.fori_loop(0, BX, body, 0)
+
+
+def filter_kernel(coef_ref, x_ref, lap_ref, pot_own_ref, v_other_ref, out_ref, ea, eb, pot, img):
+    second = coef_ref[7] > 0.5
+    for s in range(HALF_TILES):
+        other = jnp.transpose(v_other_ref[pl.ds(s, BLOCKS, stride=HALF_TILES), :]).reshape(BX, BZ, LANES)
+        mine = pot_own_ref[:, s]
+        pot[:, s] = jnp.where(second, other, mine)
+        pot[:, s + HALF_TILES] = jnp.where(second, mine, other)
+
+    def image(total, centre, i, y0, scale, shift):
+        local = pot[i, y0 : y0 + YS] - shift
+        return (scale * KINETIC) * total + scale * (local * centre)
 
     def first(i, carry):
-        for y0 in range(0, BY, ys):
-            eb[i + OX, OY + y0 : OY + y0 + ys, OZ : OZ + BZ] = image(ea, i, y0, ys, coef_ref[0], coef_ref[1])
-        return carry
-
-    def later(src, dst, scale, back):
-        def body(i, squares):
-            for y0 in range(0, BY, ys):
-                new = image(src, i, y0, ys, scale, coef_ref[1]) - back * part(dst, i, y0, ys)
-                dst[i + OX, OY + y0 : OY + y0 + ys, OZ : OZ + BZ] = new
-                squares = squares + jnp.sum(new * new, axis=0)
-            return squares
-
-        return body
-
-    def last(i, carry):
-        for y0 in range(0, BY, ys):
-            img[i, y0 : y0 + ys] = image(eb, i, y0, ys, 1.0, 0.0)
-        return carry
-
-    zero = jnp.zeros((BZ, LANES), jnp.float32)
-    spread(ea)
+        for y0 in range(0, BY, YS):
+            total, centre = lap_ref[i, y0 : y0 + YS], x_ref[i, y0 : y0 + YS]
+            set_own(eb, i, y0, image(total, centre, i, y0, coef_ref[0], coef_ref[1]))
+        return carry
+
+    def next_field(i, carry):
+        for y0 in range(0, BY, YS):
+            new = image(laplace(eb, i, y0), own(eb, i, y0), i, y0, coef_ref[2], coef_ref[1])
+            set_own(ea, i, y0, new - coef_ref[3] * x_ref[i, y0 : y0 + YS])
+        return carry
+
+    def last_field(i, squares):
+        for y0 in range(0, BY, YS):
+            new = image(laplace(ea, i, y0), own(ea, i, y0), i, y0, coef_ref[4], coef_ref[1])
+            new = new - coef_ref[5] * own(eb, i, y0)
+            set_own(eb, i, y0, new)
+            squares = squares + jnp.sum(new * new, axis=0)
+        return squares
+
+    def image_field(i, carry):
+        for y0 in range(0, BY, YS):
+            img[i, y0 : y0 + YS] = image(laplace(eb, i, y0), own(eb, i, y0), i, y0, 1.0, 0.0)
+        return carry
+
     lax.fori_loop(0, BX, first, 0)
-    spread(eb)
-    lax.fori_loop(0, BX, later(eb, ea, coef_ref[2], coef_ref[3]), zero)
-    spread(ea)
-    squares = lax.fori_loop(0, BX, later(ea, eb, coef_ref[4], coef_ref[5]), zero)
-    spread(eb)
-    lax.fori_loop(0, BX, last, 0)
+    margins(eb)
+    lax.fori_loop(0, BX, next_field, 0)
+    margins(ea)
+    squares = lax.fori_loop(0, BX, last_field, jnp.zeros((BZ, LANES), jnp.float32))
+    margins(eb)
+    lax.fori_loop(0, BX, image_field, 0)
     norm = jnp.sqrt(jnp.sum(squares, keepdims=True))
     for q in range(TILES):
         rows = [q * (LANES // BZ) + r for r in range(LANES // BZ)]
@@ -208,21 +234,42 @@
         out_ref[pl.ds(at + HALF_TILES, BLOCKS, stride=2 * TILES), :] = jnp.transpose(field / norm)
 
 
-def filtered_fields(coef, got, v_other):
+FIELD = (BX, BY, BZ, LANES)
+
+
+def first_laplace(got):
+    vmem = pl.BlockSpec(memory_space=pltpu.VMEM)
+    return pl.pallas_call(
+        laplace_kernel,
+        out_shape=(
+            jax.ShapeDtypeStruct(FIELD, jnp.float32),
+            jax.ShapeDtypeStruct(FIELD, jnp.float32),
+            jax.ShapeDtypeStruct((BX, HALF_TILES, BZ, LANES), jnp.float32),
+        ),
+        in_specs=[vmem],
+        out_specs=(vmem, vmem, vmem),
+        scratch_shapes=[pltpu.VMEM(EXT, jnp.float32)],
+        compiler_params=pltpu.CompilerParams(vmem_limit_bytes=24 * 1024 * 1024),
+        cost_estimate=pl.CostEstimate(flops=20_000_000, bytes_accessed=20_000_000, transcendentals=0),
+    )(got)
+
+
+def filtered_fields(coef, x, lap, pot_own, v_other):
     vmem = pl.BlockSpec(memory_space=pltpu.VMEM)
     return pl.pallas_call(
         filter_kernel,
         out_shape=jax.ShapeDtypeStruct((BLOCKS * 2 * TILES, LANES), jnp.float32),
-        in_specs=[pl.BlockSpec(memory_space=pltpu.SMEM), vmem, vmem],
+        in_specs=[pl.BlockSpec(memory_space=pltpu.SMEM), vmem, vmem, vmem, vmem],
         out_specs=vmem,
         scratch_shapes=[
             pltpu.VMEM(EXT, jnp.float32),
             pltpu.VMEM(EXT, jnp.float32),
-            pltpu.VMEM((BX, BY, BZ, LANES), jnp.float32),
-            pltpu.VMEM((BX, BY, BZ, LANES), jnp.float32),
+            pltpu.VMEM(FIELD, jnp.float32),
+            pltpu.VMEM(FIELD, jnp.float32),
         ],
-        compiler_params=pltpu.CompilerParams(vmem_limit_bytes=40 * 1024 * 1024),
-    )(coef, got, v_other)
+        compiler_params=pltpu.CompilerParams(vmem_limit_bytes=36 * 1024 * 1024),
+        cost_estimate=pl.CostEstimate(flops=60_000_000, bytes_accessed=40_000_000, transcendentals=0),
+    )(coef, x, lap, pot_own, v_other)
 
 
 def filter_coefficients(bounds, second):
@@ -270,9 +317,8 @@
     got, rotation_near = lax.optimization_barrier((got, rotation))
     rotation_far = lax.ppermute(rotation_near, "band", Z_SWAP)
     v_other = lax.ppermute(got[:, :, CELLS:], "band", CORE_SWAP)
-    images = filtered_fields(
-        coef, got.reshape(BLOCKS * SENT, LANES), v_other.reshape(BLOCKS * HALF_TILES, LANES)
-    )
+    x, lap, pot_own = first_laplace(got.reshape(BLOCKS * SENT, LANES))
+    images = filtered_fields(coef, x, lap, pot_own, v_other.reshape(BLOCKS * HALF_TILES, LANES))
 
     images, rotation_far = lax.optimization_barrier((images, rotation_far))
     got = exchange(images.reshape(2 * BLOCKS, 1, CELLS), CORE_GROUPS)
@@ -288,23 +334,30 @@
         swapped = jnp.where(core == 0, weights, weights[:, ::-1])
         return swapped.transpose(1, 0, 2, 3).reshape(4 * BLOCKS, width)
 
-    def rotate(weights):
-        weights = by_core(weights)
-        return contract(phi, weights[: 2 * BLOCKS], ((0,), (0,))) + contract(
-            phi_other, weights[2 * BLOCKS :], ((0,), (0,))
+    def rotate(weights, start, end):
+        cells = slice(start, end)
+        return contract(phi[:, cells], weights[: 2 * BLOCKS], ((0,), (0,))) + contract(
+            phi_other[:, cells], weights[2 * BLOCKS :], ((0,), (0,))
         )
 
-    rotated_far = rotate(rotation_far)
-    gram, rotated_far = lax.optimization_barrier((gram, rotated_far))
-    rotated_far = lax.ppermute(rotated_far, "band", Z_SWAP)
-    rotated_near = rotate(rotation_near)
-
+    far = by_core(rotation_far)
+    cuts = (0, HALF // 2, 5 * HALF // 6, HALF)
+    parts = []
+
+    def send_part(k, tie):
+        tie, part = lax.optimization_barrier((tie, rotate(far, cuts[k], cuts[k + 1])))
+        parts.append(lax.ppermute(part, "band", Z_SWAP))
+        return tie
+
+    gram = send_part(0, gram)
     terms = exchange(gram.reshape(4, BLOCKS, 4 * BLOCKS), X_GROUPS)
-    terms, rotated_far = lax.optimization_barrier((terms, rotated_far))
+    terms, parts[0] = lax.optimization_barrier((terms, parts[0]))
     terms = jnp.sum(terms, axis=0)
     terms = terms.reshape(32, 4, 2, 2, BLOCKS).transpose(0, 3, 1, 2, 4).reshape(64, 8 * BLOCKS)
+    terms = send_part(1, terms)
     terms = exchange(terms.reshape(64, 1, 8 * BLOCKS), PLANE_GROUPS)
-    terms = jnp.sum(terms, axis=0)
+    terms, parts[1] = lax.optimization_barrier((terms, parts[1]))
+    terms = send_part(2, jnp.sum(terms, axis=0))
     whole = lax.all_to_all(
         jnp.broadcast_to(terms[None], (BLOCKS, 1, 8 * BLOCKS)), "dom", 0, 0, tiled=True
     )
@@ -312,6 +365,8 @@
     whole = whole.reshape(2, 2, 2, BLOCKS, BLOCKS)
     whole = jnp.where(core == 0, whole, whole[:, :, ::-1])
     whole = whole.reshape(2, 4 * BLOCKS, BLOCKS)
+    rotated_near = rotate(by_core(rotation_near), 0, HALF)
+    rotated_far = jnp.concatenate(parts, axis=0)
     lower = jnp.where(z_hi == 0, rotated_near, rotated_far)
     upper = jnp.where(z_hi == 0, rotated_far, rotated_near)
     rotated = jnp.concatenate([lower, upper], axis=0).reshape(1, BX, BY, BZ, width)

time: 224 us -> 223 us (level)
  blocking collectives: 74.2 us -> 48.9 us
  starting transfers between devices: 43.8 us -> 66.8 us
    all_to_all x1 -> x0, blocking collectives: 25.3 us -> none  [exchange(): lax.all_to_all(x, ('band', 'dom'), 0, 0, tiled=True, axis_index_groups=gr...]
    all_to_all x1, waiting for transfers between devices: 14.9 us -> 1.47 us  [local(): lax.all_to_all(jnp.broadcast_to(terms[None], (BLOCKS, 1, 8 * BLOCKS)), 'd...]
    ppermute x1 -> x3, waiting for transfers between devices: 15.1 us -> 26.6 us  [send_part(): parts.append(lax.ppermute(part, 'band', Z_SWAP))]
    ppermute x1 -> x3, starting transfers between devices: 5.04 us -> 15.6 us  [send_part(): parts.append(lax.ppermute(part, 'band', Z_SWAP))]
    all_to_all x2 -> x3, starting transfers between devices: 13.1 us -> 22.2 us  [exchange(): lax.all_to_all(x, ('band', 'dom'), 0, 0, tiled=True, axis_index_groups=gr...]
    pallas_call x0 -> x1, Pallas kernels: none -> 3.39 us  [first_laplace(): pl.pallas_call(laplace_kernel, out_shape=(jax.ShapeDtypeStruct(FIELD, jnp...]
    all_to_all x1, starting transfers between devices: 8.17 us -> 11.5 us  [local(): lax.all_to_all(jnp.broadcast_to(terms[None], (BLOCKS, 1, 8 * BLOCKS)), 'd...]
    pallas_call x1, Pallas kernels: 14.7 us -> 11.4 us  [filtered_fields(): pl.pallas_call(filter_kernel, out_shape=jax.ShapeDtypeStruct((BLOCKS * 2...]
  transfers between devices with their start and end apart: 7 -> 10, of which waited for: 3 -> 7; matrix products, arithmetic and copies ran while one was open for 2% -> 3% of each run, Pallas kernels for 7% -> 7%
where the time goes in v4:
time: 223 us; the launch traced here: 221 us
  waiting for transfers between devices  69 us (31%)
  starting transfers between devices  66.8 us (30%)
  blocking collectives  48.9 us (22%)
  Pallas kernels  15.4 us (7%)
  local copies, waits for them, and re-layouts  8.4 us (4%)
  matrix products  6.28 us (3%)
  between operations  4.31 us (2%)
  other arithmetic  2.34 us (1%)
    all_to_all x1, blocking collectives, local(): lax.all_to_all(sent.reshape(BLOCKS, 1, SENT * LANES), 'dom', 0, 0, tiled=...  48.9 us
    all_to_all x3, waiting for transfers between devices, exchange(): lax.all_to_all(x, ('band', 'dom'), 0, 0, tiled=True, axis_index_groups=gr...  40.6 us
    ppermute x3, waiting for transfers between devices, send_part(): parts.append(lax.ppermute(part, 'band', Z_SWAP))  26.6 us
    all_to_all x3, starting transfers between devices, exchange(): lax.all_to_all(x, ('band', 'dom'), 0, 0, tiled=True, axis_index_groups=gr...  22.2 us
    ppermute x3, starting transfers between devices, send_part(): parts.append(lax.ppermute(part, 'band', Z_SWAP))  15.6 us
    all_to_all x1, starting transfers between devices, local(): lax.all_to_all(jnp.broadcast_to(terms[None], (BLOCKS, 1, 8 * BLOCKS)), 'd...  11.5 us
    pallas_call x1, Pallas kernels, filtered_fields(): pl.pallas_call(filter_kernel, out_shape=jax.ShapeDtypeStruct((BLOCKS * 2...  11.4 us
    ppermute x1, starting transfers between devices, local(): rotation_far = lax.ppermute(rotation_near, 'band', Z_SWAP)  7.94 us
  transfers between devices with their start and end apart: 10, of which 7 were waited for; matrix products, arithmetic and copies ran while one was open for 3% of the time, Pallas kernels for 7%

profile of v4, /device:TPU:1, one launch (start us, length us, event | category | flops | bytes accessed | tf_op | source)
XLA Modules:
  0.0 221.4 jit_solution(13835831707976405248)
XLA Ops:
  1.5 1.1 copy-done.1
  2.9 48.9 %all_to_all.25 = f32[128,1,2304]{2,1,0:T(1,128)S(1)} all-to-all(f32[128,1,2304]{2,1,0:T(1,128)S(1)} %bitcast.57), channel_id=1, replica_groups={{0,32,64,96,8,40,72,104,16,48,80,112,24,56,88,120,1,33,65,97,9,41,73,10..., dimensions={0} | all-to-all | bytes 2359296 | tf_op jit(solution)/shard_map/all_to_all | solution.py:314
  51.9 4.8 %collective-permute-start = (f32[128,1,768]{2,1,0:T(1,128)S(1)}, f32[128,1,768]{2,1,0:T(1,128)S(1)}, u32[]{:S(2)}, u32[]{:S(2)}) collective-permute-start(f32[128,1,768]{2,1,0:T(1,128)S(1)} %slice.69), channel_id=1, source_target_pairs={{0,128},{128,0},{256,384},{384,256},{1,129},{129,1},{257,385},{385... | collective-permute-start | bytes 1179656 | tf_op jit(solution)/shard_map/ppermute | solution.py:319
  56.7 7.9 %collective-permute-start.1 = (f32[512,128]{1,0:T(8,128)S(1)}, f32[512,128]{1,0:T(8,128)S(1)}, u32[]{:S(2)}, u32[]{:S(2)}) collective-permute-start(f32[512,128]{1,0:T(8,128)S(1)} %copy-done.2), channel_id=1, source_target_pairs={{0,256},{256,0},{128,384},{384,128},{1,257},{257,1},{129,385},{385... | collective-permute-start | bytes 786440 | tf_op jit(solution)/shard_map/ppermute | solution.py:318
  68.7 3.4 %shard_map.68 = (f32[8,12,16,128]{3,2,1,0:T(8,128)S(1)}, f32[8,12,16,128]{3,2,1,0:T(8,128)S(1)}, f32[8,6,16,128]{3,2,1,0:T(8,128)S(1)}) custom-call(f32[2304,128]{1,0:T(8,128)S(1)} %bitcast.54), custom_call_target="tpu_custom_call" | custom-call | flops 20000000 | bytes 20000000 | tf_op jit(solution)/shard_map/pallas_call | solution.py:242
  72.1 11.4 %shard_map.69 = f32[3072,128]{1,0:T(8,128)S(1)} custom-call(f32[8]{0:T(128)S(1)} %stack.28.coef_ref, f32[8,12,16,128]{3,2,1,0:T(8,128)S(1)} %get-tuple-element.26.x_ref, f32[8,12,16,128]{3,2,1,0:T(8,128)S(1)} %get-tuple-element.27.lap_ref, f32[8,6,16,128]{3,2,1,0:T(8,128)S(1)} %get-tuple-element.28.pot_own_ref, f32[768,128]{1,0:T(8,128)S(1)} %bitcast.59), custom_call_target="tpu_custom_call" | custom-call | flops 60000000 | bytes 40000000 | tf_op jit(solution)/shard_map/pallas_call | solution.py:259
  83.5 1.2 copy-done
  84.7 9.3 %all-to-all-start.1 = ((f32[256,1,1536]{2,1,0:T(1,128)}), f32[256,1,1536]{2,1,0:T(1,128)S(1)}, u32[]{:S(2)}, u32[]{:S(2)}) async-start(f32[256,1,1536]{2,1,0:T(1,128)} %bitcast.56), calls=%async_computation.1 | async-start | bytes 3145728 | tf_op jit(solution)/shard_map/all_to_all | solution.py:58
  94.0 38.8 %all-to-all-done.1 = f32[256,1,1536]{2,1,0:T(1,128)S(1)} async-done(((f32[256,1,1536]{2,1,0:T(1,128)}), f32[256,1,1536]{2,1,0:T(1,128)S(1)}, u32[]{:S(2)}, u32[]{:S(2)}) %all-to-all-start.1) | async-done | bytes 1572896 | tf_op jit(solution)/shard_map/all_to_all | solution.py:58
  133.1 4.9 %collective-permute-start.2 = (f32[256,768]{1,0:T(8,128)S(1)}, f32[256,768]{1,0:T(8,128)S(1)}, u32[]{:S(2)}, u32[]{:S(2)}) collective-permute-start(f32[256,768]{1,0:T(8,128)S(1)} %get-tuple-element.33), channel_id=1, source_target_pairs={{0,128},{128,0},{256,384},{384,256},{1,129},{129,1},{257,385},{385... | collective-permute-start | bytes 2359304 | tf_op jit(solution)/shard_map/ppermute | solution.py:327
  140.5 1.1 pad_maximum_fusion
  141.6 1.2 convolution_add_fusion.1
  142.8 3.8 %all-to-all-start.2 = ((f32[4,128,512]{2,1,0:T(8,128)}), f32[4,128,512]{2,1,0:T(8,128)S(1)}, u32[]{:S(2)}, u32[]{:S(2)}) async-start(f32[4,128,512]{2,1,0:T(8,128)} %bitcast.24), calls=%async_computation.2 | async-start | bytes 2097152 | tf_op jit(solution)/shard_map/all_to_all | solution.py:58
  146.9 5.1 %collective-permute-start.3 = (f32[384,128]{1,0:T(8,128)}, f32[384,128]{1,0:T(8,128)}, u32[]{:S(2)}, u32[]{:S(2)}) collective-permute-start(f32[384,128]{1,0:T(8,128)} %convolution_add_fusion.1), channel_id=1, source_target_pairs={{0,256},{256,0},{128,384},{384,128},{1,257},{257,1},{129,385},{385... | collective-permute-start | bytes 589832 | tf_op jit(solution)/shard_map/ppermute | solution.py:349
  152.4 7.0 %collective-permute-done.3 = f32[384,128]{1,0:T(8,128)} collective-permute-done((f32[384,128]{1,0:T(8,128)}, f32[384,128]{1,0:T(8,128)}, u32[]{:S(2)}, u32[]{:S(2)}) %collective-permute-start.3) | collective-permute-done | bytes 196640 | tf_op jit(solution)/shard_map/ppermute | solution.py:349
  159.4 1.8 all-to-all-done.2
  162.8 9.1 %all-to-all-start.3 = ((f32[64,1,1024]{2,1,0:T(1,128)}), f32[64,1,1024]{2,1,0:T(1,128)S(1)}, u32[]{:S(2)}, u32[]{:S(2)}) async-start(f32[64,1,1024]{2,1,0:T(1,128)} %copy.16), calls=%async_computation.3 | async-start | bytes 524288 | tf_op jit(solution)/shard_map/all_to_all | solution.py:58
  172.2 6.8 %collective-permute-start.4 = (f32[256,128]{1,0:T(8,128)S(1)}, f32[256,128]{1,0:T(8,128)S(1)}, u32[]{:S(2)}, u32[]{:S(2)}) collective-permute-start(f32[256,128]{1,0:T(8,128)S(1)} %convolution_add_fusion.2), channel_id=1, source_target_pairs={{0,256},{256,0},{128,384},{384,128},{1,257},{257,1},{129,385},{385... | collective-permute-start | bytes 393224 | tf_op jit(solution)/shard_map/ppermute | solution.py:349
  179.3 9.6 %collective-permute-done.4 = f32[256,128]{1,0:T(8,128)S(1)} collective-permute-done((f32[256,128]{1,0:T(8,128)S(1)}, f32[256,128]{1,0:T(8,128)S(1)}, u32[]{:S(2)}, u32[]{:S(2)}) %collective-permute-start.4) | collective-permute-done | bytes 131104 | tf_op jit(solution)/shard_map/ppermute | solution.py:349
  189.1 1.1 broadcast_in_dim.9
  190.1 11.5 %all-to-all-start.4 = ((f32[128,1,1024]{2,1,0:T(1,128)}), f32[128,1,1024]{2,1,0:T(1,128)S(1)}, u32[]{:S(2)}, u32[]{:S(2)}) async-start(f32[128,1,1024]{2,1,0:T(1,128)} %broadcast_in_dim.9), calls=%async_computation.4 | async-start | bytes 1048576 | tf_op jit(solution)/shard_map/all_to_all | solution.py:361
  203.4 3.7 %collective-permute-start.5 = (f32[128,128]{1,0:T(8,128)S(1)}, f32[128,128]{1,0:T(8,128)S(1)}, u32[]{:S(2)}, u32[]{:S(2)}) collective-permute-start(f32[128,128]{1,0:T(8,128)S(1)} %convolution_add_fusion.3), channel_id=1, source_target_pairs={{0,256},{256,0},{128,384},{384,128},{1,257},{257,1},{129,385},{385... | collective-permute-start | bytes 196616 | tf_op jit(solution)/shard_map/ppermute | solution.py:349
  207.1 10.1 %collective-permute-done.5 = f32[128,128]{1,0:T(8,128)S(1)} collective-permute-done((f32[128,128]{1,0:T(8,128)S(1)}, f32[128,128]{1,0:T(8,128)S(1)}, u32[]{:S(2)}, u32[]{:S(2)}) %collective-permute-start.5) | collective-permute-done | bytes 65568 | tf_op jit(solution)/shard_map/ppermute | solution.py:349
  218.9 1.5 all-to-all-done.4
  (41 shorter events, 12.3 us)
Async XLA Ops:
  1.5 1.1 copy-start.1
  2.9 53.8 %copy-start.2 = (f32[512,128]{1,0:T(8,128)S(1)}, f32[512,128]{1,0:T(8,128)}, u32[]{:S(2)}) copy-start(f32[512,128]{1,0:T(8,128)} %param.7) | copy-start | bytes 786436
  2.9 61.7 %copy-start.3 = (f32[3]{0:T(128)S(1)}, f32[3]{0:T(128)}, u32[]{:S(2)}) copy-start(f32[3]{0:T(128)} %param.6) | copy-start | bytes 40
  51.9 20.2 %collective-permute-start = (f32[128,1,768]{2,1,0:T(1,128)S(1)}, f32[128,1,768]{2,1,0:T(1,128)S(1)}, u32[]{:S(2)}, u32[]{:S(2)}) collective-permute-start(f32[128,1,768]{2,1,0:T(1,128)S(1)} %slice.69), channel_id=1, source_target_pairs={{0,128},{128,0},{256,384},{384,256},{1,129},{129,1},{257,385},{385... | collective-permute-start | bytes 1179656 | tf_op jit(solution)/shard_map/ppermute | solution.py:319
  56.7 28.0 %collective-permute-start.1 = (f32[512,128]{1,0:T(8,128)S(1)}, f32[512,128]{1,0:T(8,128)S(1)}, u32[]{:S(2)}, u32[]{:S(2)}) collective-permute-start(f32[512,128]{1,0:T(8,128)S(1)} %copy-done.2), channel_id=1, source_target_pairs={{0,256},{256,0},{128,384},{384,128},{1,257},{257,1},{129,385},{385... | collective-permute-start | bytes 786440 | tf_op jit(solution)/shard_map/ppermute | solution.py:318
  83.5 1.2 copy-start
  84.7 48.1 %all-to-all-start.1 = ((f32[256,1,1536]{2,1,0:T(1,128)}), f32[256,1,1536]{2,1,0:T(1,128)S(1)}, u32[]{:S(2)}, u32[]{:S(2)}) async-start(f32[256,1,1536]{2,1,0:T(1,128)} %bitcast.56), calls=%async_computation.1 | async-start | bytes 3145728 | tf_op jit(solution)/shard_map/all_to_all | solution.py:58
  133.1 6.6 %collective-permute-start.2 = (f32[256,768]{1,0:T(8,128)S(1)}, f32[256,768]{1,0:T(8,128)S(1)}, u32[]{:S(2)}, u32[]{:S(2)}) collective-permute-start(f32[256,768]{1,0:T(8,128)S(1)} %get-tuple-element.33), channel_id=1, source_target_pairs={{0,128},{128,0},{256,384},{384,256},{1,129},{129,1},{257,385},{385... | collective-permute-start | bytes 2359304 | tf_op jit(solution)/shard_map/ppermute | solution.py:327
  142.8 18.4 %all-to-all-start.2 = ((f32[4,128,512]{2,1,0:T(8,128)}), f32[4,128,512]{2,1,0:T(8,128)S(1)}, u32[]{:S(2)}, u32[]{:S(2)}) async-start(f32[4,128,512]{2,1,0:T(8,128)} %bitcast.24), calls=%async_computation.2 | async-start | bytes 2097152 | tf_op jit(solution)/shard_map/all_to_all | solution.py:58
  146.9 12.4 %collective-permute-start.3 = (f32[384,128]{1,0:T(8,128)}, f32[384,128]{1,0:T(8,128)}, u32[]{:S(2)}, u32[]{:S(2)}) collective-permute-start(f32[384,128]{1,0:T(8,128)} %convolution_add_fusion.1), channel_id=1, source_target_pairs={{0,256},{256,0},{128,384},{384,128},{1,257},{257,1},{129,385},{385... | collective-permute-start | bytes 589832 | tf_op jit(solution)/shard_map/ppermute | solution.py:349
  162.8 26.1 %all-to-all-start.3 = ((f32[64,1,1024]{2,1,0:T(1,128)}), f32[64,1,1024]{2,1,0:T(1,128)S(1)}, u32[]{:S(2)}, u32[]{:S(2)}) async-start(f32[64,1,1024]{2,1,0:T(1,128)} %copy.16), calls=%async_computation.3 | async-start | bytes 524288 | tf_op jit(solution)/shard_map/all_to_all | solution.py:58
  172.2 16.7 %collective-permute-start.4 = (f32[256,128]{1,0:T(8,128)S(1)}, f32[256,128]{1,0:T(8,128)S(1)}, u32[]{:S(2)}, u32[]{:S(2)}) collective-permute-start(f32[256,128]{1,0:T(8,128)S(1)} %convolution_add_fusion.2), channel_id=1, source_target_pairs={{0,256},{256,0},{128,384},{384,128},{1,257},{257,1},{129,385},{385... | collective-permute-start | bytes 393224 | tf_op jit(solution)/shard_map/ppermute | solution.py:349
  190.1 30.3 %all-to-all-start.4 = ((f32[128,1,1024]{2,1,0:T(1,128)}), f32[128,1,1024]{2,1,0:T(1,128)S(1)}, u32[]{:S(2)}, u32[]{:S(2)}) async-start(f32[128,1,1024]{2,1,0:T(1,128)} %broadcast_in_dim.9), calls=%async_computation.4 | async-start | bytes 1048576 | tf_op jit(solution)/shard_map/all_to_all | solution.py:361
  203.4 13.8 %collective-permute-start.5 = (f32[128,128]{1,0:T(8,128)S(1)}, f32[128,128]{1,0:T(8,128)S(1)}, u32[]{:S(2)}, u32[]{:S(2)}) collective-permute-start(f32[128,128]{1,0:T(8,128)S(1)} %convolution_add_fusion.3), channel_id=1, source_target_pairs={{0,256},{256,0},{128,384},{384,128},{1,257},{257,1},{129,385},{385... | collective-permute-start | bytes 196616 | tf_op jit(solution)/shard_map/ppermute | solution.py:349

commit v5 on v4

--- a/solution.py
+++ b/solution.py
@@ -39,12 +39,6 @@
 
 
 CORE_GROUPS = [[flat(2 * h + c, d) for d in ORDER for h in range(2)] for c in range(2)]
-X_GROUPS = [
-    [flat(b, chip(y, x, z)) for x in range(4)]
-    for b in range(4)
-    for y in range(8)
-    for z in range(4)
-]
 PLANE_GROUPS = [
     [flat(2 * h + c, chip(y, x, z)) for y in range(8) for z in range(4) for h in range(2)]
     for c in range(2)
@@ -334,30 +328,27 @@
         swapped = jnp.where(core == 0, weights, weights[:, ::-1])
         return swapped.transpose(1, 0, 2, 3).reshape(4 * BLOCKS, width)
 
-    def rotate(weights, start, end):
-        cells = slice(start, end)
-        return contract(phi[:, cells], weights[: 2 * BLOCKS], ((0,), (0,))) + contract(
-            phi_other[:, cells], weights[2 * BLOCKS :], ((0,), (0,))
+    def rotate(weights):
+        weights = by_core(weights)
+        return contract(phi, weights[: 2 * BLOCKS], ((0,), (0,))) + contract(
+            phi_other, weights[2 * BLOCKS :], ((0,), (0,))
         )
 
-    far = by_core(rotation_far)
-    cuts = (0, HALF // 2, 5 * HALF // 6, HALF)
-    parts = []
-
-    def send_part(k, tie):
-        tie, part = lax.optimization_barrier((tie, rotate(far, cuts[k], cuts[k + 1])))
-        parts.append(lax.ppermute(part, "band", Z_SWAP))
-        return tie
-
-    gram = send_part(0, gram)
-    terms = exchange(gram.reshape(4, BLOCKS, 4 * BLOCKS), X_GROUPS)
-    terms, parts[0] = lax.optimization_barrier((terms, parts[0]))
+    rotated_far = lax.ppermute(rotate(rotation_far), "band", Z_SWAP)
+
+    gram = gram.reshape(4, BLOCKS, 4 * BLOCKS)
+    place = lax.axis_index("dom") // 4 % 4
+    pieces = [lax.dynamic_index_in_dim(gram, (place + k) % 4, 0, keepdims=False) for k in range(4)]
+    for k in (2, 1, 3):
+        pairs = [
+            (chip(y, x, z), chip(y, (x + k) % 4, z)) for y in range(8) for x in range(4) for z in range(4)
+        ]
+        pieces[k] = lax.ppermute(pieces[k], "dom", pairs)
+    terms, rotated_far = lax.optimization_barrier((pieces, rotated_far))
+    terms = (terms[0] + terms[1]) + (terms[2] + terms[3])
+    terms = terms.reshape(32, 4, 2, 2, BLOCKS).transpose(0, 3, 1, 2, 4).reshape(64, 8 * BLOCKS)
+    terms = exchange(terms.reshape(64, 1, 8 * BLOCKS), PLANE_GROUPS)
     terms = jnp.sum(terms, axis=0)
-    terms = terms.reshape(32, 4, 2, 2, BLOCKS).transpose(0, 3, 1, 2, 4).reshape(64, 8 * BLOCKS)
-    terms = send_part(1, terms)
-    terms = exchange(terms.reshape(64, 1, 8 * BLOCKS), PLANE_GROUPS)
-    terms, parts[1] = lax.optimization_barrier((terms, parts[1]))
-    terms = send_part(2, jnp.sum(terms, axis=0))
     whole = lax.all_to_all(
         jnp.broadcast_to(terms[None], (BLOCKS, 1, 8 * BLOCKS)), "dom", 0, 0, tiled=True
     )
@@ -365,8 +356,7 @@
     whole = whole.reshape(2, 2, 2, BLOCKS, BLOCKS)
     whole = jnp.where(core == 0, whole, whole[:, :, ::-1])
     whole = whole.reshape(2, 4 * BLOCKS, BLOCKS)
-    rotated_near = rotate(by_core(rotation_near), 0, HALF)
-    rotated_far = jnp.concatenate(parts, axis=0)
+    rotated_near = rotate(rotation_near)
     lower = jnp.where(z_hi == 0, rotated_near, rotated_far)
     upper = jnp.where(z_hi == 0, rotated_far, rotated_near)
     rotated = jnp.concatenate([lower, upper], axis=0).reshape(1, BX, BY, BZ, width)

time: 223 us -> 218 us (0.978)
  blocking collectives: 48.9 us -> 69.3 us
  starting transfers between devices: 66.8 us -> 50.1 us
  waiting for transfers between devices: 69 us -> 63.6 us
  local copies, waits for them, and re-layouts: 8.4 us -> 5.19 us
    all_to_all x0 -> x1, blocking collectives: none -> 20.5 us  [exchange(): lax.all_to_all(x, ('band', 'dom'), 0, 0, tiled=True, axis_index_groups=gr...]
    ppermute x3 -> x4, waiting for transfers between devices: 26.6 us -> 9.85 us  [the longest x3 9.85 us: local(): pieces[k] = lax.ppermute(pieces[k], 'dom', pairs)]
    all_to_all x1, waiting for transfers between devices: 1.47 us -> 14.9 us  [local(): lax.all_to_all(jnp.broadcast_to(terms[None], (BLOCKS, 1, 8 * BLOCKS)), 'd...]
    all_to_all x3 -> x1, starting transfers between devices: 22.2 us -> 9.31 us  [exchange(): lax.all_to_all(x, ('band', 'dom'), 0, 0, tiled=True, axis_index_groups=gr...]
    all_to_all x3 -> x1, waiting for transfers between devices: 40.6 us -> 38.7 us  [exchange(): lax.all_to_all(x, ('band', 'dom'), 0, 0, tiled=True, axis_index_groups=gr...]
    ppermute x3 -> x4, starting transfers between devices: 15.6 us -> 14 us  [the longest x3 8.55 us: local(): pieces[k] = lax.ppermute(pieces[k], 'dom', pairs)]
    dot_general x10 -> x6, matrix products: 6.28 us -> 4.89 us  [contract(): lax.dot_general(left, right, (dims, ((), ())), precision=lax.Precision.HI...]
  transfers between devices with their start and end apart: 10 -> 9, of which waited for: 7 -> 6; matrix products, arithmetic and copies ran while one was open for 3% -> 3% of each run, Pallas kernels for 7% -> 7%
where the time goes in v5:
time: 218 us; the launch traced here: 216 us
  blocking collectives  69.3 us (32%)
  waiting for transfers between devices  63.6 us (29%)
  starting transfers between devices  50.1 us (23%)
  Pallas kernels  16.6 us (8%)
  local copies, waits for them, and re-layouts  5.19 us (2%)
  matrix products  4.89 us (2%)
  between operations  4.56 us (2%)
    all_to_all x1, blocking collectives, local(): lax.all_to_all(sent.reshape(BLOCKS, 1, SENT * LANES), 'dom', 0, 0, tiled=...  48.9 us
    all_to_all x1, waiting for transfers between devices, exchange(): lax.all_to_all(x, ('band', 'dom'), 0, 0, tiled=True, axis_index_groups=gr...  38.7 us
    all_to_all x1, blocking collectives, exchange(): lax.all_to_all(x, ('band', 'dom'), 0, 0, tiled=True, axis_index_groups=gr...  20.5 us
    all_to_all x1, waiting for transfers between devices, local(): lax.all_to_all(jnp.broadcast_to(terms[None], (BLOCKS, 1, 8 * BLOCKS)), 'd...  14.9 us
    pallas_call x1, Pallas kernels, filtered_fields(): pl.pallas_call(filter_kernel, out_shape=jax.ShapeDtypeStruct((BLOCKS * 2...  12.6 us
    ppermute x3, waiting for transfers between devices, local(): pieces[k] = lax.ppermute(pieces[k], 'dom', pairs)  9.85 us
    all_to_all x1, starting transfers between devices, local(): lax.all_to_all(jnp.broadcast_to(terms[None], (BLOCKS, 1, 8 * BLOCKS)), 'd...  9.4 us
    all_to_all x1, starting transfers between devices, exchange(): lax.all_to_all(x, ('band', 'dom'), 0, 0, tiled=True, axis_index_groups=gr...  9.31 us
  transfers between devices with their start and end apart: 9, of which 6 were waited for; matrix products, arithmetic and copies ran while one was open for 3% of the time, Pallas kernels for 7%

profile of v5, /device:TPU:1, one launch (start us, length us, event | category | flops | bytes accessed | tf_op | source)
XLA Modules:
  0.0 215.6 jit_solution(6849104882287435887)
XLA Ops:
  1.5 1.1 copy-done
  2.9 48.9 %all_to_all.20 = f32[128,1,2304]{2,1,0:T(1,128)S(1)} all-to-all(f32[128,1,2304]{2,1,0:T(1,128)S(1)} %bitcast.60), channel_id=1, replica_groups={{0,32,64,96,8,40,72,104,16,48,80,112,24,56,88,120,1,33,65,97,9,41,73,10..., dimensions={0} | all-to-all | bytes 2359296 | tf_op jit(solution)/shard_map/all_to_all | solution.py:308
  51.9 4.8 %collective-permute-start = (f32[128,1,768]{2,1,0:T(1,128)S(1)}, f32[128,1,768]{2,1,0:T(1,128)S(1)}, u32[]{:S(2)}, u32[]{:S(2)}) collective-permute-start(f32[128,1,768]{2,1,0:T(1,128)S(1)} %slice.47), channel_id=1, source_target_pairs={{0,128},{128,0},{256,384},{384,256},{1,129},{129,1},{257,385},{385... | collective-permute-start | bytes 1179656 | tf_op jit(solution)/shard_map/ppermute | solution.py:313
  56.7 7.9 %collective-permute-start.1 = (f32[512,128]{1,0:T(8,128)S(1)}, f32[512,128]{1,0:T(8,128)S(1)}, u32[]{:S(2)}, u32[]{:S(2)}) collective-permute-start(f32[512,128]{1,0:T(8,128)S(1)} %copy-done.1), channel_id=1, source_target_pairs={{0,256},{256,0},{128,384},{384,128},{1,257},{257,1},{129,385},{385... | collective-permute-start | bytes 786440 | tf_op jit(solution)/shard_map/ppermute | solution.py:312
  68.8 3.4 %shard_map.68 = (f32[8,12,16,128]{3,2,1,0:T(8,128)S(1)}, f32[8,12,16,128]{3,2,1,0:T(8,128)S(1)}, f32[8,6,16,128]{3,2,1,0:T(8,128)S(1)}) custom-call(f32[2304,128]{1,0:T(8,128)S(1)} %bitcast.58), custom_call_target="tpu_custom_call" | custom-call | flops 20000000 | bytes 20000000 | tf_op jit(solution)/shard_map/pallas_call | solution.py:236
  72.3 12.6 %shard_map.69 = f32[3072,128]{1,0:T(8,128)} custom-call(f32[8]{0:T(128)S(1)} %stack.28.coef_ref, f32[8,12,16,128]{3,2,1,0:T(8,128)S(1)} %get-tuple-element.21.x_ref, f32[8,12,16,128]{3,2,1,0:T(8,128)S(1)} %get-tuple-element.22.lap_ref, f32[8,6,16,128]{3,2,1,0:T(8,128)S(1)} %get-tuple-element.23.pot_own_ref, f32[768,128]{1,0:T(8,128)S(1)} %bitcast.62), custom_call_target="tpu_custom_call" | custom-call | flops 60000000 | bytes 40000000 | tf_op jit(solution)/shard_map/pallas_call | solution.py:253
  84.9 9.3 %all-to-all-start.1 = ((f32[256,1,1536]{2,1,0:T(1,128)}), f32[256,1,1536]{2,1,0:T(1,128)S(1)}, u32[]{:S(2)}, u32[]{:S(2)}) async-start(f32[256,1,1536]{2,1,0:T(1,128)} %bitcast.14), calls=%async_computation.1 | async-start | bytes 3145728 | tf_op jit(solution)/shard_map/all_to_all | solution.py:52
  94.3 38.7 %all-to-all-done.1 = f32[256,1,1536]{2,1,0:T(1,128)S(1)} async-done(((f32[256,1,1536]{2,1,0:T(1,128)}), f32[256,1,1536]{2,1,0:T(1,128)S(1)}, u32[]{:S(2)}, u32[]{:S(2)}) %all-to-all-start.1) | async-done | bytes 1572896 | tf_op jit(solution)/shard_map/all_to_all | solution.py:52
  133.3 4.7 %collective-permute-start.2 = (f32[256,768]{1,0:T(8,128)S(1)}, f32[256,768]{1,0:T(8,128)S(1)}, u32[]{:S(2)}, u32[]{:S(2)}) collective-permute-start(f32[256,768]{1,0:T(8,128)S(1)} %get-tuple-element.28), channel_id=1, source_target_pairs={{0,128},{128,0},{256,384},{384,256},{1,129},{129,1},{257,385},{385... | collective-permute-start | bytes 2359304 | tf_op jit(solution)/shard_map/ppermute | solution.py:321
  138.9 0.8 fusion.7
  140.7 5.5 %collective-permute-start.6 = (f32[768,128]{1,0:T(8,128)S(1)}, f32[768,128]{1,0:T(8,128)S(1)}, u32[]{:S(2)}, u32[]{:S(2)}) collective-permute-start(f32[768,128]{1,0:T(8,128)S(1)} %convolution_add_fusion), channel_id=1, source_target_pairs={{0,256},{256,0},{128,384},{384,128},{1,257},{257,1},{129,385},{385... | collective-permute-start | bytes 1179656 | tf_op jit(solution)/shard_map/ppermute | solution.py:337
  146.1 0.8 fusion.8
  147.2 2.3 %collective-permute-start.3 = (f32[128,512]{1,0:T(8,128)S(1)}, f32[128,512]{1,0:T(8,128)S(1)}, u32[]{:S(2)}, u32[]{:S(2)}) collective-permute-start(f32[128,512]{1,0:T(8,128)S(1)} %get-tuple-element.39), channel_id=1, source_target_pairs={{0,4},{1,5},{2,6},{3,7},{4,8},{5,9},{6,10},{7,11},{8,12},{9,13},{1... | collective-permute-start | bytes 786440 | tf_op jit(solution)/shard_map/ppermute | solution.py:346
  149.5 3.7 %collective-permute-start.4 = (f32[128,512]{1,0:T(8,128)S(1)}, f32[128,512]{1,0:T(8,128)S(1)}, u32[]{:S(2)}, u32[]{:S(2)}) collective-permute-start(f32[128,512]{1,0:T(8,128)S(1)} %get-tuple-element.38), channel_id=1, source_target_pairs={{0,8},{1,9},{2,10},{3,11},{4,12},{5,13},{6,14},{7,15},{8,0},{9,1},... | collective-permute-start | bytes 786440 | tf_op jit(solution)/shard_map/ppermute | solution.py:346
  153.2 2.5 %collective-permute-start.5 = (f32[128,512]{1,0:T(8,128)S(1)}, f32[128,512]{1,0:T(8,128)S(1)}, u32[]{:S(2)}, u32[]{:S(2)}) collective-permute-start(f32[128,512]{1,0:T(8,128)S(1)} %get-tuple-element.37), channel_id=1, source_target_pairs={{0,12},{1,13},{2,14},{3,15},{4,0},{5,1},{6,2},{7,3},{8,4},{9,5},{1... | collective-permute-start | bytes 786440 | tf_op jit(solution)/shard_map/ppermute | solution.py:346
  155.8 2.2 %collective-permute-done.3 = f32[128,512]{1,0:T(8,128)S(1)} collective-permute-done((f32[128,512]{1,0:T(8,128)S(1)}, f32[128,512]{1,0:T(8,128)S(1)}, u32[]{:S(2)}, u32[]{:S(2)}) %collective-permute-start.3) | collective-permute-done | bytes 262176 | tf_op jit(solution)/shard_map/ppermute | solution.py:346
  157.9 4.8 %collective-permute-done.4 = f32[128,512]{1,0:T(8,128)S(1)} collective-permute-done((f32[128,512]{1,0:T(8,128)S(1)}, f32[128,512]{1,0:T(8,128)S(1)}, u32[]{:S(2)}, u32[]{:S(2)}) %collective-permute-start.4) | collective-permute-done | bytes 262176 | tf_op jit(solution)/shard_map/ppermute | solution.py:346
  162.7 2.9 %collective-permute-done.5 = f32[128,512]{1,0:T(8,128)S(1)} collective-permute-done((f32[128,512]{1,0:T(8,128)S(1)}, f32[128,512]{1,0:T(8,128)S(1)}, u32[]{:S(2)}, u32[]{:S(2)}) %collective-permute-start.5) | collective-permute-done | bytes 262176 | tf_op jit(solution)/shard_map/ppermute | solution.py:346
  166.0 20.5 %all_to_all.21 = f32[64,1,1024]{2,1,0:T(1,128)S(1)} all-to-all(f32[64,1,1024]{2,1,0:T(1,128)S(1)} %bitcast.68), channel_id=1, replica_groups={{0,256,1,257,2,258,3,259,16,272,17,273,18,274,19,275,32,288,33,289,34,2..., dimensions={0} | all-to-all | bytes 524288 | tf_op jit(solution)/shard_map/all_to_all | solution.py:52
  186.7 1.1 broadcast_in_dim.2
  187.7 9.4 %all-to-all-start.3 = ((f32[128,1,1024]{2,1,0:T(1,128)}), f32[128,1,1024]{2,1,0:T(1,128)S(1)}, u32[]{:S(2)}, u32[]{:S(2)}) async-start(f32[128,1,1024]{2,1,0:T(1,128)} %broadcast_in_dim.2), calls=%async_computation.3 | async-start | bytes 1048576 | tf_op jit(solution)/shard_map/all_to_all | solution.py:352
  198.8 0.9 pad_maximum_fusion.1
  199.7 14.9 %all-to-all-done.3 = f32[128,1,1024]{2,1,0:T(1,128)S(1)} async-done(((f32[128,1,1024]{2,1,0:T(1,128)}), f32[128,1,1024]{2,1,0:T(1,128)S(1)}, u32[]{:S(2)}, u32[]{:S(2)}) %all-to-all-start.3) | async-done | bytes 524320 | tf_op jit(solution)/shard_map/all_to_all | solution.py:352
  214.8 0.8 fusion.2
  (30 shorter events, 6.6 us)
Async XLA Ops:
  1.5 1.1 copy-start
  2.9 53.8 %copy-start.1 = (f32[512,128]{1,0:T(8,128)S(1)}, f32[512,128]{1,0:T(8,128)}, u32[]{:S(2)}) copy-start(f32[512,128]{1,0:T(8,128)} %param.7) | copy-start | bytes 786436
  2.9 61.7 %copy-start.2 = (f32[3]{0:T(128)S(1)}, f32[3]{0:T(128)}, u32[]{:S(2)}) copy-start(f32[3]{0:T(128)} %param.6) | copy-start | bytes 40
  51.9 20.3 %collective-permute-start = (f32[128,1,768]{2,1,0:T(1,128)S(1)}, f32[128,1,768]{2,1,0:T(1,128)S(1)}, u32[]{:S(2)}, u32[]{:S(2)}) collective-permute-start(f32[128,1,768]{2,1,0:T(1,128)S(1)} %slice.47), channel_id=1, source_target_pairs={{0,128},{128,0},{256,384},{384,256},{1,129},{129,1},{257,385},{385... | collective-permute-start | bytes 1179656 | tf_op jit(solution)/shard_map/ppermute | solution.py:313
  56.7 28.2 %collective-permute-start.1 = (f32[512,128]{1,0:T(8,128)S(1)}, f32[512,128]{1,0:T(8,128)S(1)}, u32[]{:S(2)}, u32[]{:S(2)}) collective-permute-start(f32[512,128]{1,0:T(8,128)S(1)} %copy-done.1), channel_id=1, source_target_pairs={{0,256},{256,0},{128,384},{384,128},{1,257},{257,1},{129,385},{385... | collective-permute-start | bytes 786440 | tf_op jit(solution)/shard_map/ppermute | solution.py:312
  84.9 48.1 %all-to-all-start.1 = ((f32[256,1,1536]{2,1,0:T(1,128)}), f32[256,1,1536]{2,1,0:T(1,128)S(1)}, u32[]{:S(2)}, u32[]{:S(2)}) async-start(f32[256,1,1536]{2,1,0:T(1,128)} %bitcast.14), calls=%async_computation.1 | async-start | bytes 3145728 | tf_op jit(solution)/shard_map/all_to_all | solution.py:52
  133.3 6.6 %collective-permute-start.2 = (f32[256,768]{1,0:T(8,128)S(1)}, f32[256,768]{1,0:T(8,128)S(1)}, u32[]{:S(2)}, u32[]{:S(2)}) collective-permute-start(f32[256,768]{1,0:T(8,128)S(1)} %get-tuple-element.28), channel_id=1, source_target_pairs={{0,128},{128,0},{256,384},{384,256},{1,129},{129,1},{257,385},{385... | collective-permute-start | bytes 2359304 | tf_op jit(solution)/shard_map/ppermute | solution.py:321
  140.7 24.9 %collective-permute-start.6 = (f32[768,128]{1,0:T(8,128)S(1)}, f32[768,128]{1,0:T(8,128)S(1)}, u32[]{:S(2)}, u32[]{:S(2)}) collective-permute-start(f32[768,128]{1,0:T(8,128)S(1)} %convolution_add_fusion), channel_id=1, source_target_pairs={{0,256},{256,0},{128,384},{384,128},{1,257},{257,1},{129,385},{385... | collective-permute-start | bytes 1179656 | tf_op jit(solution)/shard_map/ppermute | solution.py:337
  147.2 10.8 %collective-permute-start.3 = (f32[128,512]{1,0:T(8,128)S(1)}, f32[128,512]{1,0:T(8,128)S(1)}, u32[]{:S(2)}, u32[]{:S(2)}) collective-permute-start(f32[128,512]{1,0:T(8,128)S(1)} %get-tuple-element.39), channel_id=1, source_target_pairs={{0,4},{1,5},{2,6},{3,7},{4,8},{5,9},{6,10},{7,11},{8,12},{9,13},{1... | collective-permute-start | bytes 786440 | tf_op jit(solution)/shard_map/ppermute | solution.py:346
  149.5 13.2 %collective-permute-start.4 = (f32[128,512]{1,0:T(8,128)S(1)}, f32[128,512]{1,0:T(8,128)S(1)}, u32[]{:S(2)}, u32[]{:S(2)}) collective-permute-start(f32[128,512]{1,0:T(8,128)S(1)} %get-tuple-element.38), channel_id=1, source_target_pairs={{0,8},{1,9},{2,10},{3,11},{4,12},{5,13},{6,14},{7,15},{8,0},{9,1},... | collective-permute-start | bytes 786440 | tf_op jit(solution)/shard_map/ppermute | solution.py:346
  153.2 12.4 %collective-permute-start.5 = (f32[128,512]{1,0:T(8,128)S(1)}, f32[128,512]{1,0:T(8,128)S(1)}, u32[]{:S(2)}, u32[]{:S(2)}) collective-permute-start(f32[128,512]{1,0:T(8,128)S(1)} %get-tuple-element.37), channel_id=1, source_target_pairs={{0,12},{1,13},{2,14},{3,15},{4,0},{5,1},{6,2},{7,3},{8,4},{9,5},{1... | collective-permute-start | bytes 786440 | tf_op jit(solution)/shard_map/ppermute | solution.py:346
  187.7 26.9 %all-to-all-start.3 = ((f32[128,1,1024]{2,1,0:T(1,128)}), f32[128,1,1024]{2,1,0:T(1,128)S(1)}, u32[]{:S(2)}, u32[]{:S(2)}) async-start(f32[128,1,1024]{2,1,0:T(1,128)} %broadcast_in_dim.2), calls=%async_computation.3 | async-start | bytes 1048576 | tf_op jit(solution)/shard_map/all_to_all | solution.py:352

commit v6 on v5

--- a/solution.py
+++ b/solution.py
@@ -105,31 +105,29 @@
 
 
 def margins(ext):
-    lane = lax.broadcasted_iota(jnp.int32, (1, LANES), 1)
+    lane = lax.broadcasted_iota(jnp.int32, (8, LANES), 1)
     iz, iy, ix = lane // STEP_Z, lane // STEP_Y % PY, lane // STEP_X % PX
-    own_y, own_z = slice(OY, OY + BY), slice(OZ, OZ + BZ)
-
-    def below(v, step, keep):
-        return jnp.where(keep, pltpu.roll(v, step, v.ndim - 1), 0.0)
-
-    def above(v, step, keep):
-        return jnp.where(keep, pltpu.roll(v, LANES - step, v.ndim - 1), 0.0)
-
-    def inner(i, carry):
-        at = i + OX
-        ext[at, own_y, 0:8] = below(ext[at, own_y, OZ + 8 : OZ + 16], STEP_Z, iz > 0)
-        ext[at, own_y, OZ + BZ : OZ + BZ + 8] = above(ext[at, own_y, OZ : OZ + 8], STEP_Z, iz < PZ - 1)
-        ext[at, 0:OY, own_z] = below(ext[at, BY : BY + OY, own_z], STEP_Y, iy > 0)
-        ext[at, OY + BY :, own_z] = above(ext[at, OY : 2 * OY, own_z], STEP_Y, iy < PY - 1)
-        return carry
-
-    def outer(i, carry):
-        ext[i, own_y, own_z] = below(ext[i + BX, own_y, own_z], STEP_X, ix > 0)
-        ext[i + OX + BX, own_y, own_z] = above(ext[i + OX, own_y, own_z], STEP_X, ix < PX - 1)
-        return carry
-
-    lax.fori_loop(0, BX, inner, 0)
-    lax.fori_loop(0, REACH, outer, 0)
+    masks = {0: (ix > 0, ix < PX - 1), 1: (iy > 0, iy < PY - 1), 2: (iz > 0, iz < PZ - 1)}
+    steps = (STEP_X, STEP_Y, STEP_Z)
+
+    def carry(dim, to_below, to_above, from_below, from_above):
+        below, above = masks[dim]
+        ext[to_below] = jnp.where(below, pltpu.roll(ext[from_below], steps[dim], 1), 0.0)
+        ext[to_above] = jnp.where(above, pltpu.roll(ext[from_above], LANES - steps[dim], 1), 0.0)
+
+    def at(x, y, z):
+        return (x, y, slice(z, z + 8))
+
+    for x in range(OX, OX + BX):
+        for y in range(OY, OY + BY):
+            carry(2, at(x, y, OZ - 8), at(x, y, OZ + BZ), at(x, y, OZ + BZ - 8), at(x, y, OZ))
+        for y in range(OY):
+            for z in range(OZ, OZ + BZ, 8):
+                carry(1, at(x, y, z), at(x, y + OY + BY, z), at(x, y + BY, z), at(x, y + OY, z))
+    for x in range(OX):
+        for y in range(OY, OY + BY):
+            for z in range(OZ, OZ + BZ, 8):
+                carry(0, at(x, y, z), at(x + OX + BX, y, z), at(x + BX, y, z), at(x + OX, y, z))
 
 
 YS = BY // 2
@@ -174,41 +172,54 @@
     lax.fori_loop(0, BX, body, 0)
 
 
-def filter_kernel(coef_ref, x_ref, lap_ref, pot_own_ref, v_other_ref, out_ref, ea, eb, pot, img):
-    second = coef_ref[7] > 0.5
+def filter_coefficients(bounds_ref):
+    lowest, cutoff, highest = (jnp.full((1, LANES), bounds_ref[k], jnp.float32) for k in range(3))
+    half_width = (highest - cutoff) / 2.0
+    centre = (highest + cutoff) / 2.0
+    s1 = half_width / (lowest - centre)
+    tau = 2.0 / s1
+    s2 = 1.0 / (tau - s1)
+    s3 = 1.0 / (tau - s2)
+    scales = (s1 / half_width, 2.0 * s2 / half_width, 2.0 * s3 / half_width)
+    return centre, scales, (None, s1 * s2, s2 * s3)
+
+
+def filter_kernel(core_ref, bounds_ref, x_ref, lap_ref, pot_own_ref, v_other_ref, out_ref, ea, eb, pot, img):
+    shift, scales, backs = filter_coefficients(bounds_ref)
+    second = core_ref[0] == 1
     for s in range(HALF_TILES):
         other = jnp.transpose(v_other_ref[pl.ds(s, BLOCKS, stride=HALF_TILES), :]).reshape(BX, BZ, LANES)
         mine = pot_own_ref[:, s]
         pot[:, s] = jnp.where(second, other, mine)
         pot[:, s + HALF_TILES] = jnp.where(second, mine, other)
 
-    def image(total, centre, i, y0, scale, shift):
-        local = pot[i, y0 : y0 + YS] - shift
-        return (scale * KINETIC) * total + scale * (local * centre)
+    def image(total, centre, i, y0):
+        return KINETIC * total + (pot[i, y0 : y0 + YS] - shift) * centre
 
     def first(i, carry):
         for y0 in range(0, BY, YS):
             total, centre = lap_ref[i, y0 : y0 + YS], x_ref[i, y0 : y0 + YS]
-            set_own(eb, i, y0, image(total, centre, i, y0, coef_ref[0], coef_ref[1]))
+            set_own(eb, i, y0, scales[0] * image(total, centre, i, y0))
         return carry
 
     def next_field(i, carry):
         for y0 in range(0, BY, YS):
-            new = image(laplace(eb, i, y0), own(eb, i, y0), i, y0, coef_ref[2], coef_ref[1])
-            set_own(ea, i, y0, new - coef_ref[3] * x_ref[i, y0 : y0 + YS])
+            new = scales[1] * image(laplace(eb, i, y0), own(eb, i, y0), i, y0)
+            set_own(ea, i, y0, new - backs[1] * x_ref[i, y0 : y0 + YS])
         return carry
 
     def last_field(i, squares):
         for y0 in range(0, BY, YS):
-            new = image(laplace(ea, i, y0), own(ea, i, y0), i, y0, coef_ref[4], coef_ref[1])
-            new = new - coef_ref[5] * own(eb, i, y0)
+            new = scales[2] * image(laplace(ea, i, y0), own(ea, i, y0), i, y0)
+            new = new - backs[2] * own(eb, i, y0)
             set_own(eb, i, y0, new)
             squares = squares + jnp.sum(new * new, axis=0)
         return squares
 
     def image_field(i, carry):
         for y0 in range(0, BY, YS):
-            img[i, y0 : y0 + YS] = image(laplace(eb, i, y0), own(eb, i, y0), i, y0, 1.0, 0.0)
+            centre = own(eb, i, y0)
+            img[i, y0 : y0 + YS] = KINETIC * laplace(eb, i, y0) + pot[i, y0 : y0 + YS] * centre
         return carry
 
     lax.fori_loop(0, BX, first, 0)
@@ -248,12 +259,12 @@
     )(got)
 
 
-def filtered_fields(coef, x, lap, pot_own, v_other):
+def filtered_fields(core, bounds, x, lap, pot_own, v_other):
     vmem = pl.BlockSpec(memory_space=pltpu.VMEM)
     return pl.pallas_call(
         filter_kernel,
         out_shape=jax.ShapeDtypeStruct((BLOCKS * 2 * TILES, LANES), jnp.float32),
-        in_specs=[pl.BlockSpec(memory_space=pltpu.SMEM), vmem, vmem, vmem, vmem],
+        in_specs=[pl.BlockSpec(memory_space=pltpu.SMEM)] * 2 + [vmem] * 4,
         out_specs=vmem,
         scratch_shapes=[
             pltpu.VMEM(EXT, jnp.float32),
@@ -263,29 +274,7 @@
         ],
         compiler_params=pltpu.CompilerParams(vmem_limit_bytes=36 * 1024 * 1024),
         cost_estimate=pl.CostEstimate(flops=60_000_000, bytes_accessed=40_000_000, transcendentals=0),
-    )(coef, x, lap, pot_own, v_other)
-
-
-def filter_coefficients(bounds, second):
-    lowest, cutoff, highest = bounds[0], bounds[1], bounds[2]
-    half_width = (highest - cutoff) / 2.0
-    centre = (highest + cutoff) / 2.0
-    s1 = half_width / (lowest - centre)
-    tau = 2.0 / s1
-    s2 = 1.0 / (tau - s1)
-    s3 = 1.0 / (tau - s2)
-    return jnp.stack(
-        [
-            s1 / half_width,
-            centre,
-            2.0 * s2 / half_width,
-            s1 * s2,
-            2.0 * s3 / half_width,
-            s2 * s3,
-            jnp.float32(0.0),
-            second,
-        ]
-    )
+    )(core, bounds, x, lap, pot_own, v_other)
 
 
 def contract(left, right, dims):
@@ -301,10 +290,10 @@
 def local(orbitals, potential, bounds, rotation):
     width = rotation.shape[1]
     band = lax.axis_index("band")
-    z_hi, core = band // 2, band % 2
-    coef = filter_coefficients(bounds, core.astype(jnp.float32))
-
-    sent = packed(core.reshape(1), orbitals.reshape(CELLS, width), potential[0])
+    z_hi, core = band >> 1, band & 1
+    here = core.reshape(1)
+
+    sent = packed(here, orbitals.reshape(CELLS, width), potential[0])
     got = lax.all_to_all(
         sent.reshape(BLOCKS, 1, SENT * LANES), "dom", 0, 0, tiled=True, axis_index_groups=[ORDER]
     )
@@ -312,7 +301,9 @@
     rotation_far = lax.ppermute(rotation_near, "band", Z_SWAP)
     v_other = lax.ppermute(got[:, :, CELLS:], "band", CORE_SWAP)
     x, lap, pot_own = first_laplace(got.reshape(BLOCKS * SENT, LANES))
-    images = filtered_fields(coef, x, lap, pot_own, v_other.reshape(BLOCKS * HALF_TILES, LANES))
+    images = filtered_fields(
+        here, bounds, x, lap, pot_own, v_other.reshape(BLOCKS * HALF_TILES, LANES)
+    )
 
     images, rotation_far = lax.optimization_barrier((images, rotation_far))
     got = exchange(images.reshape(2 * BLOCKS, 1, CELLS), CORE_GROUPS)
@@ -337,8 +328,8 @@
     rotated_far = lax.ppermute(rotate(rotation_far), "band", Z_SWAP)
 
     gram = gram.reshape(4, BLOCKS, 4 * BLOCKS)
-    place = lax.axis_index("dom") // 4 % 4
-    pieces = [lax.dynamic_index_in_dim(gram, (place + k) % 4, 0, keepdims=False) for k in range(4)]
+    place = (lax.axis_index("dom") >> 2) & 3
+    pieces = [lax.dynamic_index_in_dim(gram, (place + k) & 3, 0, keepdims=False) for k in range(4)]
     for k in (2, 1, 3):
         pairs = [
             (chip(y, x, z), chip(y, (x + k) % 4, z)) for y in range(8) for x in range(4) for z in range(4)

time: 218 us -> 214 us (0.982)
  starting transfers between devices: 50.1 us -> 53.9 us
  between operations: 4.56 us -> 0.93 us
  Pallas kernels: 16.6 us -> 13.1 us
    all_to_all x1, starting transfers between devices: 9.31 us -> 12.8 us  [exchange(): lax.all_to_all(x, ('band', 'dom'), 0, 0, tiled=True, axis_index_groups=gr...]
    pallas_call x1, Pallas kernels: 12.6 us -> 9.98 us  [filtered_fields(): pl.pallas_call(filter_kernel, out_shape=jax.ShapeDtypeStruct((BLOCKS * 2...]
  transfers between devices with their start and end apart: 9 -> 9, of which waited for: 6 -> 5; matrix products, arithmetic and copies ran while one was open for 3% -> 2% of each run, Pallas kernels for 7% -> 6%
where the time goes in v6:
time: 214 us; the launch traced here: 211 us
  blocking collectives  69.1 us (32%)
  waiting for transfers between devices  63.3 us (30%)
  starting transfers between devices  53.9 us (25%)
  Pallas kernels  13.1 us (6%)
  matrix products  4.9 us (2%)
  local copies, waits for them, and re-layouts  4.51 us (2%)
    all_to_all x1, blocking collectives, local(): lax.all_to_all(sent.reshape(BLOCKS, 1, SENT * LANES), 'dom', 0, 0, tiled=...  48.9 us
    all_to_all x1, waiting for transfers between devices, exchange(): lax.all_to_all(x, ('band', 'dom'), 0, 0, tiled=True, axis_index_groups=gr...  38.5 us
    all_to_all x1, blocking collectives, exchange(): lax.all_to_all(x, ('band', 'dom'), 0, 0, tiled=True, axis_index_groups=gr...  20.3 us
    all_to_all x1, waiting for transfers between devices, local(): lax.all_to_all(jnp.broadcast_to(terms[None], (BLOCKS, 1, 8 * BLOCKS)), 'd...  14.9 us
    all_to_all x1, starting transfers between devices, exchange(): lax.all_to_all(x, ('band', 'dom'), 0, 0, tiled=True, axis_index_groups=gr...  12.8 us
    pallas_call x1, Pallas kernels, filtered_fields(): pl.pallas_call(filter_kernel, out_shape=jax.ShapeDtypeStruct((BLOCKS * 2...  9.98 us
    ppermute x3, waiting for transfers between devices, local(): pieces[k] = lax.ppermute(pieces[k], 'dom', pairs)  9.88 us
    all_to_all x1, starting transfers between devices, local(): lax.all_to_all(jnp.broadcast_to(terms[None], (BLOCKS, 1, 8 * BLOCKS)), 'd...  9.4 us
  transfers between devices with their start and end apart: 9, of which 5 were waited for; matrix products, arithmetic and copies ran while one was open for 2% of the time, Pallas kernels for 6%

profile of v6, /device:TPU:1, one launch (start us, length us, event | category | flops | bytes accessed | tf_op | source)
XLA Modules:
  0.0 211.0 jit_solution(13778769279960768375)
XLA Ops:
  1.5 1.1 copy-done
  2.9 48.9 %all_to_all.20 = f32[128,1,2304]{2,1,0:T(1,128)S(1)} all-to-all(f32[128,1,2304]{2,1,0:T(1,128)S(1)} %bitcast.52), channel_id=1, replica_groups={{0,32,64,96,8,40,72,104,16,48,80,112,24,56,88,120,1,33,65,97,9,41,73,10..., dimensions={0} | all-to-all | bytes 2359296 | tf_op jit(solution)/shard_map/all_to_all | solution.py:297
  51.9 4.8 %collective-permute-start = (f32[128,1,768]{2,1,0:T(1,128)S(1)}, f32[128,1,768]{2,1,0:T(1,128)S(1)}, u32[]{:S(2)}, u32[]{:S(2)}) collective-permute-start(f32[128,1,768]{2,1,0:T(1,128)S(1)} %slice.35), channel_id=1, source_target_pairs={{0,128},{128,0},{256,384},{384,256},{1,129},{129,1},{257,385},{385... | collective-permute-start | bytes 1179656 | tf_op jit(solution)/shard_map/ppermute | solution.py:302
  56.7 7.9 %collective-permute-start.1 = (f32[512,128]{1,0:T(8,128)S(1)}, f32[512,128]{1,0:T(8,128)S(1)}, u32[]{:S(2)}, u32[]{:S(2)}) collective-permute-start(f32[512,128]{1,0:T(8,128)S(1)} %copy-done.2), channel_id=1, source_target_pairs={{0,256},{256,0},{128,384},{384,128},{1,257},{257,1},{129,385},{385... | collective-permute-start | bytes 786440 | tf_op jit(solution)/shard_map/ppermute | solution.py:301
  64.6 2.5 %shard_map.68 = (f32[8,12,16,128]{3,2,1,0:T(8,128)S(1)}, f32[8,12,16,128]{3,2,1,0:T(8,128)S(1)}, f32[8,6,16,128]{3,2,1,0:T(8,128)S(1)}) custom-call(f32[2304,128]{1,0:T(8,128)S(1)} %bitcast.50), custom_call_target="tpu_custom_call" | custom-call | flops 20000000 | bytes 20000000 | tf_op jit(solution)/shard_map/pallas_call | solution.py:247
  67.1 10.0 %shard_map.69 = f32[3072,128]{1,0:T(8,128)} custom-call(s32[1]{0:T(128)} %bitcast.core_ref, f32[3]{0:T(128)S(1)} %copy-done.1, f32[8,12,16,128]{3,2,1,0:T(8,128)S(1)} %get-tuple-element.21.x_ref, f32[8,12,16,128]{3,2,1,0:T(8,128)S(1)} %get-tuple-element.22.lap_ref, f32[8,6,16,128]{3,2,1,0:T(8,128)S(1)} %get-tuple-element.23.pot_own_ref, f32[768,128]{1,0:T(8,128)S(1)} %bitcast.54), custom_call_target="tpu_custom_call" | custom-call | flops 60000000 | bytes 40000000 | tf_op jit(solution)/shard_map/pallas_call | solution.py:264
  77.1 12.8 %all-to-all-start.1 = ((f32[256,1,1536]{2,1,0:T(1,128)}), f32[256,1,1536]{2,1,0:T(1,128)S(1)}, u32[]{:S(2)}, u32[]{:S(2)}) async-start(f32[256,1,1536]{2,1,0:T(1,128)} %bitcast.6), calls=%async_computation.1 | async-start | bytes 3145728 | tf_op jit(solution)/shard_map/all_to_all | solution.py:52
  89.9 38.5 %all-to-all-done.1 = f32[256,1,1536]{2,1,0:T(1,128)S(1)} async-done(((f32[256,1,1536]{2,1,0:T(1,128)}), f32[256,1,1536]{2,1,0:T(1,128)S(1)}, u32[]{:S(2)}, u32[]{:S(2)}) %all-to-all-start.1) | async-done | bytes 1572896 | tf_op jit(solution)/shard_map/all_to_all | solution.py:52
  128.6 5.3 %collective-permute-start.2 = (f32[256,768]{1,0:T(8,128)S(1)}, f32[256,768]{1,0:T(8,128)S(1)}, u32[]{:S(2)}, u32[]{:S(2)}) collective-permute-start(f32[256,768]{1,0:T(8,128)S(1)} %get-tuple-element.28), channel_id=1, source_target_pairs={{0,128},{128,0},{256,384},{384,256},{1,129},{129,1},{257,385},{385... | collective-permute-start | bytes 2359304 | tf_op jit(solution)/shard_map/ppermute | solution.py:312
  134.8 0.8 fusion.6
  136.5 5.2 %collective-permute-start.6 = (f32[768,128]{1,0:T(8,128)S(1)}, f32[768,128]{1,0:T(8,128)S(1)}, u32[]{:S(2)}, u32[]{:S(2)}) collective-permute-start(f32[768,128]{1,0:T(8,128)S(1)} %convolution_add_fusion), channel_id=1, source_target_pairs={{0,256},{256,0},{128,384},{384,128},{1,257},{257,1},{129,385},{385... | collective-permute-start | bytes 1179656 | tf_op jit(solution)/shard_map/ppermute | solution.py:328
  141.7 0.8 fusion.7
  142.7 2.3 %collective-permute-start.3 = (f32[128,512]{1,0:T(8,128)S(1)}, f32[128,512]{1,0:T(8,128)S(1)}, u32[]{:S(2)}, u32[]{:S(2)}) collective-permute-start(f32[128,512]{1,0:T(8,128)S(1)} %get-tuple-element.39), channel_id=1, source_target_pairs={{0,4},{1,5},{2,6},{3,7},{4,8},{5,9},{6,10},{7,11},{8,12},{9,13},{1... | collective-permute-start | bytes 786440 | tf_op jit(solution)/shard_map/ppermute | solution.py:337
  145.0 3.6 %collective-permute-start.4 = (f32[128,512]{1,0:T(8,128)S(1)}, f32[128,512]{1,0:T(8,128)S(1)}, u32[]{:S(2)}, u32[]{:S(2)}) collective-permute-start(f32[128,512]{1,0:T(8,128)S(1)} %get-tuple-element.38), channel_id=1, source_target_pairs={{0,8},{1,9},{2,10},{3,11},{4,12},{5,13},{6,14},{7,15},{8,0},{9,1},... | collective-permute-start | bytes 786440 | tf_op jit(solution)/shard_map/ppermute | solution.py:337
  148.7 2.6 %collective-permute-start.5 = (f32[128,512]{1,0:T(8,128)S(1)}, f32[128,512]{1,0:T(8,128)S(1)}, u32[]{:S(2)}, u32[]{:S(2)}) collective-permute-start(f32[128,512]{1,0:T(8,128)S(1)} %get-tuple-element.37), channel_id=1, source_target_pairs={{0,12},{1,13},{2,14},{3,15},{4,0},{5,1},{6,2},{7,3},{8,4},{9,5},{1... | collective-permute-start | bytes 786440 | tf_op jit(solution)/shard_map/ppermute | solution.py:337
  151.3 2.4 %collective-permute-done.3 = f32[128,512]{1,0:T(8,128)S(1)} collective-permute-done((f32[128,512]{1,0:T(8,128)S(1)}, f32[128,512]{1,0:T(8,128)S(1)}, u32[]{:S(2)}, u32[]{:S(2)}) %collective-permute-start.3) | collective-permute-done | bytes 262176 | tf_op jit(solution)/shard_map/ppermute | solution.py:337
  153.7 4.5 %collective-permute-done.4 = f32[128,512]{1,0:T(8,128)S(1)} collective-permute-done((f32[128,512]{1,0:T(8,128)S(1)}, f32[128,512]{1,0:T(8,128)S(1)}, u32[]{:S(2)}, u32[]{:S(2)}) %collective-permute-start.4) | collective-permute-done | bytes 262176 | tf_op jit(solution)/shard_map/ppermute | solution.py:337
  158.2 3.0 %collective-permute-done.5 = f32[128,512]{1,0:T(8,128)S(1)} collective-permute-done((f32[128,512]{1,0:T(8,128)S(1)}, f32[128,512]{1,0:T(8,128)S(1)}, u32[]{:S(2)}, u32[]{:S(2)}) %collective-permute-start.5) | collective-permute-done | bytes 262176 | tf_op jit(solution)/shard_map/ppermute | solution.py:337
  161.6 20.3 %all_to_all.21 = f32[64,1,1024]{2,1,0:T(1,128)S(1)} all-to-all(f32[64,1,1024]{2,1,0:T(1,128)S(1)} %bitcast.60), channel_id=1, replica_groups={{0,256,1,257,2,258,3,259,16,272,17,273,18,274,19,275,32,288,33,289,34,2..., dimensions={0} | all-to-all | bytes 524288 | tf_op jit(solution)/shard_map/all_to_all | solution.py:52
  182.1 1.1 broadcast_in_dim.2
  183.1 9.4 %all-to-all-start.3 = ((f32[128,1,1024]{2,1,0:T(1,128)}), f32[128,1,1024]{2,1,0:T(1,128)S(1)}, u32[]{:S(2)}, u32[]{:S(2)}) async-start(f32[128,1,1024]{2,1,0:T(1,128)} %broadcast_in_dim.2), calls=%async_computation.3 | async-start | bytes 1048576 | tf_op jit(solution)/shard_map/all_to_all | solution.py:343
  194.2 0.9 pad_maximum_fusion.1
  195.1 14.9 %all-to-all-done.3 = f32[128,1,1024]{2,1,0:T(1,128)S(1)} async-done(((f32[128,1,1024]{2,1,0:T(1,128)}), f32[128,1,1024]{2,1,0:T(1,128)S(1)}, u32[]{:S(2)}, u32[]{:S(2)}) %all-to-all-start.3) | async-done | bytes 524320 | tf_op jit(solution)/shard_map/all_to_all | solution.py:343
  210.2 0.8 fusion.2
  (28 shorter events, 5.8 us)
Async XLA Ops:
  1.5 1.1 copy-start
  2.9 53.7 %copy-start.2 = (f32[512,128]{1,0:T(8,128)S(1)}, f32[512,128]{1,0:T(8,128)}, u32[]{:S(2)}) copy-start(f32[512,128]{1,0:T(8,128)} %param.7) | copy-start | bytes 786436
  51.8 15.3 %copy-start.1 = (f32[3]{0:T(128)S(1)}, f32[3]{0:T(128)}, u32[]{:S(2)}) copy-start(f32[3]{0:T(128)} %bounds_ref.1) | copy-start | bytes 40
  51.9 15.2 %collective-permute-start = (f32[128,1,768]{2,1,0:T(1,128)S(1)}, f32[128,1,768]{2,1,0:T(1,128)S(1)}, u32[]{:S(2)}, u32[]{:S(2)}) collective-permute-start(f32[128,1,768]{2,1,0:T(1,128)S(1)} %slice.35), channel_id=1, source_target_pairs={{0,128},{128,0},{256,384},{384,256},{1,129},{129,1},{257,385},{385... | collective-permute-start | bytes 1179656 | tf_op jit(solution)/shard_map/ppermute | solution.py:302
  56.7 20.4 %collective-permute-start.1 = (f32[512,128]{1,0:T(8,128)S(1)}, f32[512,128]{1,0:T(8,128)S(1)}, u32[]{:S(2)}, u32[]{:S(2)}) collective-permute-start(f32[512,128]{1,0:T(8,128)S(1)} %copy-done.2), channel_id=1, source_target_pairs={{0,256},{256,0},{128,384},{384,128},{1,257},{257,1},{129,385},{385... | collective-permute-start | bytes 786440 | tf_op jit(solution)/shard_map/ppermute | solution.py:301
  77.1 51.3 %all-to-all-start.1 = ((f32[256,1,1536]{2,1,0:T(1,128)}), f32[256,1,1536]{2,1,0:T(1,128)S(1)}, u32[]{:S(2)}, u32[]{:S(2)}) async-start(f32[256,1,1536]{2,1,0:T(1,128)} %bitcast.6), calls=%async_computation.1 | async-start | bytes 3145728 | tf_op jit(solution)/shard_map/all_to_all | solution.py:52
  128.6 7.0 %collective-permute-start.2 = (f32[256,768]{1,0:T(8,128)S(1)}, f32[256,768]{1,0:T(8,128)S(1)}, u32[]{:S(2)}, u32[]{:S(2)}) collective-permute-start(f32[256,768]{1,0:T(8,128)S(1)} %get-tuple-element.28), channel_id=1, source_target_pairs={{0,128},{128,0},{256,384},{384,256},{1,129},{129,1},{257,385},{385... | collective-permute-start | bytes 2359304 | tf_op jit(solution)/shard_map/ppermute | solution.py:312
  136.5 24.7 %collective-permute-start.6 = (f32[768,128]{1,0:T(8,128)S(1)}, f32[768,128]{1,0:T(8,128)S(1)}, u32[]{:S(2)}, u32[]{:S(2)}) collective-permute-start(f32[768,128]{1,0:T(8,128)S(1)} %convolution_add_fusion), channel_id=1, source_target_pairs={{0,256},{256,0},{128,384},{384,128},{1,257},{257,1},{129,385},{385... | collective-permute-start | bytes 1179656 | tf_op jit(solution)/shard_map/ppermute | solution.py:328
  142.7 10.9 %collective-permute-start.3 = (f32[128,512]{1,0:T(8,128)S(1)}, f32[128,512]{1,0:T(8,128)S(1)}, u32[]{:S(2)}, u32[]{:S(2)}) collective-permute-start(f32[128,512]{1,0:T(8,128)S(1)} %get-tuple-element.39), channel_id=1, source_target_pairs={{0,4},{1,5},{2,6},{3,7},{4,8},{5,9},{6,10},{7,11},{8,12},{9,13},{1... | collective-permute-start | bytes 786440 | tf_op jit(solution)/shard_map/ppermute | solution.py:337
  145.0 13.1 %collective-permute-start.4 = (f32[128,512]{1,0:T(8,128)S(1)}, f32[128,512]{1,0:T(8,128)S(1)}, u32[]{:S(2)}, u32[]{:S(2)}) collective-permute-start(f32[128,512]{1,0:T(8,128)S(1)} %get-tuple-element.38), channel_id=1, source_target_pairs={{0,8},{1,9},{2,10},{3,11},{4,12},{5,13},{6,14},{7,15},{8,0},{9,1},... | collective-permute-start | bytes 786440 | tf_op jit(solution)/shard_map/ppermute | solution.py:337
  148.7 12.5 %collective-permute-start.5 = (f32[128,512]{1,0:T(8,128)S(1)}, f32[128,512]{1,0:T(8,128)S(1)}, u32[]{:S(2)}, u32[]{:S(2)}) collective-permute-start(f32[128,512]{1,0:T(8,128)S(1)} %get-tuple-element.37), channel_id=1, source_target_pairs={{0,12},{1,13},{2,14},{3,15},{4,0},{5,1},{6,2},{7,3},{8,4},{9,5},{1... | collective-permute-start | bytes 786440 | tf_op jit(solution)/shard_map/ppermute | solution.py:337
  183.1 26.9 %all-to-all-start.3 = ((f32[128,1,1024]{2,1,0:T(1,128)}), f32[128,1,1024]{2,1,0:T(1,128)S(1)}, u32[]{:S(2)}, u32[]{:S(2)}) async-start(f32[128,1,1024]{2,1,0:T(1,128)} %broadcast_in_dim.2), calls=%async_computation.3 | async-start | bytes 1048576 | tf_op jit(solution)/shard_map/all_to_all | solution.py:343

commit v7 on v6

--- a/solution.py
+++ b/solution.py
@@ -46,6 +46,13 @@
 ]
 CORE_SWAP = [(0, 1), (1, 0), (2, 3), (3, 2)]
 Z_SWAP = [(0, 2), (2, 0), (1, 3), (3, 1)]
+Z_MIRROR = [
+    (flat(b, chip(y, x, z)), flat(b ^ 2, chip(y, x, 3 - z)))
+    for b in range(4)
+    for y in range(8)
+    for x in range(4)
+    for z in range(4)
+]
 
 
 def exchange(x, groups):
@@ -56,25 +63,36 @@
 EXT = (BX + 2 * REACH, BY + 2 * REACH, BZ + 16, LANES)
 
 
-def pack_kernel(core_ref, orbitals_ref, potential_ref, out_ref, wide):
-    for t in range(TILES):
-        tile = orbitals_ref[t * LANES : (t + 1) * LANES]
-        out_ref[pl.ds(t, BLOCKS, stride=SENT), :] = jnp.transpose(tile)
+def pack_kernel(core_ref, orbitals_hbm, potential_hbm, out_ref, orbitals_ref, potential_ref, wide, sems):
+    first = pltpu.make_async_copy(potential_hbm, potential_ref, sems.at[0])
+    second = pltpu.make_async_copy(orbitals_hbm, orbitals_ref, sems.at[1])
+    first.start()
+    second.start()
+    first.wait()
     wide[...] = jnp.concatenate([potential_ref[i] for i in range(BX)], axis=1)
     for s in range(HALF_TILES):
         row = wide[pl.ds(core_ref[0] * HALF_TILES + s, 1), :]
         out_ref[pl.ds(TILES + s, BLOCKS, stride=SENT), :] = jnp.broadcast_to(row, (BLOCKS, LANES))
+    second.wait()
+    for t in range(TILES):
+        tile = orbitals_ref[t * LANES : (t + 1) * LANES]
+        out_ref[pl.ds(t, BLOCKS, stride=SENT), :] = jnp.transpose(tile)
 
 
 def packed(core, orbitals, potential):
-    vmem = pl.BlockSpec(memory_space=pltpu.VMEM)
+    anywhere = pl.BlockSpec(memory_space=pl.ANY)
     return pl.pallas_call(
         pack_kernel,
         out_shape=jax.ShapeDtypeStruct((BLOCKS * SENT, LANES), jnp.float32),
-        in_specs=[pl.BlockSpec(memory_space=pltpu.SMEM), vmem, vmem],
-        out_specs=vmem,
-        scratch_shapes=[pltpu.VMEM((BY, BX * BZ), jnp.float32)],
-        compiler_params=pltpu.CompilerParams(vmem_limit_bytes=16 * 1024 * 1024),
+        in_specs=[pl.BlockSpec(memory_space=pltpu.SMEM), anywhere, anywhere],
+        out_specs=pl.BlockSpec(memory_space=pltpu.VMEM),
+        scratch_shapes=[
+            pltpu.VMEM((CELLS, LANES), jnp.float32),
+            pltpu.VMEM((BX, BY, BZ), jnp.float32),
+            pltpu.VMEM((BY, BX * BZ), jnp.float32),
+            pltpu.SemaphoreType.DMA((2,)),
+        ],
+        compiler_params=pltpu.CompilerParams(vmem_limit_bytes=60 * 1024 * 1024),
     )(core, orbitals, potential)
 
 
@@ -298,7 +316,7 @@
         sent.reshape(BLOCKS, 1, SENT * LANES), "dom", 0, 0, tiled=True, axis_index_groups=[ORDER]
     )
     got, rotation_near = lax.optimization_barrier((got, rotation))
-    rotation_far = lax.ppermute(rotation_near, "band", Z_SWAP)
+    rotation_far = lax.ppermute(rotation_near, ("band", "dom"), Z_MIRROR)
     v_other = lax.ppermute(got[:, :, CELLS:], "band", CORE_SWAP)
     x, lap, pot_own = first_laplace(got.reshape(BLOCKS * SENT, LANES))
     images = filtered_fields(
@@ -320,12 +338,11 @@
         return swapped.transpose(1, 0, 2, 3).reshape(4 * BLOCKS, width)
 
     def rotate(weights):
-        weights = by_core(weights)
         return contract(phi, weights[: 2 * BLOCKS], ((0,), (0,))) + contract(
             phi_other, weights[2 * BLOCKS :], ((0,), (0,))
         )
 
-    rotated_far = lax.ppermute(rotate(rotation_far), "band", Z_SWAP)
+    rotated_far = lax.ppermute(rotate(by_core(rotation_far)), "band", Z_SWAP)
 
     gram = gram.reshape(4, BLOCKS, 4 * BLOCKS)
     place = (lax.axis_index("dom") >> 2) & 3
@@ -335,10 +352,16 @@
             (chip(y, x, z), chip(y, (x + k) % 4, z)) for y in range(8) for x in range(4) for z in range(4)
         ]
         pieces[k] = lax.ppermute(pieces[k], "dom", pairs)
-    terms, rotated_far = lax.optimization_barrier((pieces, rotated_far))
+    near = by_core(rotation_near)
+    terms, rotated_far, near = lax.optimization_barrier((pieces, rotated_far, near))
     terms = (terms[0] + terms[1]) + (terms[2] + terms[3])
     terms = terms.reshape(32, 4, 2, 2, BLOCKS).transpose(0, 3, 1, 2, 4).reshape(64, 8 * BLOCKS)
     terms = exchange(terms.reshape(64, 1, 8 * BLOCKS), PLANE_GROUPS)
+    rotated_near = rotate(near)
+    lower = jnp.where(z_hi == 0, rotated_near, rotated_far)
+    upper = jnp.where(z_hi == 0, rotated_far, rotated_near)
+    rotated = jnp.concatenate([lower, upper], axis=0).reshape(1, BX, BY, BZ, width)
+    terms, rotated = lax.optimization_barrier((terms, rotated))
     terms = jnp.sum(terms, axis=0)
     whole = lax.all_to_all(
         jnp.broadcast_to(terms[None], (BLOCKS, 1, 8 * BLOCKS)), "dom", 0, 0, tiled=True
@@ -347,10 +370,6 @@
     whole = whole.reshape(2, 2, 2, BLOCKS, BLOCKS)
     whole = jnp.where(core == 0, whole, whole[:, :, ::-1])
     whole = whole.reshape(2, 4 * BLOCKS, BLOCKS)
-    rotated_near = rotate(rotation_near)
-    lower = jnp.where(z_hi == 0, rotated_near, rotated_far)
-    upper = jnp.where(z_hi == 0, rotated_far, rotated_near)
-    rotated = jnp.concatenate([lower, upper], axis=0).reshape(1, BX, BY, BZ, width)
     return (rotated, whole[0], whole[1])
 
 

time: 214 us -> 216 us (level)
  blocking collectives: 69.1 us -> 75.9 us
  starting transfers between devices: 53.9 us -> 49.6 us
  waiting for transfers between devices: 63.3 us -> 59.3 us
    all_to_all x1 -> x0, waiting for transfers between devices: 14.9 us -> none  [local(): lax.all_to_all(jnp.broadcast_to(terms[None], (BLOCKS, 1, 8 * BLOCKS)), 'd...]
    all_to_all x1 -> x2, waiting for transfers between devices: 38.5 us -> 49.2 us  [exchange(): lax.all_to_all(x, ('band', 'dom'), 0, 0, tiled=True, axis_index_groups=gr...]
    all_to_all x1 -> x0, starting transfers between devices: 9.4 us -> none  [local(): lax.all_to_all(jnp.broadcast_to(terms[None], (BLOCKS, 1, 8 * BLOCKS)), 'd...]
    all_to_all x1, blocking collectives: 20.3 us -> 26.8 us  [local(): lax.all_to_all(jnp.broadcast_to(terms[None], (BLOCKS, 1, 8 * BLOCKS)), 'd...]
    all_to_all x1 -> x2, starting transfers between devices: 12.8 us -> 19.3 us  [exchange(): lax.all_to_all(x, ('band', 'dom'), 0, 0, tiled=True, axis_index_groups=gr...]
    pallas_call x1, Pallas kernels: 0.32 us -> 2.49 us  [packed(): pl.pallas_call(pack_kernel, out_shape=jax.ShapeDtypeStruct((BLOCKS * SENT...]
  transfers between devices with their start and end apart: 9 -> 9, of which waited for: 5 -> 5; matrix products, arithmetic and copies ran while one was open for 2% -> 3% of each run, Pallas kernels for 6% -> 6%
where the time goes in v7:
time: 216 us; the launch traced here: 213 us
  blocking collectives  75.9 us (35%)
  waiting for transfers between devices  59.3 us (27%)
  starting transfers between devices  49.6 us (23%)
  Pallas kernels  15.2 us (7%)
  matrix products  4.89 us (2%)
  local copies, waits for them, and re-layouts  4.72 us (2%)
  other arithmetic  2.46 us (1%)
    all_to_all x2, waiting for transfers between devices, exchange(): lax.all_to_all(x, ('band', 'dom'), 0, 0, tiled=True, axis_index_groups=gr...  49.2 us
    all_to_all x1, blocking collectives, local(): lax.all_to_all(sent.reshape(BLOCKS, 1, SENT * LANES), 'dom', 0, 0, tiled=...  49.1 us
    all_to_all x1, blocking collectives, local(): lax.all_to_all(jnp.broadcast_to(terms[None], (BLOCKS, 1, 8 * BLOCKS)), 'd...  26.8 us
    all_to_all x2, starting transfers between devices, exchange(): lax.all_to_all(x, ('band', 'dom'), 0, 0, tiled=True, axis_index_groups=gr...  19.3 us
    ppermute x3, waiting for transfers between devices, local(): pieces[k] = lax.ppermute(pieces[k], 'dom', pairs)  10.1 us
    pallas_call x1, Pallas kernels, filtered_fields(): pl.pallas_call(filter_kernel, out_shape=jax.ShapeDtypeStruct((BLOCKS * 2...  9.97 us
    ppermute x3, starting transfers between devices, local(): pieces[k] = lax.ppermute(pieces[k], 'dom', pairs)  8.5 us
    ppermute x1, starting transfers between devices, local(): rotation_far = lax.ppermute(rotation_near, ('band', 'dom'), Z_MIRROR)  6.54 us
  transfers between devices with their start and end apart: 9, of which 5 were waited for; matrix products, arithmetic and copies ran while one was open for 3% of the time, Pallas kernels for 6%

profile of v7, /device:TPU:1, one launch (start us, length us, event | category | flops | bytes accessed | tf_op | source)
XLA Modules:
  0.0 213.0 jit_solution(4446851024403757945)
XLA Ops:
  0.6 1.4 copy.21
  2.1 2.5 %shard_map.67 = f32[2304,128]{1,0:T(8,128)} custom-call(s32[1]{0:T(128)} %bitcast.core_ref, f32[1536,128]{1,0:T(8,128)} %bitcast.57, f32[8,12,16]{2,1,0:T(8,128)} %bitcast.61), custom_call_target="tpu_custom_call" | custom-call | tf_op jit(solution)/shard_map/pallas_call | solution.py:84
  4.6 49.1 %all_to_all.20 = f32[128,1,2304]{2,1,0:T(1,128)S(1)} all-to-all(f32[128,1,2304]{2,1,0:T(1,128)} %bitcast.50), channel_id=1, replica_groups={{0,32,64,96,8,40,72,104,16,48,80,112,24,56,88,120,1,33,65,97,9,41,73,10..., dimensions={0} | all-to-all | bytes 2359296 | tf_op jit(solution)/shard_map/all_to_all | solution.py:315
  53.8 4.8 %collective-permute-start = (f32[128,1,768]{2,1,0:T(1,128)S(1)}, f32[128,1,768]{2,1,0:T(1,128)S(1)}, u32[]{:S(2)}, u32[]{:S(2)}) collective-permute-start(f32[128,1,768]{2,1,0:T(1,128)S(1)} %slice.29), channel_id=1, source_target_pairs={{0,128},{128,0},{256,384},{384,256},{1,129},{129,1},{257,385},{385... | collective-permute-start | bytes 1179656 | tf_op jit(solution)/shard_map/ppermute | solution.py:320
  58.5 6.5 %collective-permute-start.1 = (f32[512,128]{1,0:T(8,128)S(1)}, f32[512,128]{1,0:T(8,128)S(1)}, u32[]{:S(2)}, u32[]{:S(2)}) collective-permute-start(f32[512,128]{1,0:T(8,128)S(1)} %copy-done.1), channel_id=1, source_target_pairs={{0,259},{1,258},{2,257},{3,256},{4,263},{5,262},{6,261},{7,260},{8... | collective-permute-start | bytes 786440 | tf_op jit(solution)/shard_map/ppermute | solution.py:319
  65.1 2.5 %shard_map.68 = (f32[8,12,16,128]{3,2,1,0:T(8,128)S(1)}, f32[8,12,16,128]{3,2,1,0:T(8,128)S(1)}, f32[8,6,16,128]{3,2,1,0:T(8,128)S(1)}) custom-call(f32[2304,128]{1,0:T(8,128)S(1)} %bitcast.47), custom_call_target="tpu_custom_call" | custom-call | flops 20000000 | bytes 20000000 | tf_op jit(solution)/shard_map/pallas_call | solution.py:265
  67.6 10.0 %shard_map.69 = f32[3072,128]{1,0:T(8,128)} custom-call(s32[1]{0:T(128)} %bitcast.core_ref, f32[3]{0:T(128)S(1)} %copy-done, f32[8,12,16,128]{3,2,1,0:T(8,128)S(1)} %get-tuple-element.24.x_ref, f32[8,12,16,128]{3,2,1,0:T(8,128)S(1)} %get-tuple-element.25.lap_ref, f32[8,6,16,128]{3,2,1,0:T(8,128)S(1)} %get-tuple-element.26.pot_own_ref, f32[768,128]{1,0:T(8,128)S(1)} %bitcast.49), custom_call_target="tpu_custom_call" | custom-call | flops 60000000 | bytes 40000000 | tf_op jit(solution)/shard_map/pallas_call | solution.py:282
  77.5 12.2 %all-to-all-start.1 = ((f32[256,1,1536]{2,1,0:T(1,128)}), f32[256,1,1536]{2,1,0:T(1,128)S(1)}, u32[]{:S(2)}, u32[]{:S(2)}) async-start(f32[256,1,1536]{2,1,0:T(1,128)} %bitcast.6), calls=%async_computation.1 | async-start | bytes 3145728 | tf_op jit(solution)/shard_map/all_to_all | solution.py:59
  89.7 38.4 %all-to-all-done.1 = f32[256,1,1536]{2,1,0:T(1,128)S(1)} async-done(((f32[256,1,1536]{2,1,0:T(1,128)}), f32[256,1,1536]{2,1,0:T(1,128)S(1)}, u32[]{:S(2)}, u32[]{:S(2)}) %all-to-all-start.1) | async-done | bytes 1572896 | tf_op jit(solution)/shard_map/all_to_all | solution.py:59
  128.5 5.4 %collective-permute-start.2 = (f32[256,768]{1,0:T(8,128)S(1)}, f32[256,768]{1,0:T(8,128)S(1)}, u32[]{:S(2)}, u32[]{:S(2)}) collective-permute-start(f32[256,768]{1,0:T(8,128)S(1)} %get-tuple-element.31), channel_id=1, source_target_pairs={{0,128},{128,0},{256,384},{384,256},{1,129},{129,1},{257,385},{385... | collective-permute-start | bytes 2359304 | tf_op jit(solution)/shard_map/ppermute | solution.py:330
  136.4 5.2 %collective-permute-start.6 = (f32[768,128]{1,0:T(8,128)S(1)}, f32[768,128]{1,0:T(8,128)S(1)}, u32[]{:S(2)}, u32[]{:S(2)}) collective-permute-start(f32[768,128]{1,0:T(8,128)S(1)} %convolution_add_fusion.1), channel_id=1, source_target_pairs={{0,256},{256,0},{128,384},{384,128},{1,257},{257,1},{129,385},{385... | collective-permute-start | bytes 1179656 | tf_op jit(solution)/shard_map/ppermute | solution.py:345
  142.5 0.9 dynamic-slice_bitcast_fusion
  143.4 2.3 %collective-permute-start.3 = (f32[128,512]{1,0:T(8,128)}, f32[128,512]{1,0:T(8,128)}, u32[]{:S(2)}, u32[]{:S(2)}) collective-permute-start(f32[128,512]{1,0:T(8,128)} %get-tuple-element.45), channel_id=1, source_target_pairs={{0,4},{1,5},{2,6},{3,7},{4,8},{5,9},{6,10},{7,11},{8,12},{9,13},{1... | collective-permute-start | bytes 786440 | tf_op jit(solution)/shard_map/ppermute | solution.py:354
  145.7 3.6 %collective-permute-start.4 = (f32[128,512]{1,0:T(8,128)}, f32[128,512]{1,0:T(8,128)}, u32[]{:S(2)}, u32[]{:S(2)}) collective-permute-start(f32[128,512]{1,0:T(8,128)} %get-tuple-element.44), channel_id=1, source_target_pairs={{0,8},{1,9},{2,10},{3,11},{4,12},{5,13},{6,14},{7,15},{8,0},{9,1},... | collective-permute-start | bytes 786440 | tf_op jit(solution)/shard_map/ppermute | solution.py:354
  149.3 2.6 %collective-permute-start.5 = (f32[128,512]{1,0:T(8,128)S(1)}, f32[128,512]{1,0:T(8,128)}, u32[]{:S(2)}, u32[]{:S(2)}) collective-permute-start(f32[128,512]{1,0:T(8,128)S(1)} %get-tuple-element.43), channel_id=1, source_target_pairs={{0,12},{1,13},{2,14},{3,15},{4,0},{5,1},{6,2},{7,3},{8,4},{9,5},{1... | collective-permute-start | bytes 786440 | tf_op jit(solution)/shard_map/ppermute | solution.py:354
  152.0 2.7 %collective-permute-done.3 = f32[128,512]{1,0:T(8,128)} collective-permute-done((f32[128,512]{1,0:T(8,128)}, f32[128,512]{1,0:T(8,128)}, u32[]{:S(2)}, u32[]{:S(2)}) %collective-permute-start.3) | collective-permute-done | bytes 262176 | tf_op jit(solution)/shard_map/ppermute | solution.py:354
  154.7 4.4 %collective-permute-done.4 = f32[128,512]{1,0:T(8,128)} collective-permute-done((f32[128,512]{1,0:T(8,128)}, f32[128,512]{1,0:T(8,128)}, u32[]{:S(2)}, u32[]{:S(2)}) %collective-permute-start.4) | collective-permute-done | bytes 262176 | tf_op jit(solution)/shard_map/ppermute | solution.py:354
  159.1 2.9 %collective-permute-done.5 = f32[128,512]{1,0:T(8,128)} collective-permute-done((f32[128,512]{1,0:T(8,128)S(1)}, f32[128,512]{1,0:T(8,128)}, u32[]{:S(2)}, u32[]{:S(2)}) %collective-permute-start.5) | collective-permute-done | bytes 262176 | tf_op jit(solution)/shard_map/ppermute | solution.py:354
  162.0 1.2 add_add_fusion
  163.4 0.8 copy.17
  164.2 7.1 %all-to-all-start.2 = ((f32[64,1,1024]{2,1,0:T(1,128)}), f32[64,1,1024]{2,1,0:T(1,128)S(1)}, u32[]{:S(2)}, u32[]{:S(2)}) async-start(f32[64,1,1024]{2,1,0:T(1,128)} %bitcast.21), calls=%async_computation.2 | async-start | bytes 524288 | tf_op jit(solution)/shard_map/all_to_all | solution.py:59
  173.0 0.9 pad_maximum_fusion.1
  173.9 10.8 %all-to-all-done.2 = f32[64,1,1024]{2,1,0:T(1,128)S(1)} async-done(((f32[64,1,1024]{2,1,0:T(1,128)}), f32[64,1,1024]{2,1,0:T(1,128)S(1)}, u32[]{:S(2)}, u32[]{:S(2)}) %all-to-all-start.2) | async-done | bytes 262176 | tf_op jit(solution)/shard_map/all_to_all | solution.py:59
  185.2 26.8 %all_to_all.21 = f32[128,1,1024]{2,1,0:T(1,128)S(1)} all-to-all(f32[128,1,1024]{2,1,0:T(1,128)S(1)} %broadcast_in_dim.2), channel_id=1, replica_groups=mesh['band'=4,'dom'=128] {'dom'}, dimensions={0} | all-to-all | bytes 1048576 | tf_op jit(solution)/shard_map/all_to_all | solution.py:366
  (26 shorter events, 7.1 us)
Async XLA Ops:
  4.6 54.0 %copy-start.1 = (f32[512,128]{1,0:T(8,128)S(1)}, f32[512,128]{1,0:T(8,128)}, u32[]{:S(2)}) copy-start(f32[512,128]{1,0:T(8,128)} %param.7) | copy-start | bytes 786436
  53.7 13.9 %copy-start = (f32[3]{0:T(128)S(1)}, f32[3]{0:T(128)}, u32[]{:S(2)}) copy-start(f32[3]{0:T(128)} %bounds_ref.1) | copy-start | bytes 40
  53.8 13.8 %collective-permute-start = (f32[128,1,768]{2,1,0:T(1,128)S(1)}, f32[128,1,768]{2,1,0:T(1,128)S(1)}, u32[]{:S(2)}, u32[]{:S(2)}) collective-permute-start(f32[128,1,768]{2,1,0:T(1,128)S(1)} %slice.29), channel_id=1, source_target_pairs={{0,128},{128,0},{256,384},{384,256},{1,129},{129,1},{257,385},{385... | collective-permute-start | bytes 1179656 | tf_op jit(solution)/shard_map/ppermute | solution.py:320
  58.5 19.0 %collective-permute-start.1 = (f32[512,128]{1,0:T(8,128)S(1)}, f32[512,128]{1,0:T(8,128)S(1)}, u32[]{:S(2)}, u32[]{:S(2)}) collective-permute-start(f32[512,128]{1,0:T(8,128)S(1)} %copy-done.1), channel_id=1, source_target_pairs={{0,259},{1,258},{2,257},{3,256},{4,263},{5,262},{6,261},{7,260},{8... | collective-permute-start | bytes 786440 | tf_op jit(solution)/shard_map/ppermute | solution.py:319
  77.5 50.6 %all-to-all-start.1 = ((f32[256,1,1536]{2,1,0:T(1,128)}), f32[256,1,1536]{2,1,0:T(1,128)S(1)}, u32[]{:S(2)}, u32[]{:S(2)}) async-start(f32[256,1,1536]{2,1,0:T(1,128)} %bitcast.6), calls=%async_computation.1 | async-start | bytes 3145728 | tf_op jit(solution)/shard_map/all_to_all | solution.py:59
  128.5 7.1 %collective-permute-start.2 = (f32[256,768]{1,0:T(8,128)S(1)}, f32[256,768]{1,0:T(8,128)S(1)}, u32[]{:S(2)}, u32[]{:S(2)}) collective-permute-start(f32[256,768]{1,0:T(8,128)S(1)} %get-tuple-element.31), channel_id=1, source_target_pairs={{0,128},{128,0},{256,384},{384,256},{1,129},{129,1},{257,385},{385... | collective-permute-start | bytes 2359304 | tf_op jit(solution)/shard_map/ppermute | solution.py:330
  136.4 25.6 %collective-permute-start.6 = (f32[768,128]{1,0:T(8,128)S(1)}, f32[768,128]{1,0:T(8,128)S(1)}, u32[]{:S(2)}, u32[]{:S(2)}) collective-permute-start(f32[768,128]{1,0:T(8,128)S(1)} %convolution_add_fusion.1), channel_id=1, source_target_pairs={{0,256},{256,0},{128,384},{384,128},{1,257},{257,1},{129,385},{385... | collective-permute-start | bytes 1179656 | tf_op jit(solution)/shard_map/ppermute | solution.py:345
  143.4 11.3 %collective-permute-start.3 = (f32[128,512]{1,0:T(8,128)}, f32[128,512]{1,0:T(8,128)}, u32[]{:S(2)}, u32[]{:S(2)}) collective-permute-start(f32[128,512]{1,0:T(8,128)} %get-tuple-element.45), channel_id=1, source_target_pairs={{0,4},{1,5},{2,6},{3,7},{4,8},{5,9},{6,10},{7,11},{8,12},{9,13},{1... | collective-permute-start | bytes 786440 | tf_op jit(solution)/shard_map/ppermute | solution.py:354
  145.7 13.4 %collective-permute-start.4 = (f32[128,512]{1,0:T(8,128)}, f32[128,512]{1,0:T(8,128)}, u32[]{:S(2)}, u32[]{:S(2)}) collective-permute-start(f32[128,512]{1,0:T(8,128)} %get-tuple-element.44), channel_id=1, source_target_pairs={{0,8},{1,9},{2,10},{3,11},{4,12},{5,13},{6,14},{7,15},{8,0},{9,1},... | collective-permute-start | bytes 786440 | tf_op jit(solution)/shard_map/ppermute | solution.py:354
  149.3 12.7 %collective-permute-start.5 = (f32[128,512]{1,0:T(8,128)S(1)}, f32[128,512]{1,0:T(8,128)}, u32[]{:S(2)}, u32[]{:S(2)}) collective-permute-start(f32[128,512]{1,0:T(8,128)S(1)} %get-tuple-element.43), channel_id=1, source_target_pairs={{0,12},{1,13},{2,14},{3,15},{4,0},{5,1},{6,2},{7,3},{8,4},{9,5},{1... | collective-permute-start | bytes 786440 | tf_op jit(solution)/shard_map/ppermute | solution.py:354
  164.2 20.5 %all-to-all-start.2 = ((f32[64,1,1024]{2,1,0:T(1,128)}), f32[64,1,1024]{2,1,0:T(1,128)S(1)}, u32[]{:S(2)}, u32[]{:S(2)}) async-start(f32[64,1,1024]{2,1,0:T(1,128)} %bitcast.21), calls=%async_computation.2 | async-start | bytes 524288 | tf_op jit(solution)/shard_map/all_to_all | solution.py:59

commit v8 on v6

--- a/solution.py
+++ b/solution.py
@@ -46,6 +46,13 @@
 ]
 CORE_SWAP = [(0, 1), (1, 0), (2, 3), (3, 2)]
 Z_SWAP = [(0, 2), (2, 0), (1, 3), (3, 1)]
+Z_MIRROR = [
+    (flat(b, chip(y, x, z)), flat(b ^ 2, chip(y, x, 3 - z)))
+    for b in range(4)
+    for y in range(8)
+    for x in range(4)
+    for z in range(4)
+]
 
 
 def exchange(x, groups):
@@ -169,7 +176,7 @@
             lap_ref[i, y0 : y0 + YS] = laplace(ext, i, y0)
         return carry
 
-    lax.fori_loop(0, BX, body, 0)
+    lax.fori_loop(0, BX, body, 0, unroll=True)
 
 
 def filter_coefficients(bounds_ref):
@@ -222,13 +229,13 @@
             img[i, y0 : y0 + YS] = KINETIC * laplace(eb, i, y0) + pot[i, y0 : y0 + YS] * centre
         return carry
 
-    lax.fori_loop(0, BX, first, 0)
+    lax.fori_loop(0, BX, first, 0, unroll=True)
     margins(eb)
-    lax.fori_loop(0, BX, next_field, 0)
+    lax.fori_loop(0, BX, next_field, 0, unroll=True)
     margins(ea)
-    squares = lax.fori_loop(0, BX, last_field, jnp.zeros((BZ, LANES), jnp.float32))
+    squares = lax.fori_loop(0, BX, last_field, jnp.zeros((BZ, LANES), jnp.float32), unroll=True)
     margins(eb)
-    lax.fori_loop(0, BX, image_field, 0)
+    lax.fori_loop(0, BX, image_field, 0, unroll=True)
     norm = jnp.sqrt(jnp.sum(squares, keepdims=True))
     for q in range(TILES):
         rows = [q * (LANES // BZ) + r for r in range(LANES // BZ)]
@@ -255,7 +262,7 @@
         out_specs=(vmem, vmem, vmem),
         scratch_shapes=[pltpu.VMEM(EXT, jnp.float32)],
         compiler_params=pltpu.CompilerParams(vmem_limit_bytes=24 * 1024 * 1024),
-        cost_estimate=pl.CostEstimate(flops=20_000_000, bytes_accessed=20_000_000, transcendentals=0),
+        cost_estimate=pl.CostEstimate(flops=20_000_000, bytes_accessed=150_000_000, transcendentals=0),
     )(got)
 
 
@@ -298,16 +305,21 @@
         sent.reshape(BLOCKS, 1, SENT * LANES), "dom", 0, 0, tiled=True, axis_index_groups=[ORDER]
     )
     got, rotation_near = lax.optimization_barrier((got, rotation))
-    rotation_far = lax.ppermute(rotation_near, "band", Z_SWAP)
+    rotation_far = lax.ppermute(rotation_near, ("band", "dom"), Z_MIRROR)
     v_other = lax.ppermute(got[:, :, CELLS:], "band", CORE_SWAP)
     x, lap, pot_own = first_laplace(got.reshape(BLOCKS * SENT, LANES))
     images = filtered_fields(
         here, bounds, x, lap, pot_own, v_other.reshape(BLOCKS * HALF_TILES, LANES)
     )
 
-    images, rotation_far = lax.optimization_barrier((images, rotation_far))
+    spot = lax.axis_index("dom")
+    images, rotation_far, spot, core, z_hi = lax.optimization_barrier(
+        (images, rotation_far, spot, core, z_hi)
+    )
     got = exchange(images.reshape(2 * BLOCKS, 1, CELLS), CORE_GROUPS)
-    got, rotation_near, rotation_far = lax.optimization_barrier((got, rotation_near, rotation_far))
+    got, rotation_near, rotation_far, spot, core, z_hi = lax.optimization_barrier(
+        (got, rotation_near, rotation_far, spot, core, z_hi)
+    )
     phi, both = split_fields(got.reshape(2 * BLOCKS * TILES, LANES))
     phi_other = lax.ppermute(phi, "band", CORE_SWAP)
     gram = jnp.concatenate(
@@ -328,12 +340,10 @@
     rotated_far = lax.ppermute(rotate(rotation_far), "band", Z_SWAP)
 
     gram = gram.reshape(4, BLOCKS, 4 * BLOCKS)
-    place = (lax.axis_index("dom") >> 2) & 3
-    pieces = [lax.dynamic_index_in_dim(gram, (place + k) & 3, 0, keepdims=False) for k in range(4)]
+    place = ((spot >> 2) & 3).astype(jnp.uint32)
+    pieces = [lax.dynamic_index_in_dim(gram, place ^ k, 0, keepdims=False) for k in range(4)]
     for k in (2, 1, 3):
-        pairs = [
-            (chip(y, x, z), chip(y, (x + k) % 4, z)) for y in range(8) for x in range(4) for z in range(4)
-        ]
+        pairs = [(chip(y, x, z), chip(y, x ^ k, z)) for y in range(8) for x in range(4) for z in range(4)]
         pieces[k] = lax.ppermute(pieces[k], "dom", pairs)
     terms, rotated_far = lax.optimization_barrier((pieces, rotated_far))
     terms = (terms[0] + terms[1]) + (terms[2] + terms[3])

time: 214 us -> 215 us (level)
  blocking collectives: 69.1 us -> 122 us
  waiting for transfers between devices: 63.3 us -> 28.8 us
  starting transfers between devices: 53.9 us -> 37.5 us
  Pallas kernels: 13.1 us -> 10.2 us
    all_to_all x1 -> x2, blocking collectives: 20.3 us -> 72.7 us  [exchange(): lax.all_to_all(x, ('band', 'dom'), 0, 0, tiled=True, axis_index_groups=gr...]
    all_to_all x1 -> x0, waiting for transfers between devices: 38.5 us -> none  [exchange(): lax.all_to_all(x, ('band', 'dom'), 0, 0, tiled=True, axis_index_groups=gr...]
    all_to_all x1 -> x0, starting transfers between devices: 12.8 us -> none  [exchange(): lax.all_to_all(x, ('band', 'dom'), 0, 0, tiled=True, axis_index_groups=gr...]
    all_to_all x1, starting transfers between devices: 9.4 us -> 6.3 us  [local(): lax.all_to_all(jnp.broadcast_to(terms[None], (BLOCKS, 1, 8 * BLOCKS)), 'd...]
    ppermute x1, waiting for transfers between devices: 0.01 us -> 2.7 us  [local(): rotation_far = lax.ppermute(rotation_near, ('band', 'dom'), Z_MIRROR)]
    pallas_call x1, Pallas kernels: 9.98 us -> 7.41 us  [filtered_fields(): pl.pallas_call(filter_kernel, out_shape=jax.ShapeDtypeStruct((BLOCKS * 2...]
    ppermute x3, waiting for transfers between devices: 9.88 us -> 12.3 us  [local(): pieces[k] = lax.ppermute(pieces[k], 'dom', pairs)]
  transfers between devices with their start and end apart: 9 -> 8, of which waited for: 5 -> 4; matrix products, arithmetic and copies ran while one was open for 2% -> 3% of each run, Pallas kernels for 6% -> 5%
where the time goes in v8:
time: 215 us; the launch traced here: 212 us
  blocking collectives  122 us (57%)
  starting transfers between devices  37.5 us (17%)
  waiting for transfers between devices  28.8 us (13%)
  Pallas kernels  10.2 us (5%)
  local copies, waits for them, and re-layouts  5.26 us (2%)
  matrix products  4.89 us (2%)
  other arithmetic  2.57 us (1%)
    all_to_all x2, blocking collectives, exchange(): lax.all_to_all(x, ('band', 'dom'), 0, 0, tiled=True, axis_index_groups=gr...  72.7 us
    all_to_all x1, blocking collectives, local(): lax.all_to_all(sent.reshape(BLOCKS, 1, SENT * LANES), 'dom', 0, 0, tiled=...  48.9 us
    all_to_all x1, waiting for transfers between devices, local(): lax.all_to_all(jnp.broadcast_to(terms[None], (BLOCKS, 1, 8 * BLOCKS)), 'd...  13.7 us
    ppermute x3, waiting for transfers between devices, local(): pieces[k] = lax.ppermute(pieces[k], 'dom', pairs)  12.3 us
    ppermute x3, starting transfers between devices, local(): pieces[k] = lax.ppermute(pieces[k], 'dom', pairs)  9.58 us
    pallas_call x1, Pallas kernels, filtered_fields(): pl.pallas_call(filter_kernel, out_shape=jax.ShapeDtypeStruct((BLOCKS * 2...  7.41 us
    ppermute x1, starting transfers between devices, local(): rotation_far = lax.ppermute(rotation_near, ('band', 'dom'), Z_MIRROR)  6.54 us
    all_to_all x1, starting transfers between devices, local(): lax.all_to_all(jnp.broadcast_to(terms[None], (BLOCKS, 1, 8 * BLOCKS)), 'd...  6.3 us
  transfers between devices with their start and end apart: 8, of which 4 were waited for; matrix products, arithmetic and copies ran while one was open for 3% of the time, Pallas kernels for 5%

profile of v8, /device:TPU:1, one launch (start us, length us, event | category | flops | bytes accessed | tf_op | source)
XLA Modules:
  0.0 211.7 jit_solution(11211586819848349825)
XLA Ops:
  1.5 1.1 copy-done
  2.9 48.9 %all_to_all.20 = f32[128,1,2304]{2,1,0:T(1,128)S(1)} all-to-all(f32[128,1,2304]{2,1,0:T(1,128)S(1)} %bitcast.53), channel_id=1, replica_groups={{0,32,64,96,8,40,72,104,16,48,80,112,24,56,88,120,1,33,65,97,9,41,73,10..., dimensions={0} | all-to-all | bytes 2359296 | tf_op jit(solution)/shard_map/all_to_all | solution.py:304
  51.9 4.8 %collective-permute-start = (f32[128,1,768]{2,1,0:T(1,128)S(1)}, f32[128,1,768]{2,1,0:T(1,128)S(1)}, u32[]{:S(2)}, u32[]{:S(2)}) collective-permute-start(f32[128,1,768]{2,1,0:T(1,128)S(1)} %slice.35), channel_id=1, source_target_pairs={{0,128},{128,0},{256,384},{384,256},{1,129},{129,1},{257,385},{385... | collective-permute-start | bytes 1179656 | tf_op jit(solution)/shard_map/ppermute | solution.py:309
  56.7 6.5 %collective-permute-start.1 = (f32[512,128]{1,0:T(8,128)S(1)}, f32[512,128]{1,0:T(8,128)S(1)}, u32[]{:S(2)}, u32[]{:S(2)}) collective-permute-start(f32[512,128]{1,0:T(8,128)S(1)} %copy-done.4), channel_id=1, source_target_pairs={{0,259},{1,258},{2,257},{3,256},{4,263},{5,262},{6,261},{7,260},{8... | collective-permute-start | bytes 786440 | tf_op jit(solution)/shard_map/ppermute | solution.py:308
  63.2 2.1 %shard_map.68 = (f32[8,12,16,128]{3,2,1,0:T(8,128)S(1)}, f32[8,12,16,128]{3,2,1,0:T(8,128)S(1)}, f32[8,6,16,128]{3,2,1,0:T(8,128)S(1)}) custom-call(f32[2304,128]{1,0:T(8,128)S(1)} %bitcast.50), custom_call_target="tpu_custom_call" | custom-call | flops 20000000 | bytes 150000000 | tf_op jit(solution)/shard_map/pallas_call | solution.py:254
  65.4 7.4 %shard_map.69 = f32[3072,128]{1,0:T(8,128)S(1)} custom-call(s32[1]{0:T(128)} %bitcast.core_ref, f32[3]{0:T(128)S(1)} %copy-done.1, f32[8,12,16,128]{3,2,1,0:T(8,128)S(1)} %get-tuple-element.27.x_ref, f32[8,12,16,128]{3,2,1,0:T(8,128)S(1)} %get-tuple-element.28.lap_ref, f32[8,6,16,128]{3,2,1,0:T(8,128)S(1)} %get-tuple-element.29.pot_own_ref, ...), custom_call_target="tpu_custom_call" | custom-call | flops 60000000 | bytes 40000000 | tf_op jit(solution)/shard_map/pallas_call | solution.py:271
  72.8 2.7 %collective-permute-done.1 = f32[512,128]{1,0:T(8,128)S(1)} collective-permute-done((f32[512,128]{1,0:T(8,128)S(1)}, f32[512,128]{1,0:T(8,128)S(1)}, u32[]{:S(2)}, u32[]{:S(2)}) %collective-permute-start.1) | collective-permute-done | bytes 262176 | tf_op jit(solution)/shard_map/ppermute | solution.py:308
  75.5 50.8 %all_to_all.21 = f32[256,1,1536]{2,1,0:T(1,128)S(1)} all-to-all(f32[256,1,1536]{2,1,0:T(1,128)S(1)} %bitcast.51), channel_id=1, replica_groups={{0,256,32,288,64,320,96,352,8,264,40,296,72,328,104,360,16,272,48,304,8..., dimensions={0} | all-to-all | bytes 3145728 | tf_op jit(solution)/shard_map/all_to_all | solution.py:59
  126.6 5.2 %collective-permute-start.2 = (f32[256,768]{1,0:T(8,128)S(1)}, f32[256,768]{1,0:T(8,128)S(1)}, u32[]{:S(2)}, u32[]{:S(2)}) collective-permute-start(f32[256,768]{1,0:T(8,128)S(1)} %get-tuple-element.38), channel_id=1, source_target_pairs={{0,128},{128,0},{256,384},{384,256},{1,129},{129,1},{257,385},{385... | collective-permute-start | bytes 2359304 | tf_op jit(solution)/shard_map/ppermute | solution.py:324
  131.8 1.2 fusion
  133.9 0.8 fusion.6
  135.6 5.2 %collective-permute-start.6 = (f32[768,128]{1,0:T(8,128)S(1)}, f32[768,128]{1,0:T(8,128)S(1)}, u32[]{:S(2)}, u32[]{:S(2)}) collective-permute-start(f32[768,128]{1,0:T(8,128)S(1)} %convolution_add_fusion), channel_id=1, source_target_pairs={{0,256},{256,0},{128,384},{384,128},{1,257},{257,1},{129,385},{385... | collective-permute-start | bytes 1179656 | tf_op jit(solution)/shard_map/ppermute | solution.py:340
  140.7 0.8 fusion.7
  141.7 2.3 %collective-permute-start.3 = (f32[128,512]{1,0:T(8,128)S(1)}, f32[128,512]{1,0:T(8,128)S(1)}, u32[]{:S(2)}, u32[]{:S(2)}) collective-permute-start(f32[128,512]{1,0:T(8,128)S(1)} %get-tuple-element.51), channel_id=1, source_target_pairs={{0,4},{1,5},{2,6},{3,7},{4,0},{5,1},{6,2},{7,3},{8,12},{9,13},{10,... | collective-permute-start | bytes 786440 | tf_op jit(solution)/shard_map/ppermute | solution.py:347
  144.0 3.6 %collective-permute-start.4 = (f32[128,512]{1,0:T(8,128)S(1)}, f32[128,512]{1,0:T(8,128)S(1)}, u32[]{:S(2)}, u32[]{:S(2)}) collective-permute-start(f32[128,512]{1,0:T(8,128)S(1)} %get-tuple-element.50), channel_id=1, source_target_pairs={{0,8},{1,9},{2,10},{3,11},{4,12},{5,13},{6,14},{7,15},{8,0},{9,1},... | collective-permute-start | bytes 786440 | tf_op jit(solution)/shard_map/ppermute | solution.py:347
  147.6 3.7 %collective-permute-start.5 = (f32[128,512]{1,0:T(8,128)S(1)}, f32[128,512]{1,0:T(8,128)S(1)}, u32[]{:S(2)}, u32[]{:S(2)}) collective-permute-start(f32[128,512]{1,0:T(8,128)S(1)} %get-tuple-element.49), channel_id=1, source_target_pairs={{0,12},{1,13},{2,14},{3,15},{4,8},{5,9},{6,10},{7,11},{8,4},{9,5},... | collective-permute-start | bytes 786440 | tf_op jit(solution)/shard_map/ppermute | solution.py:347
  151.3 6.1 %collective-permute-done.4 = f32[128,512]{1,0:T(8,128)S(1)} collective-permute-done((f32[128,512]{1,0:T(8,128)S(1)}, f32[128,512]{1,0:T(8,128)S(1)}, u32[]{:S(2)}, u32[]{:S(2)}) %collective-permute-start.4) | collective-permute-done | bytes 262176 | tf_op jit(solution)/shard_map/ppermute | solution.py:347
  157.5 6.2 %collective-permute-done.5 = f32[128,512]{1,0:T(8,128)S(1)} collective-permute-done((f32[128,512]{1,0:T(8,128)S(1)}, f32[128,512]{1,0:T(8,128)S(1)}, u32[]{:S(2)}, u32[]{:S(2)}) %collective-permute-start.5) | collective-permute-done | bytes 262176 | tf_op jit(solution)/shard_map/ppermute | solution.py:347
  164.8 22.0 %all_to_all.22 = f32[64,1,1024]{2,1,0:T(1,128)S(1)} all-to-all(f32[64,1,1024]{2,1,0:T(1,128)S(1)} %bitcast.61), channel_id=1, replica_groups={{0,256,1,257,2,258,3,259,16,272,17,273,18,274,19,275,32,288,33,289,34,2..., dimensions={0} | all-to-all | bytes 524288 | tf_op jit(solution)/shard_map/all_to_all | solution.py:59
  187.0 1.1 broadcast_in_dim.2
  188.1 6.3 %all-to-all-start.3 = ((f32[128,1,1024]{2,1,0:T(1,128)}), f32[128,1,1024]{2,1,0:T(1,128)S(1)}, u32[]{:S(2)}, u32[]{:S(2)}) async-start(f32[128,1,1024]{2,1,0:T(1,128)} %broadcast_in_dim.2), calls=%async_computation.3 | async-start | bytes 1048576 | tf_op jit(solution)/shard_map/all_to_all | solution.py:353
  196.0 0.9 pad_maximum_fusion.1
  197.0 13.7 %all-to-all-done.3 = f32[128,1,1024]{2,1,0:T(1,128)S(1)} async-done(((f32[128,1,1024]{2,1,0:T(1,128)}), f32[128,1,1024]{2,1,0:T(1,128)S(1)}, u32[]{:S(2)}, u32[]{:S(2)}) %all-to-all-start.3) | async-done | bytes 524320 | tf_op jit(solution)/shard_map/all_to_all | solution.py:353
  210.9 0.8 fusion.2
  (33 shorter events, 6.5 us)
Async XLA Ops:
  1.5 1.1 copy-start
  2.9 53.7 %copy-start.4 = (f32[512,128]{1,0:T(8,128)S(1)}, f32[512,128]{1,0:T(8,128)}, u32[]{:S(2)}) copy-start(f32[512,128]{1,0:T(8,128)} %param.7) | copy-start | bytes 786436
  51.8 13.6 %copy-start.1 = (f32[3]{0:T(128)S(1)}, f32[3]{0:T(128)}, u32[]{:S(2)}) copy-start(f32[3]{0:T(128)} %bounds_ref.1) | copy-start | bytes 40
  51.9 13.5 %collective-permute-start = (f32[128,1,768]{2,1,0:T(1,128)S(1)}, f32[128,1,768]{2,1,0:T(1,128)S(1)}, u32[]{:S(2)}, u32[]{:S(2)}) collective-permute-start(f32[128,1,768]{2,1,0:T(1,128)S(1)} %slice.35), channel_id=1, source_target_pairs={{0,128},{128,0},{256,384},{384,256},{1,129},{129,1},{257,385},{385... | collective-permute-start | bytes 1179656 | tf_op jit(solution)/shard_map/ppermute | solution.py:309
  56.7 18.8 %collective-permute-start.1 = (f32[512,128]{1,0:T(8,128)S(1)}, f32[512,128]{1,0:T(8,128)S(1)}, u32[]{:S(2)}, u32[]{:S(2)}) collective-permute-start(f32[512,128]{1,0:T(8,128)S(1)} %copy-done.4), channel_id=1, source_target_pairs={{0,259},{1,258},{2,257},{3,256},{4,263},{5,262},{6,261},{7,260},{8... | collective-permute-start | bytes 786440 | tf_op jit(solution)/shard_map/ppermute | solution.py:308
  75.5 50.8 %copy-start.5 = (f32[512,128]{1,0:T(8,128)}, f32[512,128]{1,0:T(8,128)S(1)}, u32[]{:S(2)}) copy-start(f32[512,128]{1,0:T(8,128)S(1)} %collective-permute-done.1) | copy-start | bytes 786436
  126.6 8.2 %collective-permute-start.2 = (f32[256,768]{1,0:T(8,128)S(1)}, f32[256,768]{1,0:T(8,128)S(1)}, u32[]{:S(2)}, u32[]{:S(2)}) collective-permute-start(f32[256,768]{1,0:T(8,128)S(1)} %get-tuple-element.38), channel_id=1, source_target_pairs={{0,128},{128,0},{256,384},{384,256},{1,129},{129,1},{257,385},{385... | collective-permute-start | bytes 2359304 | tf_op jit(solution)/shard_map/ppermute | solution.py:324
  135.6 28.1 %collective-permute-start.6 = (f32[768,128]{1,0:T(8,128)S(1)}, f32[768,128]{1,0:T(8,128)S(1)}, u32[]{:S(2)}, u32[]{:S(2)}) collective-permute-start(f32[768,128]{1,0:T(8,128)S(1)} %convolution_add_fusion), channel_id=1, source_target_pairs={{0,256},{256,0},{128,384},{384,128},{1,257},{257,1},{129,385},{385... | collective-permute-start | bytes 1179656 | tf_op jit(solution)/shard_map/ppermute | solution.py:340
  141.7 9.6 %collective-permute-start.3 = (f32[128,512]{1,0:T(8,128)S(1)}, f32[128,512]{1,0:T(8,128)S(1)}, u32[]{:S(2)}, u32[]{:S(2)}) collective-permute-start(f32[128,512]{1,0:T(8,128)S(1)} %get-tuple-element.51), channel_id=1, source_target_pairs={{0,4},{1,5},{2,6},{3,7},{4,0},{5,1},{6,2},{7,3},{8,12},{9,13},{10,... | collective-permute-start | bytes 786440 | tf_op jit(solution)/shard_map/ppermute | solution.py:347
  144.0 13.5 %collective-permute-start.4 = (f32[128,512]{1,0:T(8,128)S(1)}, f32[128,512]{1,0:T(8,128)S(1)}, u32[]{:S(2)}, u32[]{:S(2)}) collective-permute-start(f32[128,512]{1,0:T(8,128)S(1)} %get-tuple-element.50), channel_id=1, source_target_pairs={{0,8},{1,9},{2,10},{3,11},{4,12},{5,13},{6,14},{7,15},{8,0},{9,1},... | collective-permute-start | bytes 786440 | tf_op jit(solution)/shard_map/ppermute | solution.py:347
  147.6 16.1 %collective-permute-start.5 = (f32[128,512]{1,0:T(8,128)S(1)}, f32[128,512]{1,0:T(8,128)S(1)}, u32[]{:S(2)}, u32[]{:S(2)}) collective-permute-start(f32[128,512]{1,0:T(8,128)S(1)} %get-tuple-element.49), channel_id=1, source_target_pairs={{0,12},{1,13},{2,14},{3,15},{4,8},{5,9},{6,10},{7,11},{8,4},{9,5},... | collective-permute-start | bytes 786440 | tf_op jit(solution)/shard_map/ppermute | solution.py:347
  163.7 0.7 copy-start.2
  188.1 7.2 %copy-start.3 = (f32[768,128]{1,0:T(8,128)S(1)}, f32[768,128]{1,0:T(8,128)}, u32[]{:S(2)}) copy-start(f32[768,128]{1,0:T(8,128)} %copy-done.2) | copy-start | bytes 1179652
  188.1 22.6 %all-to-all-start.3 = ((f32[128,1,1024]{2,1,0:T(1,128)}), f32[128,1,1024]{2,1,0:T(1,128)S(1)}, u32[]{:S(2)}, u32[]{:S(2)}) async-start(f32[128,1,1024]{2,1,0:T(1,128)} %broadcast_in_dim.2), calls=%async_computation.3 | async-start | bytes 1048576 | tf_op jit(solution)/shard_map/all_to_all | solution.py:353

commit v9 on v8

--- a/solution.py
+++ b/solution.py
@@ -304,8 +304,8 @@
     got = lax.all_to_all(
         sent.reshape(BLOCKS, 1, SENT * LANES), "dom", 0, 0, tiled=True, axis_index_groups=[ORDER]
     )
-    got, rotation_near = lax.optimization_barrier((got, rotation))
-    rotation_far = lax.ppermute(rotation_near, ("band", "dom"), Z_MIRROR)
+    rotation_far = lax.ppermute(rotation, ("band", "dom"), Z_MIRROR)
+    got, rotation_far = lax.optimization_barrier((got, rotation_far))
     v_other = lax.ppermute(got[:, :, CELLS:], "band", CORE_SWAP)
     x, lap, pot_own = first_laplace(got.reshape(BLOCKS * SENT, LANES))
     images = filtered_fields(
@@ -313,13 +313,8 @@
     )
 
     spot = lax.axis_index("dom")
-    images, rotation_far, spot, core, z_hi = lax.optimization_barrier(
-        (images, rotation_far, spot, core, z_hi)
-    )
     got = exchange(images.reshape(2 * BLOCKS, 1, CELLS), CORE_GROUPS)
-    got, rotation_near, rotation_far, spot, core, z_hi = lax.optimization_barrier(
-        (got, rotation_near, rotation_far, spot, core, z_hi)
-    )
+    got, rotation_near, rotation_far = lax.optimization_barrier((got, rotation, rotation_far))
     phi, both = split_fields(got.reshape(2 * BLOCKS * TILES, LANES))
     phi_other = lax.ppermute(phi, "band", CORE_SWAP)
     gram = jnp.concatenate(
@@ -341,9 +336,11 @@
 
     gram = gram.reshape(4, BLOCKS, 4 * BLOCKS)
     place = ((spot >> 2) & 3).astype(jnp.uint32)
-    pieces = [lax.dynamic_index_in_dim(gram, place ^ k, 0, keepdims=False) for k in range(4)]
+    pieces = [lax.dynamic_index_in_dim(gram, (place + k) & 3, 0, keepdims=False) for k in range(4)]
     for k in (2, 1, 3):
-        pairs = [(chip(y, x, z), chip(y, x ^ k, z)) for y in range(8) for x in range(4) for z in range(4)]
+        pairs = [
+            (chip(y, x, z), chip(y, (x + k) % 4, z)) for y in range(8) for x in range(4) for z in range(4)
+        ]
         pieces[k] = lax.ppermute(pieces[k], "dom", pairs)
     terms, rotated_far = lax.optimization_barrier((pieces, rotated_far))
     terms = (terms[0] + terms[1]) + (terms[2] + terms[3])

time: 215 us -> 207 us (0.963)
  blocking collectives: 122 us -> 20.5 us
  waiting for transfers between devices: 28.8 us -> 87.5 us
  starting transfers between devices: 37.5 us -> 72.6 us
    all_to_all x0 -> x2, waiting for transfers between devices: none -> 55.8 us  [the longest x1 39.1 us: exchange(): lax.all_to_all(x, ('band', 'dom'), 0, 0, tiled=True, axis_index_groups=gr...]
    all_to_all x2 -> x1, blocking collectives: 72.7 us -> 20.5 us  [exchange(): lax.all_to_all(x, ('band', 'dom'), 0, 0, tiled=True, axis_index_groups=gr...]
    all_to_all x1 -> x0, blocking collectives: 48.9 us -> none  [local(): lax.all_to_all(sent.reshape(BLOCKS, 1, SENT * LANES), 'dom', 0, 0, tiled=...]
    all_to_all x0 -> x2, starting transfers between devices: none -> 32.8 us  [the longest x1 17.9 us: local(): lax.all_to_all(sent.reshape(BLOCKS, 1, SENT * LANES), 'dom', 0, 0, tiled=...]
    ppermute x1, waiting for transfers between devices: 2.7 us -> 6.9 us  [local(): rotation_far = lax.ppermute(rotation, ('band', 'dom'), Z_MIRROR)]
    all_to_all x1, starting transfers between devices: 6.3 us -> 9.38 us  [local(): lax.all_to_all(jnp.broadcast_to(terms[None], (BLOCKS, 1, 8 * BLOCKS)), 'd...]
    ppermute x3, waiting for transfers between devices: 12.3 us -> 9.77 us  [local(): pieces[k] = lax.ppermute(pieces[k], 'dom', pairs)]
  transfers between devices with their start and end apart: 8 -> 10, of which waited for: 4 -> 8; matrix products, arithmetic and copies ran while one was open for 3% -> 3% of each run, Pallas kernels for 5% -> 1%
where the time goes in v9:
time: 207 us; the launch traced here: 205 us
  waiting for transfers between devices  87.5 us (42%)
  starting transfers between devices  72.6 us (35%)
  blocking collectives  20.5 us (10%)
  Pallas kernels  11.2 us (5%)
  local copies, waits for them, and re-layouts  5.68 us (3%)
  matrix products  4.9 us (2%)
    all_to_all x1, waiting for transfers between devices, exchange(): lax.all_to_all(x, ('band', 'dom'), 0, 0, tiled=True, axis_index_groups=gr...  39.1 us
    all_to_all x1, blocking collectives, exchange(): lax.all_to_all(x, ('band', 'dom'), 0, 0, tiled=True, axis_index_groups=gr...  20.5 us
    all_to_all x1, starting transfers between devices, local(): lax.all_to_all(sent.reshape(BLOCKS, 1, SENT * LANES), 'dom', 0, 0, tiled=...  17.9 us
    all_to_all x1, waiting for transfers between devices, local(): lax.all_to_all(sent.reshape(BLOCKS, 1, SENT * LANES), 'dom', 0, 0, tiled=...  16.7 us
    all_to_all x1, waiting for transfers between devices, local(): lax.all_to_all(jnp.broadcast_to(terms[None], (BLOCKS, 1, 8 * BLOCKS)), 'd...  14.9 us
    all_to_all x1, starting transfers between devices, exchange(): lax.all_to_all(x, ('band', 'dom'), 0, 0, tiled=True, axis_index_groups=gr...  14.9 us
    ppermute x3, waiting for transfers between devices, local(): pieces[k] = lax.ppermute(pieces[k], 'dom', pairs)  9.77 us
    all_to_all x1, starting transfers between devices, local(): lax.all_to_all(jnp.broadcast_to(terms[None], (BLOCKS, 1, 8 * BLOCKS)), 'd...  9.38 us
  transfers between devices with their start and end apart: 10, of which 8 were waited for; matrix products, arithmetic and copies ran while one was open for 3% of the time, Pallas kernels for 1%

profile of v9, /device:TPU:1, one launch (start us, length us, event | category | flops | bytes accessed | tf_op | source)
XLA Modules:
  0.0 204.7 jit_solution(17593482893073645349)
XLA Ops:
  1.5 1.1 copy-done.1
  2.6 1.4 shard_map.67
  4.0 17.9 %all-to-all-start = ((f32[128,1,2304]{2,1,0:T(1,128)}), f32[128,1,2304]{2,1,0:T(1,128)S(1)}, u32[]{:S(2)}, u32[]{:S(2)}) async-start(f32[128,1,2304]{2,1,0:T(1,128)} %bitcast.3), calls=%async_computation | async-start | bytes 2359296 | tf_op jit(solution)/shard_map/all_to_all | solution.py:304
  21.9 7.5 %collective-permute-start = (f32[512,128]{1,0:T(8,128)S(1)}, f32[512,128]{1,0:T(8,128)S(1)}, u32[]{:S(2)}, u32[]{:S(2)}) collective-permute-start(f32[512,128]{1,0:T(8,128)S(1)} %copy-done.3), channel_id=1, source_target_pairs={{0,259},{1,258},{2,257},{3,256},{4,263},{5,262},{6,261},{7,260},{8... | collective-permute-start | bytes 786440 | tf_op jit(solution)/shard_map/ppermute | solution.py:307
  29.4 6.9 %collective-permute-done = f32[512,128]{1,0:T(8,128)S(1)} collective-permute-done((f32[512,128]{1,0:T(8,128)S(1)}, f32[512,128]{1,0:T(8,128)S(1)}, u32[]{:S(2)}, u32[]{:S(2)}) %collective-permute-start) | collective-permute-done | bytes 262176 | tf_op jit(solution)/shard_map/ppermute | solution.py:307
  36.3 16.7 %all-to-all-done = f32[128,1,2304]{2,1,0:T(1,128)S(1)} async-done(((f32[128,1,2304]{2,1,0:T(1,128)}), f32[128,1,2304]{2,1,0:T(1,128)S(1)}, u32[]{:S(2)}, u32[]{:S(2)}) %all-to-all-start) | async-done | bytes 1179680 | tf_op jit(solution)/shard_map/all_to_all | solution.py:304
  53.1 4.8 %collective-permute-start.1 = (f32[128,1,768]{2,1,0:T(1,128)S(1)}, f32[128,1,768]{2,1,0:T(1,128)S(1)}, u32[]{:S(2)}, u32[]{:S(2)}) collective-permute-start(f32[128,1,768]{2,1,0:T(1,128)S(1)} %slice.35), channel_id=1, source_target_pairs={{0,128},{128,0},{256,384},{384,256},{1,129},{129,1},{257,385},{385... | collective-permute-start | bytes 1179656 | tf_op jit(solution)/shard_map/ppermute | solution.py:309
  57.9 2.1 %shard_map.68 = (f32[8,12,16,128]{3,2,1,0:T(8,128)S(1)}, f32[8,12,16,128]{3,2,1,0:T(8,128)S(1)}, f32[8,6,16,128]{3,2,1,0:T(8,128)S(1)}) custom-call(f32[2304,128]{1,0:T(8,128)S(1)} %bitcast.50), custom_call_target="tpu_custom_call" | custom-call | flops 20000000 | bytes 150000000 | tf_op jit(solution)/shard_map/pallas_call | solution.py:254
  60.0 7.4 %shard_map.69 = f32[3072,128]{1,0:T(8,128)S(1)} custom-call(s32[1]{0:T(128)} %bitcast.core_ref, f32[3]{0:T(128)S(1)} %copy-done.2, f32[8,12,16,128]{3,2,1,0:T(8,128)S(1)} %get-tuple-element.19.x_ref, f32[8,12,16,128]{3,2,1,0:T(8,128)S(1)} %get-tuple-element.20.lap_ref, f32[8,6,16,128]{3,2,1,0:T(8,128)S(1)} %get-tuple-element.21.pot_own_ref, ...), custom_call_target="tpu_custom_call" | custom-call | flops 60000000 | bytes 40000000 | tf_op jit(solution)/shard_map/pallas_call | solution.py:271
  67.5 1.2 copy-done
  68.6 14.9 %all-to-all-start.1 = ((f32[256,1,1536]{2,1,0:T(1,128)}), f32[256,1,1536]{2,1,0:T(1,128)S(1)}, u32[]{:S(2)}, u32[]{:S(2)}) async-start(f32[256,1,1536]{2,1,0:T(1,128)} %bitcast.52), calls=%async_computation.1 | async-start | bytes 3145728 | tf_op jit(solution)/shard_map/all_to_all | solution.py:59
  83.5 39.1 %all-to-all-done.1 = f32[256,1,1536]{2,1,0:T(1,128)S(1)} async-done(((f32[256,1,1536]{2,1,0:T(1,128)}), f32[256,1,1536]{2,1,0:T(1,128)S(1)}, u32[]{:S(2)}, u32[]{:S(2)}) %all-to-all-start.1) | async-done | bytes 1572896 | tf_op jit(solution)/shard_map/all_to_all | solution.py:59
  122.9 3.8 %collective-permute-start.2 = (f32[256,768]{1,0:T(8,128)S(1)}, f32[256,768]{1,0:T(8,128)S(1)}, u32[]{:S(2)}, u32[]{:S(2)}) collective-permute-start(f32[256,768]{1,0:T(8,128)S(1)} %get-tuple-element.24), channel_id=1, source_target_pairs={{0,128},{128,0},{256,384},{384,256},{1,129},{129,1},{257,385},{385... | collective-permute-start | bytes 2359304 | tf_op jit(solution)/shard_map/ppermute | solution.py:319
  129.4 5.8 %collective-permute-start.6 = (f32[768,128]{1,0:T(8,128)S(1)}, f32[768,128]{1,0:T(8,128)S(1)}, u32[]{:S(2)}, u32[]{:S(2)}) collective-permute-start(f32[768,128]{1,0:T(8,128)S(1)} %convolution_add_fusion), channel_id=1, source_target_pairs={{0,256},{256,0},{128,384},{384,128},{1,257},{257,1},{129,385},{385... | collective-permute-start | bytes 1179656 | tf_op jit(solution)/shard_map/ppermute | solution.py:335
  136.2 2.4 %collective-permute-start.3 = (f32[128,512]{1,0:T(8,128)S(1)}, f32[128,512]{1,0:T(8,128)S(1)}, u32[]{:S(2)}, u32[]{:S(2)}) collective-permute-start(f32[128,512]{1,0:T(8,128)S(1)} %get-tuple-element.35), channel_id=1, source_target_pairs={{0,4},{1,5},{2,6},{3,7},{4,8},{5,9},{6,10},{7,11},{8,12},{9,13},{1... | collective-permute-start | bytes 786440 | tf_op jit(solution)/shard_map/ppermute | solution.py:344
  138.6 3.5 %collective-permute-start.4 = (f32[128,512]{1,0:T(8,128)S(1)}, f32[128,512]{1,0:T(8,128)S(1)}, u32[]{:S(2)}, u32[]{:S(2)}) collective-permute-start(f32[128,512]{1,0:T(8,128)S(1)} %get-tuple-element.34), channel_id=1, source_target_pairs={{0,8},{1,9},{2,10},{3,11},{4,12},{5,13},{6,14},{7,15},{8,0},{9,1},... | collective-permute-start | bytes 786440 | tf_op jit(solution)/shard_map/ppermute | solution.py:344
  142.1 2.7 %collective-permute-start.5 = (f32[128,512]{1,0:T(8,128)S(1)}, f32[128,512]{1,0:T(8,128)S(1)}, u32[]{:S(2)}, u32[]{:S(2)}) collective-permute-start(f32[128,512]{1,0:T(8,128)S(1)} %get-tuple-element.33), channel_id=1, source_target_pairs={{0,12},{1,13},{2,14},{3,15},{4,0},{5,1},{6,2},{7,3},{8,4},{9,5},{1... | collective-permute-start | bytes 786440 | tf_op jit(solution)/shard_map/ppermute | solution.py:344
  144.8 2.2 %collective-permute-done.3 = f32[128,512]{1,0:T(8,128)S(1)} collective-permute-done((f32[128,512]{1,0:T(8,128)S(1)}, f32[128,512]{1,0:T(8,128)S(1)}, u32[]{:S(2)}, u32[]{:S(2)}) %collective-permute-start.3) | collective-permute-done | bytes 262176 | tf_op jit(solution)/shard_map/ppermute | solution.py:344
  147.0 4.5 %collective-permute-done.4 = f32[128,512]{1,0:T(8,128)S(1)} collective-permute-done((f32[128,512]{1,0:T(8,128)S(1)}, f32[128,512]{1,0:T(8,128)S(1)}, u32[]{:S(2)}, u32[]{:S(2)}) %collective-permute-start.4) | collective-permute-done | bytes 262176 | tf_op jit(solution)/shard_map/ppermute | solution.py:344
  151.6 3.0 %collective-permute-done.5 = f32[128,512]{1,0:T(8,128)S(1)} collective-permute-done((f32[128,512]{1,0:T(8,128)S(1)}, f32[128,512]{1,0:T(8,128)S(1)}, u32[]{:S(2)}, u32[]{:S(2)}) %collective-permute-start.5) | collective-permute-done | bytes 262176 | tf_op jit(solution)/shard_map/ppermute | solution.py:344
  155.0 20.5 %all_to_all.20 = f32[64,1,1024]{2,1,0:T(1,128)S(1)} all-to-all(f32[64,1,1024]{2,1,0:T(1,128)S(1)} %bitcast.60), channel_id=1, replica_groups={{0,256,1,257,2,258,3,259,16,272,17,273,18,274,19,275,32,288,33,289,34,2..., dimensions={0} | all-to-all | bytes 524288 | tf_op jit(solution)/shard_map/all_to_all | solution.py:59
  175.7 1.1 broadcast_in_dim.2
  176.8 9.4 %all-to-all-start.3 = ((f32[128,1,1024]{2,1,0:T(1,128)}), f32[128,1,1024]{2,1,0:T(1,128)S(1)}, u32[]{:S(2)}, u32[]{:S(2)}) async-start(f32[128,1,1024]{2,1,0:T(1,128)} %broadcast_in_dim.2), calls=%async_computation.3 | async-start | bytes 1048576 | tf_op jit(solution)/shard_map/all_to_all | solution.py:350
  188.8 14.9 %all-to-all-done.3 = f32[128,1,1024]{2,1,0:T(1,128)S(1)} async-done(((f32[128,1,1024]{2,1,0:T(1,128)}), f32[128,1,1024]{2,1,0:T(1,128)S(1)}, u32[]{:S(2)}, u32[]{:S(2)}) %all-to-all-start.3) | async-done | bytes 524320 | tf_op jit(solution)/shard_map/all_to_all | solution.py:350
  (31 shorter events, 9.0 us)
Async XLA Ops:
  1.5 1.1 copy-start.1
  3.9 17.9 %copy-start.3 = (f32[512,128]{1,0:T(8,128)S(1)}, f32[512,128]{1,0:T(8,128)}, u32[]{:S(2)}) copy-start(f32[512,128]{1,0:T(8,128)} %param.7) | copy-start | bytes 786436
  4.0 49.1 %all-to-all-start = ((f32[128,1,2304]{2,1,0:T(1,128)}), f32[128,1,2304]{2,1,0:T(1,128)S(1)}, u32[]{:S(2)}, u32[]{:S(2)}) async-start(f32[128,1,2304]{2,1,0:T(1,128)} %bitcast.3), calls=%async_computation | async-start | bytes 2359296 | tf_op jit(solution)/shard_map/all_to_all | solution.py:304
  21.9 38.2 %copy-start.2 = (f32[3]{0:T(128)S(1)}, f32[3]{0:T(128)}, u32[]{:S(2)}) copy-start(f32[3]{0:T(128)} %bounds_ref.1) | copy-start | bytes 40
  21.9 14.4 %collective-permute-start = (f32[512,128]{1,0:T(8,128)S(1)}, f32[512,128]{1,0:T(8,128)S(1)}, u32[]{:S(2)}, u32[]{:S(2)}) collective-permute-start(f32[512,128]{1,0:T(8,128)S(1)} %copy-done.3), channel_id=1, source_target_pairs={{0,259},{1,258},{2,257},{3,256},{4,263},{5,262},{6,261},{7,260},{8... | collective-permute-start | bytes 786440 | tf_op jit(solution)/shard_map/ppermute | solution.py:307
  53.1 6.9 %collective-permute-start.1 = (f32[128,1,768]{2,1,0:T(1,128)S(1)}, f32[128,1,768]{2,1,0:T(1,128)S(1)}, u32[]{:S(2)}, u32[]{:S(2)}) collective-permute-start(f32[128,1,768]{2,1,0:T(1,128)S(1)} %slice.35), channel_id=1, source_target_pairs={{0,128},{128,0},{256,384},{384,256},{1,129},{129,1},{257,385},{385... | collective-permute-start | bytes 1179656 | tf_op jit(solution)/shard_map/ppermute | solution.py:309
  67.5 1.2 copy-start
  68.6 54.0 %all-to-all-start.1 = ((f32[256,1,1536]{2,1,0:T(1,128)}), f32[256,1,1536]{2,1,0:T(1,128)S(1)}, u32[]{:S(2)}, u32[]{:S(2)}) async-start(f32[256,1,1536]{2,1,0:T(1,128)} %bitcast.52), calls=%async_computation.1 | async-start | bytes 3145728 | tf_op jit(solution)/shard_map/all_to_all | solution.py:59
  122.9 5.7 %collective-permute-start.2 = (f32[256,768]{1,0:T(8,128)S(1)}, f32[256,768]{1,0:T(8,128)S(1)}, u32[]{:S(2)}, u32[]{:S(2)}) collective-permute-start(f32[256,768]{1,0:T(8,128)S(1)} %get-tuple-element.24), channel_id=1, source_target_pairs={{0,128},{128,0},{256,384},{384,256},{1,129},{129,1},{257,385},{385... | collective-permute-start | bytes 2359304 | tf_op jit(solution)/shard_map/ppermute | solution.py:319
  129.4 25.2 %collective-permute-start.6 = (f32[768,128]{1,0:T(8,128)S(1)}, f32[768,128]{1,0:T(8,128)S(1)}, u32[]{:S(2)}, u32[]{:S(2)}) collective-permute-start(f32[768,128]{1,0:T(8,128)S(1)} %convolution_add_fusion), channel_id=1, source_target_pairs={{0,256},{256,0},{128,384},{384,128},{1,257},{257,1},{129,385},{385... | collective-permute-start | bytes 1179656 | tf_op jit(solution)/shard_map/ppermute | solution.py:335
  136.2 10.8 %collective-permute-start.3 = (f32[128,512]{1,0:T(8,128)S(1)}, f32[128,512]{1,0:T(8,128)S(1)}, u32[]{:S(2)}, u32[]{:S(2)}) collective-permute-start(f32[128,512]{1,0:T(8,128)S(1)} %get-tuple-element.35), channel_id=1, source_target_pairs={{0,4},{1,5},{2,6},{3,7},{4,8},{5,9},{6,10},{7,11},{8,12},{9,13},{1... | collective-permute-start | bytes 786440 | tf_op jit(solution)/shard_map/ppermute | solution.py:344
  138.6 13.0 %collective-permute-start.4 = (f32[128,512]{1,0:T(8,128)S(1)}, f32[128,512]{1,0:T(8,128)S(1)}, u32[]{:S(2)}, u32[]{:S(2)}) collective-permute-start(f32[128,512]{1,0:T(8,128)S(1)} %get-tuple-element.34), channel_id=1, source_target_pairs={{0,8},{1,9},{2,10},{3,11},{4,12},{5,13},{6,14},{7,15},{8,0},{9,1},... | collective-permute-start | bytes 786440 | tf_op jit(solution)/shard_map/ppermute | solution.py:344
  142.1 12.5 %collective-permute-start.5 = (f32[128,512]{1,0:T(8,128)S(1)}, f32[128,512]{1,0:T(8,128)S(1)}, u32[]{:S(2)}, u32[]{:S(2)}) collective-permute-start(f32[128,512]{1,0:T(8,128)S(1)} %get-tuple-element.33), channel_id=1, source_target_pairs={{0,12},{1,13},{2,14},{3,15},{4,0},{5,1},{6,2},{7,3},{8,4},{9,5},{1... | collective-permute-start | bytes 786440 | tf_op jit(solution)/shard_map/ppermute | solution.py:344
  176.8 26.9 %all-to-all-start.3 = ((f32[128,1,1024]{2,1,0:T(1,128)}), f32[128,1,1024]{2,1,0:T(1,128)S(1)}, u32[]{:S(2)}, u32[]{:S(2)}) async-start(f32[128,1,1024]{2,1,0:T(1,128)} %broadcast_in_dim.2), calls=%async_computation.3 | async-start | bytes 1048576 | tf_op jit(solution)/shard_map/all_to_all | solution.py:350

commit v10 on v9

--- a/solution.py
+++ b/solution.py
@@ -63,13 +63,13 @@
 EXT = (BX + 2 * REACH, BY + 2 * REACH, BZ + 16, LANES)
 
 
-def pack_kernel(core_ref, orbitals_ref, potential_ref, out_ref, wide):
+def pack_kernel(core_ref, orbitals_ref, potential_ref, out_ref):
     for t in range(TILES):
         tile = orbitals_ref[t * LANES : (t + 1) * LANES]
         out_ref[pl.ds(t, BLOCKS, stride=SENT), :] = jnp.transpose(tile)
-    wide[...] = jnp.concatenate([potential_ref[i] for i in range(BX)], axis=1)
     for s in range(HALF_TILES):
-        row = wide[pl.ds(core_ref[0] * HALF_TILES + s, 1), :]
+        plane = potential_ref[core_ref[0] * HALF_TILES + s]
+        row = jnp.concatenate([plane[i : i + 1] for i in range(BX)], axis=1)
         out_ref[pl.ds(TILES + s, BLOCKS, stride=SENT), :] = jnp.broadcast_to(row, (BLOCKS, LANES))
 
 
@@ -80,7 +80,6 @@
         out_shape=jax.ShapeDtypeStruct((BLOCKS * SENT, LANES), jnp.float32),
         in_specs=[pl.BlockSpec(memory_space=pltpu.SMEM), vmem, vmem],
         out_specs=vmem,
-        scratch_shapes=[pltpu.VMEM((BY, BX * BZ), jnp.float32)],
         compiler_params=pltpu.CompilerParams(vmem_limit_bytes=16 * 1024 * 1024),
     )(core, orbitals, potential)
 
@@ -300,7 +299,7 @@
     z_hi, core = band >> 1, band & 1
     here = core.reshape(1)
 
-    sent = packed(here, orbitals.reshape(CELLS, width), potential[0])
+    sent = packed(here, orbitals.reshape(CELLS, width), potential[0].transpose(1, 0, 2))
     got = lax.all_to_all(
         sent.reshape(BLOCKS, 1, SENT * LANES), "dom", 0, 0, tiled=True, axis_index_groups=[ORDER]
     )

time: 207 us -> 207 us (level)
  no operation moved by 1% of the time
where the time goes in v10:
time: 207 us; the launch traced here: 205 us
  waiting for transfers between devices  87.5 us (42%)
  starting transfers between devices  72.6 us (35%)
  blocking collectives  20.5 us (10%)
  Pallas kernels  11.2 us (5%)
  local copies, waits for them, and re-layouts  5.65 us (3%)
  matrix products  4.9 us (2%)
    all_to_all x1, waiting for transfers between devices, exchange(): lax.all_to_all(x, ('band', 'dom'), 0, 0, tiled=True, axis_index_groups=gr...  39.1 us
    all_to_all x1, blocking collectives, exchange(): lax.all_to_all(x, ('band', 'dom'), 0, 0, tiled=True, axis_index_groups=gr...  20.5 us
    all_to_all x1, starting transfers between devices, local(): lax.all_to_all(sent.reshape(BLOCKS, 1, SENT * LANES), 'dom', 0, 0, tiled=...  17.9 us
    all_to_all x1, waiting for transfers between devices, local(): lax.all_to_all(sent.reshape(BLOCKS, 1, SENT * LANES), 'dom', 0, 0, tiled=...  16.7 us
    all_to_all x1, waiting for transfers between devices, local(): lax.all_to_all(jnp.broadcast_to(terms[None], (BLOCKS, 1, 8 * BLOCKS)), 'd...  14.9 us
    all_to_all x1, starting transfers between devices, exchange(): lax.all_to_all(x, ('band', 'dom'), 0, 0, tiled=True, axis_index_groups=gr...  14.9 us
    ppermute x3, waiting for transfers between devices, local(): pieces[k] = lax.ppermute(pieces[k], 'dom', pairs)  9.77 us
    all_to_all x1, starting transfers between devices, local(): lax.all_to_all(jnp.broadcast_to(terms[None], (BLOCKS, 1, 8 * BLOCKS)), 'd...  9.38 us
  transfers between devices with their start and end apart: 10, of which 8 were waited for; matrix products, arithmetic and copies ran while one was open for 3% of the time, Pallas kernels for 1%

profile of v10, /device:TPU:1, one launch (start us, length us, event | category | flops | bytes accessed | tf_op | source)
XLA Modules:
  0.0 204.7 jit_solution(16540460146193302961)
XLA Ops:
  0.6 1.1 copy-done.1
  2.6 1.4 shard_map.67
  4.0 17.9 %all-to-all-start = ((f32[128,1,2304]{2,1,0:T(1,128)}), f32[128,1,2304]{2,1,0:T(1,128)S(1)}, u32[]{:S(2)}, u32[]{:S(2)}) async-start(f32[128,1,2304]{2,1,0:T(1,128)} %bitcast.4), calls=%async_computation | async-start | bytes 2359296 | tf_op jit(solution)/shard_map/all_to_all | solution.py:303
  21.9 7.5 %collective-permute-start = (f32[512,128]{1,0:T(8,128)S(1)}, f32[512,128]{1,0:T(8,128)S(1)}, u32[]{:S(2)}, u32[]{:S(2)}) collective-permute-start(f32[512,128]{1,0:T(8,128)S(1)} %copy-done.4), channel_id=1, source_target_pairs={{0,259},{1,258},{2,257},{3,256},{4,263},{5,262},{6,261},{7,260},{8... | collective-permute-start | bytes 786440 | tf_op jit(solution)/shard_map/ppermute | solution.py:306
  29.4 6.9 %collective-permute-done = f32[512,128]{1,0:T(8,128)S(1)} collective-permute-done((f32[512,128]{1,0:T(8,128)S(1)}, f32[512,128]{1,0:T(8,128)S(1)}, u32[]{:S(2)}, u32[]{:S(2)}) %collective-permute-start) | collective-permute-done | bytes 262176 | tf_op jit(solution)/shard_map/ppermute | solution.py:306
  36.3 16.7 %all-to-all-done = f32[128,1,2304]{2,1,0:T(1,128)S(1)} async-done(((f32[128,1,2304]{2,1,0:T(1,128)}), f32[128,1,2304]{2,1,0:T(1,128)S(1)}, u32[]{:S(2)}, u32[]{:S(2)}) %all-to-all-start) | async-done | bytes 1179680 | tf_op jit(solution)/shard_map/all_to_all | solution.py:303
  53.1 4.8 %collective-permute-start.1 = (f32[128,1,768]{2,1,0:T(1,128)S(1)}, f32[128,1,768]{2,1,0:T(1,128)S(1)}, u32[]{:S(2)}, u32[]{:S(2)}) collective-permute-start(f32[128,1,768]{2,1,0:T(1,128)S(1)} %slice.35), channel_id=1, source_target_pairs={{0,128},{128,0},{256,384},{384,256},{1,129},{129,1},{257,385},{385... | collective-permute-start | bytes 1179656 | tf_op jit(solution)/shard_map/ppermute | solution.py:308
  57.9 2.1 %shard_map.68 = (f32[8,12,16,128]{3,2,1,0:T(8,128)S(1)}, f32[8,12,16,128]{3,2,1,0:T(8,128)S(1)}, f32[8,6,16,128]{3,2,1,0:T(8,128)S(1)}) custom-call(f32[2304,128]{1,0:T(8,128)S(1)} %bitcast.50), custom_call_target="tpu_custom_call" | custom-call | flops 20000000 | bytes 150000000 | tf_op jit(solution)/shard_map/pallas_call | solution.py:253
  60.0 7.4 %shard_map.69 = f32[3072,128]{1,0:T(8,128)S(1)} custom-call(s32[1]{0:T(128)} %bitcast.core_ref, f32[3]{0:T(128)S(1)} %copy-done.3, f32[8,12,16,128]{3,2,1,0:T(8,128)S(1)} %get-tuple-element.19.x_ref, f32[8,12,16,128]{3,2,1,0:T(8,128)S(1)} %get-tuple-element.20.lap_ref, f32[8,6,16,128]{3,2,1,0:T(8,128)S(1)} %get-tuple-element.21.pot_own_ref, ...), custom_call_target="tpu_custom_call" | custom-call | flops 60000000 | bytes 40000000 | tf_op jit(solution)/shard_map/pallas_call | solution.py:270
  67.5 1.2 copy-done
  68.6 14.9 %all-to-all-start.1 = ((f32[256,1,1536]{2,1,0:T(1,128)}), f32[256,1,1536]{2,1,0:T(1,128)S(1)}, u32[]{:S(2)}, u32[]{:S(2)}) async-start(f32[256,1,1536]{2,1,0:T(1,128)} %bitcast.52), calls=%async_computation.1 | async-start | bytes 3145728 | tf_op jit(solution)/shard_map/all_to_all | solution.py:59
  83.5 39.1 %all-to-all-done.1 = f32[256,1,1536]{2,1,0:T(1,128)S(1)} async-done(((f32[256,1,1536]{2,1,0:T(1,128)}), f32[256,1,1536]{2,1,0:T(1,128)S(1)}, u32[]{:S(2)}, u32[]{:S(2)}) %all-to-all-start.1) | async-done | bytes 1572896 | tf_op jit(solution)/shard_map/all_to_all | solution.py:59
  122.9 3.8 %collective-permute-start.2 = (f32[256,768]{1,0:T(8,128)S(1)}, f32[256,768]{1,0:T(8,128)S(1)}, u32[]{:S(2)}, u32[]{:S(2)}) collective-permute-start(f32[256,768]{1,0:T(8,128)S(1)} %get-tuple-element.24), channel_id=1, source_target_pairs={{0,128},{128,0},{256,384},{384,256},{1,129},{129,1},{257,385},{385... | collective-permute-start | bytes 2359304 | tf_op jit(solution)/shard_map/ppermute | solution.py:318
  129.4 5.8 %collective-permute-start.6 = (f32[768,128]{1,0:T(8,128)S(1)}, f32[768,128]{1,0:T(8,128)S(1)}, u32[]{:S(2)}, u32[]{:S(2)}) collective-permute-start(f32[768,128]{1,0:T(8,128)S(1)} %convolution_add_fusion), channel_id=1, source_target_pairs={{0,256},{256,0},{128,384},{384,128},{1,257},{257,1},{129,385},{385... | collective-permute-start | bytes 1179656 | tf_op jit(solution)/shard_map/ppermute | solution.py:334
  136.2 2.4 %collective-permute-start.3 = (f32[128,512]{1,0:T(8,128)S(1)}, f32[128,512]{1,0:T(8,128)S(1)}, u32[]{:S(2)}, u32[]{:S(2)}) collective-permute-start(f32[128,512]{1,0:T(8,128)S(1)} %get-tuple-element.35), channel_id=1, source_target_pairs={{0,4},{1,5},{2,6},{3,7},{4,8},{5,9},{6,10},{7,11},{8,12},{9,13},{1... | collective-permute-start | bytes 786440 | tf_op jit(solution)/shard_map/ppermute | solution.py:343
  138.6 3.5 %collective-permute-start.4 = (f32[128,512]{1,0:T(8,128)S(1)}, f32[128,512]{1,0:T(8,128)S(1)}, u32[]{:S(2)}, u32[]{:S(2)}) collective-permute-start(f32[128,512]{1,0:T(8,128)S(1)} %get-tuple-element.34), channel_id=1, source_target_pairs={{0,8},{1,9},{2,10},{3,11},{4,12},{5,13},{6,14},{7,15},{8,0},{9,1},... | collective-permute-start | bytes 786440 | tf_op jit(solution)/shard_map/ppermute | solution.py:343
  142.1 2.7 %collective-permute-start.5 = (f32[128,512]{1,0:T(8,128)S(1)}, f32[128,512]{1,0:T(8,128)S(1)}, u32[]{:S(2)}, u32[]{:S(2)}) collective-permute-start(f32[128,512]{1,0:T(8,128)S(1)} %get-tuple-element.33), channel_id=1, source_target_pairs={{0,12},{1,13},{2,14},{3,15},{4,0},{5,1},{6,2},{7,3},{8,4},{9,5},{1... | collective-permute-start | bytes 786440 | tf_op jit(solution)/shard_map/ppermute | solution.py:343
  144.8 2.2 %collective-permute-done.3 = f32[128,512]{1,0:T(8,128)S(1)} collective-permute-done((f32[128,512]{1,0:T(8,128)S(1)}, f32[128,512]{1,0:T(8,128)S(1)}, u32[]{:S(2)}, u32[]{:S(2)}) %collective-permute-start.3) | collective-permute-done | bytes 262176 | tf_op jit(solution)/shard_map/ppermute | solution.py:343
  147.1 4.5 %collective-permute-done.4 = f32[128,512]{1,0:T(8,128)S(1)} collective-permute-done((f32[128,512]{1,0:T(8,128)S(1)}, f32[128,512]{1,0:T(8,128)S(1)}, u32[]{:S(2)}, u32[]{:S(2)}) %collective-permute-start.4) | collective-permute-done | bytes 262176 | tf_op jit(solution)/shard_map/ppermute | solution.py:343
  151.6 3.0 %collective-permute-done.5 = f32[128,512]{1,0:T(8,128)S(1)} collective-permute-done((f32[128,512]{1,0:T(8,128)S(1)}, f32[128,512]{1,0:T(8,128)S(1)}, u32[]{:S(2)}, u32[]{:S(2)}) %collective-permute-start.5) | collective-permute-done | bytes 262176 | tf_op jit(solution)/shard_map/ppermute | solution.py:343
  155.0 20.5 %all_to_all.20 = f32[64,1,1024]{2,1,0:T(1,128)S(1)} all-to-all(f32[64,1,1024]{2,1,0:T(1,128)S(1)} %bitcast.60), channel_id=1, replica_groups={{0,256,1,257,2,258,3,259,16,272,17,273,18,274,19,275,32,288,33,289,34,2..., dimensions={0} | all-to-all | bytes 524288 | tf_op jit(solution)/shard_map/all_to_all | solution.py:59
  175.7 1.1 broadcast_in_dim.2
  176.8 9.4 %all-to-all-start.3 = ((f32[128,1,1024]{2,1,0:T(1,128)}), f32[128,1,1024]{2,1,0:T(1,128)S(1)}, u32[]{:S(2)}, u32[]{:S(2)}) async-start(f32[128,1,1024]{2,1,0:T(1,128)} %broadcast_in_dim.2), calls=%async_computation.3 | async-start | bytes 1048576 | tf_op jit(solution)/shard_map/all_to_all | solution.py:349
  188.8 14.9 %all-to-all-done.3 = f32[128,1,1024]{2,1,0:T(1,128)S(1)} async-done(((f32[128,1,1024]{2,1,0:T(1,128)}), f32[128,1,1024]{2,1,0:T(1,128)S(1)}, u32[]{:S(2)}, u32[]{:S(2)}) %all-to-all-start.3) | async-done | bytes 524320 | tf_op jit(solution)/shard_map/all_to_all | solution.py:349
  (32 shorter events, 9.0 us)
Async XLA Ops:
  0.6 1.1 copy-start.1
  1.8 0.8 copy-start.2
  4.0 17.9 %copy-start.4 = (f32[512,128]{1,0:T(8,128)S(1)}, f32[512,128]{1,0:T(8,128)}, u32[]{:S(2)}) copy-start(f32[512,128]{1,0:T(8,128)} %param.7) | copy-start | bytes 786436
  4.0 49.1 %all-to-all-start = ((f32[128,1,2304]{2,1,0:T(1,128)}), f32[128,1,2304]{2,1,0:T(1,128)S(1)}, u32[]{:S(2)}, u32[]{:S(2)}) async-start(f32[128,1,2304]{2,1,0:T(1,128)} %bitcast.4), calls=%async_computation | async-start | bytes 2359296 | tf_op jit(solution)/shard_map/all_to_all | solution.py:303
  21.9 38.2 %copy-start.3 = (f32[3]{0:T(128)S(1)}, f32[3]{0:T(128)}, u32[]{:S(2)}) copy-start(f32[3]{0:T(128)} %bounds_ref.1) | copy-start | bytes 40
  21.9 14.4 %collective-permute-start = (f32[512,128]{1,0:T(8,128)S(1)}, f32[512,128]{1,0:T(8,128)S(1)}, u32[]{:S(2)}, u32[]{:S(2)}) collective-permute-start(f32[512,128]{1,0:T(8,128)S(1)} %copy-done.4), channel_id=1, source_target_pairs={{0,259},{1,258},{2,257},{3,256},{4,263},{5,262},{6,261},{7,260},{8... | collective-permute-start | bytes 786440 | tf_op jit(solution)/shard_map/ppermute | solution.py:306
  53.1 6.9 %collective-permute-start.1 = (f32[128,1,768]{2,1,0:T(1,128)S(1)}, f32[128,1,768]{2,1,0:T(1,128)S(1)}, u32[]{:S(2)}, u32[]{:S(2)}) collective-permute-start(f32[128,1,768]{2,1,0:T(1,128)S(1)} %slice.35), channel_id=1, source_target_pairs={{0,128},{128,0},{256,384},{384,256},{1,129},{129,1},{257,385},{385... | collective-permute-start | bytes 1179656 | tf_op jit(solution)/shard_map/ppermute | solution.py:308
  67.5 1.2 copy-start
  68.6 54.0 %all-to-all-start.1 = ((f32[256,1,1536]{2,1,0:T(1,128)}), f32[256,1,1536]{2,1,0:T(1,128)S(1)}, u32[]{:S(2)}, u32[]{:S(2)}) async-start(f32[256,1,1536]{2,1,0:T(1,128)} %bitcast.52), calls=%async_computation.1 | async-start | bytes 3145728 | tf_op jit(solution)/shard_map/all_to_all | solution.py:59
  122.9 5.7 %collective-permute-start.2 = (f32[256,768]{1,0:T(8,128)S(1)}, f32[256,768]{1,0:T(8,128)S(1)}, u32[]{:S(2)}, u32[]{:S(2)}) collective-permute-start(f32[256,768]{1,0:T(8,128)S(1)} %get-tuple-element.24), channel_id=1, source_target_pairs={{0,128},{128,0},{256,384},{384,256},{1,129},{129,1},{257,385},{385... | collective-permute-start | bytes 2359304 | tf_op jit(solution)/shard_map/ppermute | solution.py:318
  129.4 25.2 %collective-permute-start.6 = (f32[768,128]{1,0:T(8,128)S(1)}, f32[768,128]{1,0:T(8,128)S(1)}, u32[]{:S(2)}, u32[]{:S(2)}) collective-permute-start(f32[768,128]{1,0:T(8,128)S(1)} %convolution_add_fusion), channel_id=1, source_target_pairs={{0,256},{256,0},{128,384},{384,128},{1,257},{257,1},{129,385},{385... | collective-permute-start | bytes 1179656 | tf_op jit(solution)/shard_map/ppermute | solution.py:334
  136.2 10.9 %collective-permute-start.3 = (f32[128,512]{1,0:T(8,128)S(1)}, f32[128,512]{1,0:T(8,128)S(1)}, u32[]{:S(2)}, u32[]{:S(2)}) collective-permute-start(f32[128,512]{1,0:T(8,128)S(1)} %get-tuple-element.35), channel_id=1, source_target_pairs={{0,4},{1,5},{2,6},{3,7},{4,8},{5,9},{6,10},{7,11},{8,12},{9,13},{1... | collective-permute-start | bytes 786440 | tf_op jit(solution)/shard_map/ppermute | solution.py:343
  138.6 13.0 %collective-permute-start.4 = (f32[128,512]{1,0:T(8,128)S(1)}, f32[128,512]{1,0:T(8,128)S(1)}, u32[]{:S(2)}, u32[]{:S(2)}) collective-permute-start(f32[128,512]{1,0:T(8,128)S(1)} %get-tuple-element.34), channel_id=1, source_target_pairs={{0,8},{1,9},{2,10},{3,11},{4,12},{5,13},{6,14},{7,15},{8,0},{9,1},... | collective-permute-start | bytes 786440 | tf_op jit(solution)/shard_map/ppermute | solution.py:343
  142.1 12.5 %collective-permute-start.5 = (f32[128,512]{1,0:T(8,128)S(1)}, f32[128,512]{1,0:T(8,128)S(1)}, u32[]{:S(2)}, u32[]{:S(2)}) collective-permute-start(f32[128,512]{1,0:T(8,128)S(1)} %get-tuple-element.33), channel_id=1, source_target_pairs={{0,12},{1,13},{2,14},{3,15},{4,0},{5,1},{6,2},{7,3},{8,4},{9,5},{1... | collective-permute-start | bytes 786440 | tf_op jit(solution)/shard_map/ppermute | solution.py:343
  176.8 26.9 %all-to-all-start.3 = ((f32[128,1,1024]{2,1,0:T(1,128)}), f32[128,1,1024]{2,1,0:T(1,128)S(1)}, u32[]{:S(2)}, u32[]{:S(2)}) async-start(f32[128,1,1024]{2,1,0:T(1,128)} %broadcast_in_dim.2), calls=%async_computation.3 | async-start | bytes 1048576 | tf_op jit(solution)/shard_map/all_to_all | solution.py:349

commit v11 on v10

--- a/solution.py
+++ b/solution.py
@@ -40,7 +40,7 @@
 
 CORE_GROUPS = [[flat(2 * h + c, d) for d in ORDER for h in range(2)] for c in range(2)]
 PLANE_GROUPS = [
-    [flat(2 * h + c, chip(y, x, z)) for y in range(8) for z in range(4) for h in range(2)]
+    [flat(2 * h + c, chip(y, x, z)) for z in range(4) for y in range(8) for h in range(2)]
     for c in range(2)
     for x in range(4)
 ]
@@ -349,7 +349,7 @@
     whole = lax.all_to_all(
         jnp.broadcast_to(terms[None], (BLOCKS, 1, 8 * BLOCKS)), "dom", 0, 0, tiled=True
     )
-    whole = whole.reshape(8, 2, 2, 4, 4, 2, BLOCKS).transpose(5, 2, 1, 0, 3, 4, 6)
+    whole = whole.reshape(8, 2, 2, 4, 4, 2, BLOCKS).transpose(5, 2, 1, 3, 0, 4, 6)
     whole = whole.reshape(2, 2, 2, BLOCKS, BLOCKS)
     whole = jnp.where(core == 0, whole, whole[:, :, ::-1])
     whole = whole.reshape(2, 4 * BLOCKS, BLOCKS)

time: 207 us -> 207 us (level)
  no operation moved by 1% of the time
where the time goes in v11:
time: 207 us; the launch traced here: 205 us
  waiting for transfers between devices  87.5 us (42%)
  starting transfers between devices  73.5 us (36%)
  blocking collectives  19.8 us (10%)
  Pallas kernels  11.2 us (5%)
  local copies, waits for them, and re-layouts  5.65 us (3%)
  matrix products  4.89 us (2%)
    all_to_all x1, waiting for transfers between devices, exchange(): lax.all_to_all(x, ('band', 'dom'), 0, 0, tiled=True, axis_index_groups=gr...  39.1 us
    all_to_all x1, blocking collectives, exchange(): lax.all_to_all(x, ('band', 'dom'), 0, 0, tiled=True, axis_index_groups=gr...  19.8 us
    all_to_all x1, starting transfers between devices, local(): lax.all_to_all(sent.reshape(BLOCKS, 1, SENT * LANES), 'dom', 0, 0, tiled=...  17.9 us
    all_to_all x1, waiting for transfers between devices, local(): lax.all_to_all(sent.reshape(BLOCKS, 1, SENT * LANES), 'dom', 0, 0, tiled=...  16.7 us
    all_to_all x1, waiting for transfers between devices, local(): lax.all_to_all(jnp.broadcast_to(terms[None], (BLOCKS, 1, 8 * BLOCKS)), 'd...  14.9 us
    all_to_all x1, starting transfers between devices, exchange(): lax.all_to_all(x, ('band', 'dom'), 0, 0, tiled=True, axis_index_groups=gr...  14.9 us
    all_to_all x1, starting transfers between devices, local(): lax.all_to_all(jnp.broadcast_to(terms[None], (BLOCKS, 1, 8 * BLOCKS)), 'd...  10.3 us
    ppermute x3, waiting for transfers between devices, local(): pieces[k] = lax.ppermute(pieces[k], 'dom', pairs)  9.77 us
  transfers between devices with their start and end apart: 10, of which 8 were waited for; matrix products, arithmetic and copies ran while one was open for 3% of the time, Pallas kernels for 1%

profile of v11, /device:TPU:1, one launch (start us, length us, event | category | flops | bytes accessed | tf_op | source)
XLA Modules:
  0.0 204.9 jit_solution(4951327721386602556)
XLA Ops:
  0.6 1.1 copy-done.1
  2.6 1.4 shard_map.67
  4.0 17.9 %all-to-all-start = ((f32[128,1,2304]{2,1,0:T(1,128)}), f32[128,1,2304]{2,1,0:T(1,128)S(1)}, u32[]{:S(2)}, u32[]{:S(2)}) async-start(f32[128,1,2304]{2,1,0:T(1,128)} %bitcast.4), calls=%async_computation | async-start | bytes 2359296 | tf_op jit(solution)/shard_map/all_to_all | solution.py:303
  21.9 7.5 %collective-permute-start = (f32[512,128]{1,0:T(8,128)S(1)}, f32[512,128]{1,0:T(8,128)S(1)}, u32[]{:S(2)}, u32[]{:S(2)}) collective-permute-start(f32[512,128]{1,0:T(8,128)S(1)} %copy-done.4), channel_id=1, source_target_pairs={{0,259},{1,258},{2,257},{3,256},{4,263},{5,262},{6,261},{7,260},{8... | collective-permute-start | bytes 786440 | tf_op jit(solution)/shard_map/ppermute | solution.py:306
  29.4 6.9 %collective-permute-done = f32[512,128]{1,0:T(8,128)S(1)} collective-permute-done((f32[512,128]{1,0:T(8,128)S(1)}, f32[512,128]{1,0:T(8,128)S(1)}, u32[]{:S(2)}, u32[]{:S(2)}) %collective-permute-start) | collective-permute-done | bytes 262176 | tf_op jit(solution)/shard_map/ppermute | solution.py:306
  36.3 16.7 %all-to-all-done = f32[128,1,2304]{2,1,0:T(1,128)S(1)} async-done(((f32[128,1,2304]{2,1,0:T(1,128)}), f32[128,1,2304]{2,1,0:T(1,128)S(1)}, u32[]{:S(2)}, u32[]{:S(2)}) %all-to-all-start) | async-done | bytes 1179680 | tf_op jit(solution)/shard_map/all_to_all | solution.py:303
  53.1 4.8 %collective-permute-start.1 = (f32[128,1,768]{2,1,0:T(1,128)S(1)}, f32[128,1,768]{2,1,0:T(1,128)S(1)}, u32[]{:S(2)}, u32[]{:S(2)}) collective-permute-start(f32[128,1,768]{2,1,0:T(1,128)S(1)} %slice.35), channel_id=1, source_target_pairs={{0,128},{128,0},{256,384},{384,256},{1,129},{129,1},{257,385},{385... | collective-permute-start | bytes 1179656 | tf_op jit(solution)/shard_map/ppermute | solution.py:308
  57.9 2.1 %shard_map.68 = (f32[8,12,16,128]{3,2,1,0:T(8,128)S(1)}, f32[8,12,16,128]{3,2,1,0:T(8,128)S(1)}, f32[8,6,16,128]{3,2,1,0:T(8,128)S(1)}) custom-call(f32[2304,128]{1,0:T(8,128)S(1)} %bitcast.50), custom_call_target="tpu_custom_call" | custom-call | flops 20000000 | bytes 150000000 | tf_op jit(solution)/shard_map/pallas_call | solution.py:253
  60.0 7.4 %shard_map.69 = f32[3072,128]{1,0:T(8,128)S(1)} custom-call(s32[1]{0:T(128)} %bitcast.core_ref, f32[3]{0:T(128)S(1)} %copy-done.3, f32[8,12,16,128]{3,2,1,0:T(8,128)S(1)} %get-tuple-element.19.x_ref, f32[8,12,16,128]{3,2,1,0:T(8,128)S(1)} %get-tuple-element.20.lap_ref, f32[8,6,16,128]{3,2,1,0:T(8,128)S(1)} %get-tuple-element.21.pot_own_ref, ...), custom_call_target="tpu_custom_call" | custom-call | flops 60000000 | bytes 40000000 | tf_op jit(solution)/shard_map/pallas_call | solution.py:270
  67.5 1.2 copy-done
  68.6 14.9 %all-to-all-start.1 = ((f32[256,1,1536]{2,1,0:T(1,128)}), f32[256,1,1536]{2,1,0:T(1,128)S(1)}, u32[]{:S(2)}, u32[]{:S(2)}) async-start(f32[256,1,1536]{2,1,0:T(1,128)} %bitcast.52), calls=%async_computation.1 | async-start | bytes 3145728 | tf_op jit(solution)/shard_map/all_to_all | solution.py:59
  83.5 39.1 %all-to-all-done.1 = f32[256,1,1536]{2,1,0:T(1,128)S(1)} async-done(((f32[256,1,1536]{2,1,0:T(1,128)}), f32[256,1,1536]{2,1,0:T(1,128)S(1)}, u32[]{:S(2)}, u32[]{:S(2)}) %all-to-all-start.1) | async-done | bytes 1572896 | tf_op jit(solution)/shard_map/all_to_all | solution.py:59
  122.9 3.8 %collective-permute-start.2 = (f32[256,768]{1,0:T(8,128)S(1)}, f32[256,768]{1,0:T(8,128)S(1)}, u32[]{:S(2)}, u32[]{:S(2)}) collective-permute-start(f32[256,768]{1,0:T(8,128)S(1)} %get-tuple-element.24), channel_id=1, source_target_pairs={{0,128},{128,0},{256,384},{384,256},{1,129},{129,1},{257,385},{385... | collective-permute-start | bytes 2359304 | tf_op jit(solution)/shard_map/ppermute | solution.py:318
  129.4 5.8 %collective-permute-start.6 = (f32[768,128]{1,0:T(8,128)S(1)}, f32[768,128]{1,0:T(8,128)S(1)}, u32[]{:S(2)}, u32[]{:S(2)}) collective-permute-start(f32[768,128]{1,0:T(8,128)S(1)} %convolution_add_fusion), channel_id=1, source_target_pairs={{0,256},{256,0},{128,384},{384,128},{1,257},{257,1},{129,385},{385... | collective-permute-start | bytes 1179656 | tf_op jit(solution)/shard_map/ppermute | solution.py:334
  136.2 2.4 %collective-permute-start.3 = (f32[128,512]{1,0:T(8,128)S(1)}, f32[128,512]{1,0:T(8,128)S(1)}, u32[]{:S(2)}, u32[]{:S(2)}) collective-permute-start(f32[128,512]{1,0:T(8,128)S(1)} %get-tuple-element.35), channel_id=1, source_target_pairs={{0,4},{1,5},{2,6},{3,7},{4,8},{5,9},{6,10},{7,11},{8,12},{9,13},{1... | collective-permute-start | bytes 786440 | tf_op jit(solution)/shard_map/ppermute | solution.py:343
  138.6 3.5 %collective-permute-start.4 = (f32[128,512]{1,0:T(8,128)S(1)}, f32[128,512]{1,0:T(8,128)S(1)}, u32[]{:S(2)}, u32[]{:S(2)}) collective-permute-start(f32[128,512]{1,0:T(8,128)S(1)} %get-tuple-element.34), channel_id=1, source_target_pairs={{0,8},{1,9},{2,10},{3,11},{4,12},{5,13},{6,14},{7,15},{8,0},{9,1},... | collective-permute-start | bytes 786440 | tf_op jit(solution)/shard_map/ppermute | solution.py:343
  142.1 2.7 %collective-permute-start.5 = (f32[128,512]{1,0:T(8,128)S(1)}, f32[128,512]{1,0:T(8,128)S(1)}, u32[]{:S(2)}, u32[]{:S(2)}) collective-permute-start(f32[128,512]{1,0:T(8,128)S(1)} %get-tuple-element.33), channel_id=1, source_target_pairs={{0,12},{1,13},{2,14},{3,15},{4,0},{5,1},{6,2},{7,3},{8,4},{9,5},{1... | collective-permute-start | bytes 786440 | tf_op jit(solution)/shard_map/ppermute | solution.py:343
  144.8 2.2 %collective-permute-done.3 = f32[128,512]{1,0:T(8,128)S(1)} collective-permute-done((f32[128,512]{1,0:T(8,128)S(1)}, f32[128,512]{1,0:T(8,128)S(1)}, u32[]{:S(2)}, u32[]{:S(2)}) %collective-permute-start.3) | collective-permute-done | bytes 262176 | tf_op jit(solution)/shard_map/ppermute | solution.py:343
  147.1 4.5 %collective-permute-done.4 = f32[128,512]{1,0:T(8,128)S(1)} collective-permute-done((f32[128,512]{1,0:T(8,128)S(1)}, f32[128,512]{1,0:T(8,128)S(1)}, u32[]{:S(2)}, u32[]{:S(2)}) %collective-permute-start.4) | collective-permute-done | bytes 262176 | tf_op jit(solution)/shard_map/ppermute | solution.py:343
  151.6 3.0 %collective-permute-done.5 = f32[128,512]{1,0:T(8,128)S(1)} collective-permute-done((f32[128,512]{1,0:T(8,128)S(1)}, f32[128,512]{1,0:T(8,128)S(1)}, u32[]{:S(2)}, u32[]{:S(2)}) %collective-permute-start.5) | collective-permute-done | bytes 262176 | tf_op jit(solution)/shard_map/ppermute | solution.py:343
  155.0 19.8 %all_to_all.20 = f32[64,1,1024]{2,1,0:T(1,128)S(1)} all-to-all(f32[64,1,1024]{2,1,0:T(1,128)S(1)} %bitcast.60), channel_id=1, replica_groups={{0,256,16,272,32,288,48,304,64,320,80,336,96,352,112,368,1,257,17,273,3..., dimensions={0} | all-to-all | bytes 524288 | tf_op jit(solution)/shard_map/all_to_all | solution.py:59
  175.0 1.1 broadcast_in_dim.2
  176.1 10.3 %all-to-all-start.3 = ((f32[128,1,1024]{2,1,0:T(1,128)}), f32[128,1,1024]{2,1,0:T(1,128)S(1)}, u32[]{:S(2)}, u32[]{:S(2)}) async-start(f32[128,1,1024]{2,1,0:T(1,128)} %broadcast_in_dim.2), calls=%async_computation.3 | async-start | bytes 1048576 | tf_op jit(solution)/shard_map/all_to_all | solution.py:349
  189.0 14.9 %all-to-all-done.3 = f32[128,1,1024]{2,1,0:T(1,128)S(1)} async-done(((f32[128,1,1024]{2,1,0:T(1,128)}), f32[128,1,1024]{2,1,0:T(1,128)S(1)}, u32[]{:S(2)}, u32[]{:S(2)}) %all-to-all-start.3) | async-done | bytes 524320 | tf_op jit(solution)/shard_map/all_to_all | solution.py:349
  (32 shorter events, 9.0 us)
Async XLA Ops:
  0.6 1.1 copy-start.1
  1.8 0.8 copy-start.2
  4.0 17.9 %copy-start.4 = (f32[512,128]{1,0:T(8,128)S(1)}, f32[512,128]{1,0:T(8,128)}, u32[]{:S(2)}) copy-start(f32[512,128]{1,0:T(8,128)} %param.7) | copy-start | bytes 786436
  4.0 49.1 %all-to-all-start = ((f32[128,1,2304]{2,1,0:T(1,128)}), f32[128,1,2304]{2,1,0:T(1,128)S(1)}, u32[]{:S(2)}, u32[]{:S(2)}) async-start(f32[128,1,2304]{2,1,0:T(1,128)} %bitcast.4), calls=%async_computation | async-start | bytes 2359296 | tf_op jit(solution)/shard_map/all_to_all | solution.py:303
  21.9 38.2 %copy-start.3 = (f32[3]{0:T(128)S(1)}, f32[3]{0:T(128)}, u32[]{:S(2)}) copy-start(f32[3]{0:T(128)} %bounds_ref.1) | copy-start | bytes 40
  21.9 14.4 %collective-permute-start = (f32[512,128]{1,0:T(8,128)S(1)}, f32[512,128]{1,0:T(8,128)S(1)}, u32[]{:S(2)}, u32[]{:S(2)}) collective-permute-start(f32[512,128]{1,0:T(8,128)S(1)} %copy-done.4), channel_id=1, source_target_pairs={{0,259},{1,258},{2,257},{3,256},{4,263},{5,262},{6,261},{7,260},{8... | collective-permute-start | bytes 786440 | tf_op jit(solution)/shard_map/ppermute | solution.py:306
  53.1 6.9 %collective-permute-start.1 = (f32[128,1,768]{2,1,0:T(1,128)S(1)}, f32[128,1,768]{2,1,0:T(1,128)S(1)}, u32[]{:S(2)}, u32[]{:S(2)}) collective-permute-start(f32[128,1,768]{2,1,0:T(1,128)S(1)} %slice.35), channel_id=1, source_target_pairs={{0,128},{128,0},{256,384},{384,256},{1,129},{129,1},{257,385},{385... | collective-permute-start | bytes 1179656 | tf_op jit(solution)/shard_map/ppermute | solution.py:308
  67.5 1.2 copy-start
  68.6 54.0 %all-to-all-start.1 = ((f32[256,1,1536]{2,1,0:T(1,128)}), f32[256,1,1536]{2,1,0:T(1,128)S(1)}, u32[]{:S(2)}, u32[]{:S(2)}) async-start(f32[256,1,1536]{2,1,0:T(1,128)} %bitcast.52), calls=%async_computation.1 | async-start | bytes 3145728 | tf_op jit(solution)/shard_map/all_to_all | solution.py:59
  122.9 5.7 %collective-permute-start.2 = (f32[256,768]{1,0:T(8,128)S(1)}, f32[256,768]{1,0:T(8,128)S(1)}, u32[]{:S(2)}, u32[]{:S(2)}) collective-permute-start(f32[256,768]{1,0:T(8,128)S(1)} %get-tuple-element.24), channel_id=1, source_target_pairs={{0,128},{128,0},{256,384},{384,256},{1,129},{129,1},{257,385},{385... | collective-permute-start | bytes 2359304 | tf_op jit(solution)/shard_map/ppermute | solution.py:318
  129.4 25.2 %collective-permute-start.6 = (f32[768,128]{1,0:T(8,128)S(1)}, f32[768,128]{1,0:T(8,128)S(1)}, u32[]{:S(2)}, u32[]{:S(2)}) collective-permute-start(f32[768,128]{1,0:T(8,128)S(1)} %convolution_add_fusion), channel_id=1, source_target_pairs={{0,256},{256,0},{128,384},{384,128},{1,257},{257,1},{129,385},{385... | collective-permute-start | bytes 1179656 | tf_op jit(solution)/shard_map/ppermute | solution.py:334
  136.2 10.9 %collective-permute-start.3 = (f32[128,512]{1,0:T(8,128)S(1)}, f32[128,512]{1,0:T(8,128)S(1)}, u32[]{:S(2)}, u32[]{:S(2)}) collective-permute-start(f32[128,512]{1,0:T(8,128)S(1)} %get-tuple-element.35), channel_id=1, source_target_pairs={{0,4},{1,5},{2,6},{3,7},{4,8},{5,9},{6,10},{7,11},{8,12},{9,13},{1... | collective-permute-start | bytes 786440 | tf_op jit(solution)/shard_map/ppermute | solution.py:343
  138.6 13.0 %collective-permute-start.4 = (f32[128,512]{1,0:T(8,128)S(1)}, f32[128,512]{1,0:T(8,128)S(1)}, u32[]{:S(2)}, u32[]{:S(2)}) collective-permute-start(f32[128,512]{1,0:T(8,128)S(1)} %get-tuple-element.34), channel_id=1, source_target_pairs={{0,8},{1,9},{2,10},{3,11},{4,12},{5,13},{6,14},{7,15},{8,0},{9,1},... | collective-permute-start | bytes 786440 | tf_op jit(solution)/shard_map/ppermute | solution.py:343
  142.1 12.5 %collective-permute-start.5 = (f32[128,512]{1,0:T(8,128)S(1)}, f32[128,512]{1,0:T(8,128)S(1)}, u32[]{:S(2)}, u32[]{:S(2)}) collective-permute-start(f32[128,512]{1,0:T(8,128)S(1)} %get-tuple-element.33), channel_id=1, source_target_pairs={{0,12},{1,13},{2,14},{3,15},{4,0},{5,1},{6,2},{7,3},{8,4},{9,5},{1... | collective-permute-start | bytes 786440 | tf_op jit(solution)/shard_map/ppermute | solution.py:343
  176.1 27.8 %all-to-all-start.3 = ((f32[128,1,1024]{2,1,0:T(1,128)}), f32[128,1,1024]{2,1,0:T(1,128)S(1)}, u32[]{:S(2)}, u32[]{:S(2)}) async-start(f32[128,1,1024]{2,1,0:T(1,128)} %broadcast_in_dim.2), calls=%async_computation.3 | async-start | bytes 1048576 | tf_op jit(solution)/shard_map/all_to_all | solution.py:349
